TPU v7x, 256 devices: a whole 4x4x8 slice. The times are simulated.
256 devices in a mesh: layer: 4 (over x), plane: 64 (over y, z, core).
Axes of the slice: x: 4, y: 4, z: 8, core: 2. Of those that a mesh axis runs over, the one named last changes fastest.
Arguments:
- basis_init: float32 [8, 64, 512, 128], P(None, 'layer', 'plane'), may hold values from 0.05 to 1
- permeability: float32 [64, 512, 128], P('layer', 'plane'), may hold values from 0.02 to 0.2
- accumulation: float32 [64, 512, 128], P('layer', 'plane'), may hold values from 0.002 to 0.02
- pressure: float32 [64, 512, 128], P('layer', 'plane'), may hold values from -1.2 to 1.2
- source: float32 [64, 512, 128], P('layer', 'plane'), may hold values from -0.6 to 0.6
- support: int32 [8, 64, 512, 128], P(None, 'layer', 'plane'), may hold values from 0 to 1, as said below
- block_of: int32 [64, 512, 128], P('layer', 'plane'), may hold values from 0 to 9359, as said below
- curve_rank: int32 [9360], replicated, may hold values from 0 to 9359, as said below
Outputs:
- smoothed_basis: float32 [8, 64, 512, 128], P(None, 'layer', 'plane')
- coarse_matrix: float32 [27, 9472], P(None, ('layer', 'plane'))
- coarse_residual: float32 [9472], P(('layer', 'plane'))
Inputs may be any that keep to these rules, and one draw needn't show every extreme that they name: `block_of`: cells with equal (z + 4) // 8, (x + 4) // 8 and y // 8 share one label, and distinct such bricks carry distinct labels. `curve_rank`: A permutation of the block labels' positions along the curve. `support`: slot 0 is 1 at every cell; a slot is 0 wherever its coarse block lies outside the 9 x 65 x 16 coarse grid.
All inputs are finite; a program needn't handle non-finite values.
Results may differ from a plain program's by a relative error of at most 0.00022.
Values sent between devices are 32-bit elements; how exact they have to be, the bound alone decides.
A program may use at most 128 MiB of HBM per device.

v0:
```python
import jax
import jax.numpy as jnp
from jax import lax
from jax.sharding import PartitionSpec as P

ITERS = 2


OMEGA = 2.0 / 3.0
CELL_SHIFTS = (4, 4, 0)


def with_halo(shard, sides, width):
    for axis, dim in sides:
        size, length = (lax.axis_size(axis), shard.shape[dim])
        up = [(i, (i + 1) % size) for i in range(size - 1)]
        down = [(j, i) for i, j in up]
        last = lax.slice_in_dim(shard, length - width, length, axis=dim)
        leading = lax.slice_in_dim(shard, 0, width, axis=dim)
        before = lax.ppermute(last, axis, up)
        after = lax.ppermute(leading, axis, down)
        shard = jnp.concatenate([before, shard, after], axis=dim)
    return shard


def two_blocks(where_at, shift_by):
    moved_pos = where_at + shift_by
    anchor = moved_pos // 8
    toward = jnp.where(moved_pos % 8 >= 4, 1, -1)
    return jnp.stack([anchor, anchor + toward])


def make_coords(positions):
    home_q, lower_q, upper_q = ([], [], [])
    for grid_dim in range(3):
        where_at = positions[grid_dim]
        shift_by = CELL_SHIFTS[grid_dim]
        home_q.append(two_blocks(where_at, shift_by))
        lower_q.append(two_blocks(where_at - 1, shift_by))
        upper_q.append(two_blocks(where_at + 1, shift_by))
    return (tuple(home_q), tuple(lower_q), tuple(upper_q))


def near_slice(padded, grid_dim, side_sign):
    windows = [slice(1, -1)] * 3
    windows[grid_dim] = slice(0, -2) if side_sign < 0 else slice(2, None)
    leading = [slice(None)] * (padded.ndim - 3)
    return padded[tuple(leading + windows)]


def pick_same(beside_vals, home_blocks, beside_blocks, grid_dim):
    agree = (home_blocks[:, None, :] == beside_blocks[None, :, :]).astype(jnp.float32)
    shape_one = [2, 2, 1, 1, 1]
    shape_one[2 + grid_dim] = home_blocks.shape[1]
    agree = agree.reshape(shape_one)
    leading = jnp.moveaxis(beside_vals, grid_dim, 0)
    result = (
        agree[:, 0][:, None, None] * leading[0][None]
        + agree[:, 1][:, None, None] * leading[1][None]
    )
    return jnp.moveaxis(result, 0, grid_dim)


def apply_basis(basis_now, padded, rock_perm, rock_padded, accum_rate, coords):
    home_q, lower_q, upper_q = coords
    applied = accum_rate * basis_now
    diagonal = accum_rate
    for grid_dim in range(3):
        for side_sign, beside_q in ((-1, lower_q), (1, upper_q)):
            beside_vals = near_slice(padded, grid_dim, side_sign)
            beside_perm = near_slice(rock_padded, grid_dim, side_sign)
            transmit = 2.0 * rock_perm * beside_perm / (rock_perm + beside_perm)
            matched = pick_same(beside_vals, home_q[grid_dim], beside_q[grid_dim], grid_dim)
            applied = applied + transmit * (basis_now - matched)
            diagonal = diagonal + transmit
    return (applied, diagonal)


def apply_scalar(field, padded, rock_perm, rock_padded, accum_rate):
    applied = accum_rate * field
    for grid_dim in range(3):
        for side_sign in (-1, 1):
            beside_vals = near_slice(padded, grid_dim, side_sign)
            beside_perm = near_slice(rock_padded, grid_dim, side_sign)
            transmit = 2.0 * rock_perm * beside_perm / (rock_perm + beside_perm)
            applied = applied + transmit * (field - beside_vals)
    return applied


def fold_bits(values, lookup, bit_axis, grid_dim):
    leading = jnp.moveaxis(values, bit_axis, 0)
    rest_nd = leading.ndim - 1
    shape_one = [1] * rest_nd
    shape_one[rest_nd - 3 + grid_dim] = lookup.shape[2]
    result = (
        lookup[:, 0].reshape([3] + shape_one) * leading[0][None]
        + lookup[:, 1].reshape([3] + shape_one) * leading[1][None]
    )
    return jnp.moveaxis(result, 0, bit_axis)


def block_terms(applied, residual, home_q):
    folded = applied
    for grid_dim in range(3):
        toward = home_q[grid_dim][1] - home_q[grid_dim][0]
        offset = jnp.stack([jnp.zeros_like(toward), toward])
        lookup = (offset[None] + 1 == jnp.arange(3)[:, None, None]).astype(jnp.float32)
        folded = fold_bits(folded, lookup, grid_dim, grid_dim)
    folded = folded.reshape((27,) + applied.shape[3:])
    return jnp.concatenate([folded, residual[None]], axis=0)


def sum_blocks(terms):
    padded = jnp.pad(terms, ((0, 0), (4, 4), (4, 4), (0, 0)))
    count, z_len, x_len, y_len = padded.shape
    grouped = padded.reshape(count, z_len // 8, 8, x_len // 8, 8, y_len // 8, 8)
    return grouped.sum(axis=(2, 4, 6)).reshape(count, -1)


def block_labels(block_of):
    z_len, x_len, y_len = block_of.shape
    rep_z = jnp.clip(8 * jnp.arange(z_len // 8 + 1) - 4, 0, z_len - 1)
    rep_x = jnp.clip(8 * jnp.arange(x_len // 8 + 1) - 4, 0, x_len - 1)
    rep_y = 8 * jnp.arange(y_len // 8)
    return block_of[rep_z[:, None, None], rep_x[None, :, None], rep_y[None, None, :]].reshape(-1)


def basis_halo(values):
    padded = with_halo(values, (("layer", 3), ("plane", 4)), 1)
    return jnp.pad(padded, ((0, 0),) * 5 + ((1, 1),))


def per_device(
    basis_init, permeability, accumulation, pressure, source, support, block_of, curve_rank
):
    slot_count, z_cells, x_cells, y_cells = basis_init.shape
    z_position = lax.axis_index("layer") * z_cells + jnp.arange(z_cells)
    x_position = lax.axis_index("plane") * x_cells + jnp.arange(x_cells)
    coords = make_coords((z_position, x_position, jnp.arange(y_cells)))
    grid_shape = (2, 2, 2, z_cells, x_cells, y_cells)
    in_support = support.reshape(grid_shape).astype(jnp.float32)
    initial = basis_init.reshape(grid_shape) * in_support
    basis_now = initial / jnp.sum(initial, axis=(0, 1, 2))
    rock_halo = with_halo(jnp.stack([permeability, pressure]), (("layer", 1), ("plane", 2)), 1)
    rock_halo = jnp.pad(rock_halo, ((0, 0), (0, 0), (0, 0), (1, 1)))
    for sweep_idx in range(ITERS):
        applied, diagonal = apply_basis(
            basis_now, basis_halo(basis_now), permeability, rock_halo[0], accumulation, coords
        )
        basis_now = in_support * (basis_now - OMEGA * applied / diagonal)
        basis_now = basis_now / jnp.sum(basis_now, axis=(0, 1, 2))
    applied, diagonal = apply_basis(
        basis_now, basis_halo(basis_now), permeability, rock_halo[0], accumulation, coords
    )
    residual = source - apply_scalar(
        pressure, rock_halo[1], permeability, rock_halo[0], accumulation
    )
    partial_rows = sum_blocks(block_terms(applied, residual, coords[0]))
    row_ranks = curve_rank[block_labels(block_of)]
    layer_count = lax.axis_size("layer")
    plane_count = lax.axis_size("plane")
    devices = layer_count * plane_count
    own_rows = (curve_rank.shape[0] + devices - 1) // devices
    dense_rows = jnp.zeros((28, own_rows * devices), jnp.float32).at[:, row_ranks].set(partial_rows)
    summed = lax.psum_scatter(dense_rows, ("layer", "plane"), scatter_dimension=1, tiled=True)
    return (basis_now.reshape(slot_count, z_cells, x_cells, y_cells), summed[:27], summed[27])


def solution(mesh):
    return jax.shard_map(
        per_device,
        mesh=mesh,
        in_specs=(
            P(None, "layer", "plane", None),
            P("layer", "plane", None),
            P("layer", "plane", None),
            P("layer", "plane", None),
            P("layer", "plane", None),
            P(None, "layer", "plane", None),
            P("layer", "plane", None),
            P(),
        ),
        out_specs=(
            P(None, "layer", "plane", None),
            P(None, ("layer", "plane")),
            P(("layer", "plane")),
        ),
        check_vma=False,
    )
```

profile of v0, /device:TPU:1, one launch (start us, length us, event | category | flops | bytes accessed | tf_op | source)
XLA Modules:
  0.0 406.2 jit_solution(1199180444597111479)
XLA Ops:
  7.2 0.8 pad_maximum_fusion.39
  8.0 1.3 collective-permute-start.1
  9.3 4.6 %collective-permute-start = (f32[2,1,8,128]{3,2,1,0:T(8,128)S(1)}, f32[2,1,8,128]{3,2,1,0:T(8,128)S(1)}, u32[]{:S(2)}, u32[]{:S(2)}) collective-permute-start(f32[2,1,8,128]{3,2,1,0:T(8,128)S(1)} %get-tuple-element.102), channel_id=1, source_target_pairs={{0,64},{64,128},{128,192},{1,65},{65,129},{129,193},{2,66},{66,130... | collective-permute-start | bytes 24584 | tf_op jit(solution)/shard_map/ppermute | solution.py:20
  13.9 1.1 convert_element_type.99
  15.0 1.3 fusion.111
  16.4 1.3 collective-permute-start.5
  17.7 4.0 collective-permute-start.4
  22.5 1.7 gather_fusion
  24.3 5.7 %collective-permute-start.3 = (f32[2,18,1,128]{3,2,1,0:T(1,128)S(1)}, f32[2,18,1,128]{3,2,1,0:T(1,128)S(1)}, u32[]{:S(2)}, u32[]{:S(2)}) collective-permute-start(f32[2,18,1,128]{3,2,1,0:T(1,128)S(1)} %get-tuple-element.101), channel_id=1, source_target_pairs={{1,0},{2,1},{3,2},{4,3},{5,4},{6,5},{7,6},{8,7},{9,8},{10,9},{11,1... | collective-permute-start | bytes 55304 | tf_op jit(solution)/shard_map/ppermute | solution.py:21
  29.9 1.9 collective-permute-start.2
  31.9 1.1 collective-permute-done.2
  33.0 0.4 select_maximum_fusion.12
  33.5 0.3 fusion.76
  33.9 2.1 collective-permute-start.7
  36.0 3.8 collective-permute-start.6
  39.9 1.3 collective-permute-done.6
  41.1 1.3 select_maximum_fusion.8
  43.2 0.6 copy-done.2
  43.8 1.9 fusion.116
  45.7 0.9 multiply_divide_fusion.1
  46.5 1.3 collective-permute-start.9
  47.8 4.0 collective-permute-start.8
  51.9 1.1 gather_fusion.1
  53.1 1.9 collective-permute-start.11
  55.1 5.2 %collective-permute-start.10 = (f32[2,2,2,18,1,128]{5,4,3,2,1,0:T(1,128)S(1)}, f32[2,2,2,18,1,128]{5,4,3,2,1,0:T(1,128)S(1)}, u32[]{:S(2)}, u32[]{:S(2)}) collective-permute-start(f32[2,2,2,18,1,128]{5,4,3,2,1,0:T(1,128)S(1)} %get-tuple-element.42), channel_id=1, source_target_pairs={{0,1},{1,2},{2,3},{3,4},{4,5},{5,6},{6,7},{7,8},{8,9},{9,10},{10,1... | collective-permute-start | bytes 221192 | tf_op jit(solution)/shard_map/ppermute | solution.py:20
  60.4 1.3 collective-permute-done.10
  61.7 1.3 select_maximum_fusion.4
  63.6 0.7 copy-done.7
  64.3 1.9 fusion.114
  66.1 0.9 multiply_divide_fusion
  67.0 1.3 collective-permute-start.13
  68.3 4.6 %collective-permute-start.12 = (f32[2,2,2,1,8,128]{5,4,3,2,1,0:T(8,128)S(1)}, f32[2,2,2,1,8,128]{5,4,3,2,1,0:T(8,128)S(1)}, u32[]{:S(2)}, u32[]{:S(2)}) collective-permute-start(f32[2,2,2,1,8,128]{5,4,3,2,1,0:T(8,128)S(1)} %get-tuple-element.74), channel_id=1, source_target_pairs={{0,64},{64,128},{128,192},{1,65},{65,129},{129,193},{2,66},{66,130... | collective-permute-start | bytes 98312 | tf_op jit(solution)/shard_map/ppermute | solution.py:20
  73.0 0.9 collective-permute-done.12
  74.0 2.1 collective-permute-start.15
  76.1 5.1 %collective-permute-start.14 = (f32[2,2,2,18,1,128]{5,4,3,2,1,0:T(1,128)S(1)}, f32[2,2,2,18,1,128]{5,4,3,2,1,0:T(1,128)S(1)}, u32[]{:S(2)}, u32[]{:S(2)}) collective-permute-start(f32[2,2,2,18,1,128]{5,4,3,2,1,0:T(1,128)S(1)} %get-tuple-element.38), channel_id=1, source_target_pairs={{0,1},{1,2},{2,3},{3,4},{4,5},{5,6},{6,7},{7,8},{8,9},{9,10},{10,1... | collective-permute-start | bytes 221192 | tf_op jit(solution)/shard_map/ppermute | solution.py:20
  81.4 1.3 collective-permute-done.14
  82.7 1.3 select_maximum_fusion
  84.5 0.8 multiply_add_fusion.2
  86.3 4.8 %copy.21 = f32[28,16,8,128]{0,3,2,1:T(8,128)} copy(f32[28,16,8,128]{3,2,1,0:T(8,128)S(1)} %pad_maximum_fusion) | data formatting | bytes 3670016
  91.1 12.2 %pad.25.clone = f32[28,24,16,128]{0,3,2,1:T(8,128)} pad(f32[28,16,8,128]{0,3,2,1:T(8,128)} %copy.21, f32[]{:T(128)} %constant.185.clone.1), padding=0_0x4_4x4_4x0_0 | pad | bytes 7340036 | tf_op jit(solution)/shard_map/jit(_pad)/pad | solution.py:114
  103.3 9.5 %reduce_sum.39 = f32[28,3,2,16]{0,3,2,1:T(8,128)S(1)} reduce(f32[28,3,8,2,8,16,8]{0,6,5,4,3,2,1:T(8,128)} %bitcast.420, f32[]{:T(128)} %constant.185.clone.1), dimensions={2,4,6}, to_apply=%region_3.4 | reduce | flops 1373568 | bytes 5515780 | tf_op jit(solution)/shard_map/reduce_sum | solution.py:117
  112.8 3.3 scatter_custom_fusion
  116.1 1.0 copy-done.6
  117.2 0.8 broadcast_divide_fusion
  118.0 278.5 %all-reduce.11.cloned.1.call-done = f32[28,9472]{0,1:T(8,128)} async-done(((f32[28,9472]{0,1:T(8,128)}), f32[28,9472]{0,1:T(8,128)}) %all-reduce.11.cloned.1.call-update) | async-done | bytes 1060880
  396.5 0.7 constant_dynamic-slice_fusion
  397.2 0.7 copy.20
  397.9 1.4 dynamic-slice_reduce_fusion
  (131 shorter events, 4.0 us)
Async XLA Ops:
  7.2 15.3 %copy-start = (s32[16,8,128]{2,1,0:T(8,128)S(1)}, s32[16,8,128]{2,1,0:T(8,128)}, u32[]{:S(2)}) copy-start(s32[16,8,128]{2,1,0:T(8,128)} %param.14) | copy-start | bytes 196612
  7.2 9.1 %copy-start.4 = (f32[8,16,8,128]{3,2,1,0:T(8,128)S(1)}, f32[8,16,8,128]{3,2,1,0:T(8,128)}, u32[]{:S(2)}) copy-start(f32[8,16,8,128]{3,2,1,0:T(8,128)} %param.8) | copy-start | bytes 1572868
  7.2 389.3 %all-reduce.11.cloned.1.call-start = ((), (), s32[]{:S(2)}) async-start(), calls=%async_computation | async-start | bytes 9699328
  8.0 16.1 %collective-permute-start.1 = (f32[2,1,8,128]{3,2,1,0:T(8,128)S(1)}, f32[2,1,8,128]{3,2,1,0:T(8,128)S(1)}, u32[]{:S(2)}, u32[]{:S(2)}) collective-permute-start(f32[2,1,8,128]{3,2,1,0:T(8,128)S(1)} %get-tuple-element.103), channel_id=1, source_target_pairs={{64,0},{128,64},{192,128},{65,1},{129,65},{193,129},{66,2},{130,66... | collective-permute-start | bytes 24584 | tf_op jit(solution)/shard_map/ppermute | solution.py:21
  9.3 14.9 %collective-permute-start = (f32[2,1,8,128]{3,2,1,0:T(8,128)S(1)}, f32[2,1,8,128]{3,2,1,0:T(8,128)S(1)}, u32[]{:S(2)}, u32[]{:S(2)}) collective-permute-start(f32[2,1,8,128]{3,2,1,0:T(8,128)S(1)} %get-tuple-element.102), channel_id=1, source_target_pairs={{0,64},{64,128},{128,192},{1,65},{65,129},{129,193},{2,66},{66,130... | collective-permute-start | bytes 24584 | tf_op jit(solution)/shard_map/ppermute | solution.py:20
  16.3 7.9 %copy-start.8 = (f32[16,8,128]{2,1,0:T(8,128)S(1)}, f32[16,8,128]{2,1,0:T(8,128)}, u32[]{:S(2)}) copy-start(f32[16,8,128]{2,1,0:T(8,128)} %param.11) | copy-start | bytes 196612
  16.3 7.9 %copy-start.9 = (f32[16,8,128]{2,1,0:T(8,128)S(1)}, f32[16,8,128]{2,1,0:T(8,128)}, u32[]{:S(2)}) copy-start(f32[16,8,128]{2,1,0:T(8,128)} %param.9) | copy-start | bytes 196612
  16.4 17.4 %collective-permute-start.5 = (f32[2,2,2,1,8,128]{5,4,3,2,1,0:T(8,128)S(1)}, f32[2,2,2,1,8,128]{5,4,3,2,1,0:T(8,128)S(1)}, u32[]{:S(2)}, u32[]{:S(2)}) collective-permute-start(f32[2,2,2,1,8,128]{5,4,3,2,1,0:T(8,128)S(1)} %get-tuple-element.99), channel_id=1, source_target_pairs={{64,0},{128,64},{192,128},{65,1},{129,65},{193,129},{66,2},{130,66... | collective-permute-start | bytes 98312 | tf_op jit(solution)/shard_map/ppermute | solution.py:21
  17.7 16.1 %collective-permute-start.4 = (f32[2,2,2,1,8,128]{5,4,3,2,1,0:T(8,128)S(1)}, f32[2,2,2,1,8,128]{5,4,3,2,1,0:T(8,128)S(1)}, u32[]{:S(2)}, u32[]{:S(2)}) collective-permute-start(f32[2,2,2,1,8,128]{5,4,3,2,1,0:T(8,128)S(1)} %get-tuple-element.98), channel_id=1, source_target_pairs={{0,64},{64,128},{128,192},{1,65},{65,129},{129,193},{2,66},{66,130... | collective-permute-start | bytes 98312 | tf_op jit(solution)/shard_map/ppermute | solution.py:20
  22.5 11.0 %copy-start.5 = (f32[16,8,128]{2,1,0:T(8,128)S(1)}, f32[16,8,128]{2,1,0:T(8,128)}, u32[]{:S(2)}) copy-start(f32[16,8,128]{2,1,0:T(8,128)} %param.10) | copy-start | bytes 196612
  22.5 11.0 %copy-start.10 = (f32[16,8,128]{2,1,0:T(8,128)S(1)}, f32[16,8,128]{2,1,0:T(8,128)}, u32[]{:S(2)}) copy-start(f32[16,8,128]{2,1,0:T(8,128)} %param.12) | copy-start | bytes 196612
  24.3 7.6 %collective-permute-start.3 = (f32[2,18,1,128]{3,2,1,0:T(1,128)S(1)}, f32[2,18,1,128]{3,2,1,0:T(1,128)S(1)}, u32[]{:S(2)}, u32[]{:S(2)}) collective-permute-start(f32[2,18,1,128]{3,2,1,0:T(1,128)S(1)} %get-tuple-element.101), channel_id=1, source_target_pairs={{1,0},{2,1},{3,2},{4,3},{5,4},{6,5},{7,6},{8,7},{9,8},{10,9},{11,1... | collective-permute-start | bytes 55304 | tf_op jit(solution)/shard_map/ppermute | solution.py:21
  29.9 3.1 collective-permute-start.2
  33.9 5.9 %collective-permute-start.7 = (f32[2,2,2,18,1,128]{5,4,3,2,1,0:T(1,128)S(1)}, f32[2,2,2,18,1,128]{5,4,3,2,1,0:T(1,128)S(1)}, u32[]{:S(2)}, u32[]{:S(2)}) collective-permute-start(f32[2,2,2,18,1,128]{5,4,3,2,1,0:T(1,128)S(1)} %get-tuple-element.47), channel_id=1, source_target_pairs={{1,0},{2,1},{3,2},{4,3},{5,4},{6,5},{7,6},{8,7},{9,8},{10,9},{11,1... | collective-permute-start | bytes 221192 | tf_op jit(solution)/shard_map/ppermute | solution.py:21
  36.0 5.2 %collective-permute-start.6 = (f32[2,2,2,18,1,128]{5,4,3,2,1,0:T(1,128)S(1)}, f32[2,2,2,18,1,128]{5,4,3,2,1,0:T(1,128)S(1)}, u32[]{:S(2)}, u32[]{:S(2)}) collective-permute-start(f32[2,2,2,18,1,128]{5,4,3,2,1,0:T(1,128)S(1)} %get-tuple-element.46), channel_id=1, source_target_pairs={{0,1},{1,2},{2,3},{3,4},{4,5},{5,6},{6,7},{7,8},{8,9},{9,10},{10,1... | collective-permute-start | bytes 221192 | tf_op jit(solution)/shard_map/ppermute | solution.py:20
  42.7 1.0 copy-start.2
  45.7 6.2 %copy-start.3 = (s32[9360]{0:T(1024)S(1)}, s32[9360]{0:T(1024)}, u32[]{:S(2)}) copy-start(s32[9360]{0:T(1024)} %param.15) | copy-start | bytes 112324
  46.5 6.5 %collective-permute-start.9 = (f32[2,2,2,1,8,128]{5,4,3,2,1,0:T(8,128)S(1)}, f32[2,2,2,1,8,128]{5,4,3,2,1,0:T(8,128)S(1)}, u32[]{:S(2)}, u32[]{:S(2)}) collective-permute-start(f32[2,2,2,1,8,128]{5,4,3,2,1,0:T(8,128)S(1)} %get-tuple-element.87), channel_id=1, source_target_pairs={{64,0},{128,64},{192,128},{65,1},{129,65},{193,129},{66,2},{130,66... | collective-permute-start | bytes 98312 | tf_op jit(solution)/shard_map/ppermute | solution.py:21
  47.8 5.2 %collective-permute-start.8 = (f32[2,2,2,1,8,128]{5,4,3,2,1,0:T(8,128)S(1)}, f32[2,2,2,1,8,128]{5,4,3,2,1,0:T(8,128)S(1)}, u32[]{:S(2)}, u32[]{:S(2)}) collective-permute-start(f32[2,2,2,1,8,128]{5,4,3,2,1,0:T(8,128)S(1)} %get-tuple-element.86), channel_id=1, source_target_pairs={{0,64},{64,128},{128,192},{1,65},{65,129},{129,193},{2,66},{66,130... | collective-permute-start | bytes 98312 | tf_op jit(solution)/shard_map/ppermute | solution.py:20
  53.1 7.2 %collective-permute-start.11 = (f32[2,2,2,18,1,128]{5,4,3,2,1,0:T(1,128)S(1)}, f32[2,2,2,18,1,128]{5,4,3,2,1,0:T(1,128)S(1)}, u32[]{:S(2)}, u32[]{:S(2)}) collective-permute-start(f32[2,2,2,18,1,128]{5,4,3,2,1,0:T(1,128)S(1)} %get-tuple-element.43), channel_id=1, source_target_pairs={{1,0},{2,1},{3,2},{4,3},{5,4},{6,5},{7,6},{8,7},{9,8},{10,9},{11,1... | collective-permute-start | bytes 221192 | tf_op jit(solution)/shard_map/ppermute | solution.py:21
  55.1 6.6 %collective-permute-start.10 = (f32[2,2,2,18,1,128]{5,4,3,2,1,0:T(1,128)S(1)}, f32[2,2,2,18,1,128]{5,4,3,2,1,0:T(1,128)S(1)}, u32[]{:S(2)}, u32[]{:S(2)}) collective-permute-start(f32[2,2,2,18,1,128]{5,4,3,2,1,0:T(1,128)S(1)} %get-tuple-element.42), channel_id=1, source_target_pairs={{0,1},{1,2},{2,3},{3,4},{4,5},{5,6},{6,7},{7,8},{8,9},{9,10},{10,1... | collective-permute-start | bytes 221192 | tf_op jit(solution)/shard_map/ppermute | solution.py:20
  63.2 1.0 copy-start.7
  67.0 6.0 %collective-permute-start.13 = (f32[2,2,2,1,8,128]{5,4,3,2,1,0:T(8,128)S(1)}, f32[2,2,2,1,8,128]{5,4,3,2,1,0:T(8,128)S(1)}, u32[]{:S(2)}, u32[]{:S(2)}) collective-permute-start(f32[2,2,2,1,8,128]{5,4,3,2,1,0:T(8,128)S(1)} %get-tuple-element.75), channel_id=1, source_target_pairs={{64,0},{128,64},{192,128},{65,1},{129,65},{193,129},{66,2},{130,66... | collective-permute-start | bytes 98312 | tf_op jit(solution)/shard_map/ppermute | solution.py:21
  68.3 5.6 %collective-permute-start.12 = (f32[2,2,2,1,8,128]{5,4,3,2,1,0:T(8,128)S(1)}, f32[2,2,2,1,8,128]{5,4,3,2,1,0:T(8,128)S(1)}, u32[]{:S(2)}, u32[]{:S(2)}) collective-permute-start(f32[2,2,2,1,8,128]{5,4,3,2,1,0:T(8,128)S(1)} %get-tuple-element.74), channel_id=1, source_target_pairs={{0,64},{64,128},{128,192},{1,65},{65,129},{129,193},{2,66},{66,130... | collective-permute-start | bytes 98312 | tf_op jit(solution)/shard_map/ppermute | solution.py:20
  74.0 7.3 %collective-permute-start.15 = (f32[2,2,2,18,1,128]{5,4,3,2,1,0:T(1,128)S(1)}, f32[2,2,2,18,1,128]{5,4,3,2,1,0:T(1,128)S(1)}, u32[]{:S(2)}, u32[]{:S(2)}) collective-permute-start(f32[2,2,2,18,1,128]{5,4,3,2,1,0:T(1,128)S(1)} %get-tuple-element.39), channel_id=1, source_target_pairs={{1,0},{2,1},{3,2},{4,3},{5,4},{6,5},{7,6},{8,7},{9,8},{10,9},{11,1... | collective-permute-start | bytes 221192 | tf_op jit(solution)/shard_map/ppermute | solution.py:21
  76.1 6.5 %collective-permute-start.14 = (f32[2,2,2,18,1,128]{5,4,3,2,1,0:T(1,128)S(1)}, f32[2,2,2,18,1,128]{5,4,3,2,1,0:T(1,128)S(1)}, u32[]{:S(2)}, u32[]{:S(2)}) collective-permute-start(f32[2,2,2,18,1,128]{5,4,3,2,1,0:T(1,128)S(1)} %get-tuple-element.38), channel_id=1, source_target_pairs={{0,1},{1,2},{2,3},{3,4},{4,5},{5,6},{6,7},{7,8},{8,9},{9,10},{10,1... | collective-permute-start | bytes 221192 | tf_op jit(solution)/shard_map/ppermute | solution.py:20
  116.1 283.3 %copy-start.1 = (s32[16,8,128]{2,1,0:T(8,128)S(1)}, s32[16,8,128]{2,1,0:T(8,128)}, u32[]{:S(2)}) copy-start(s32[16,8,128]{2,1,0:T(8,128)} %param.14) | copy-start | bytes 196612
  116.1 1.1 copy-start.6
Sparse Core Ops, SparseCore 0:
  116.2 280.1 all-reduce.10
where the time goes:
time: 408 us; the launch traced here: 406 us
  waiting for transfers between devices  284 us (70%)
  starting transfers between devices  50.1 us (12%)
  local copies, waits for them, and re-layouts  29.9 us (7%)
  other arithmetic  26.6 us (7%)
  between operations  15.1 us (4%)
    unnamed x2, waiting for transfers between devices  278 us
    ppermute x8, starting transfers between devices, with_halo(): before = lax.ppermute(last, axis, up)  33.2 us
    ppermute x8, starting transfers between devices, with_halo(): after = lax.ppermute(leading, axis, down)  16.9 us
    pad x1, local copies, waits for them, and re-layouts, sum_blocks(): padded = jnp.pad(terms, ((0, 0), (4, 4), (4, 4), (0, 0)))  12.2 us
    reduce_sum x1, other arithmetic, sum_blocks(): return grouped.sum(axis=(2, 4, 6)).reshape(count, -1)  9.46 us
  transfers between devices with their start and end apart: 17, of which 6 were waited for; matrix products, arithmetic and copies ran while one was open for 2% of the time, Pallas kernels for 0%

commit v1 on v0

v1 whole, which is shorter than its diff:
```python
import functools

import jax
import jax.numpy as jnp
from jax import lax
from jax.experimental import pallas as pl
from jax.experimental.pallas import tpu as pltpu
from jax.sharding import PartitionSpec as P

MESH = pl.DeviceIdType.MESH
F32, BF16, I32 = jnp.float32, jnp.bfloat16, jnp.int32

YC, CC = 4, 2
THIRD, TWO_THIRDS = 1.0 / 3.0, 2.0 / 3.0
B0 = (0, 1, 4, 5)
A0 = (0, 1, 2, 3)


def roll_x(v, shift):
    rows = v.shape[0]
    return pltpu.roll(v.reshape(rows // 8, 8, 128), shift, 1).reshape(rows, 128)


def roll_y(v, shift):
    return pltpu.roll(v, shift, 1)


def harmonic(k, n):
    return 2.0 * k * n / (k + n)


def plane_sum(v):
    return v.reshape(-1, 8, 128).sum(axis=0)


def kernel(
    dims,
    bi_hbm, k_hbm, a_hbm, p_hbm, s_hbm, sup_hbm, blk_hbm, tab_hbm,
    v_out, cm_out, cr_out,
    bi, sup, kk, aa, pp, ss, blk, tab,
    v0, v1, sf, nn, tc, hx, hxs, hxr, hzs, hzr, hxs2, hxr2, hzs2, hzr2,
    rks, rkr, oh, xs, xb, es, cs, crv, hs, hr, ft,
    in_sem, out_sem, halo_s, halo_r, rk_s, rk_r, g_s, g_r, h_s, h_r,
):
    lx, plane, zc, own, width = dims
    gn, hn = lx * YC, zc * CC
    ml, mp = lax.axis_index("layer"), lax.axis_index("plane")
    my, mz, mc = mp // (zc * CC), (mp // CC) % zc, mp % CC

    def g_peer(r):
        dx, dy = r // YC, r % YC
        return ((ml + dx) % lx, (((my + dy) % YC) * zc + mz) * CC + mc)

    def g_inv(r):
        return ((lx - r // YC) % lx) * YC + (YC - r % YC) % YC

    def h_peer(r):
        dz, dc = r // CC, r % CC
        return (ml, (my * zc + (mz + dz) % zc) * CC + (mc + dc) % CC)

    def h_inv(r):
        return ((zc - r // CC) % zc) * CC + (CC - r % CC) % CC

    up_x, down_x = (ml, (mp + 1) % plane), (ml, (mp + plane - 1) % plane)
    up_z, down_z = ((ml + 1) % lx, mp), ((ml + lx - 1) % lx, mp)

    loads = [
        pltpu.make_async_copy(k_hbm, kk, in_sem.at[0]),
        pltpu.make_async_copy(bi_hbm, bi, in_sem.at[1]),
        pltpu.make_async_copy(sup_hbm, sup, in_sem.at[2]),
        pltpu.make_async_copy(blk_hbm, blk, in_sem.at[3]),
        pltpu.make_async_copy(tab_hbm, tab, in_sem.at[4]),
        pltpu.make_async_copy(a_hbm, aa, in_sem.at[5]),
        pltpu.make_async_copy(p_hbm, pp, in_sem.at[6]),
        pltpu.make_async_copy(s_hbm, ss, in_sem.at[7]),
    ]
    for load in loads:
        load.start()

    barrier = pltpu.get_barrier_semaphore()
    partners = [up_x, down_x]
    partners += [g_peer(r) for r in range(1, gn)] + [h_peer(r) for r in range(1, hn)]
    for who in partners:
        pl.semaphore_signal(barrier, inc=1, device_id=who, device_id_type=MESH)

    hx[...] = jnp.zeros_like(hx)

    lane = lax.broadcasted_iota(I32, (32, 128), 1)
    row = lax.broadcasted_iota(I32, (32, 128), 0)
    m, x = lane % 8, row % 8
    m1, x1 = m[:8], x[:8]
    is_m = [m == i for i in range(8)]
    is_x = [x == i for i in range(8)]

    loads[0].wait()
    loads[1].wait()
    loads[2].wait()

    def first(g, carry):
        rows = pl.ds(pl.multiple_of(g * 32, 32), 32)
        vals = []
        for s in range(8):
            on = sup[s, rows, :].astype(F32)
            sf[s, rows, :] = on
            vals.append(bi[s, rows, :] * on)
        total = sum(vals[1:], vals[0])
        inv = 1.0 / total
        for s in range(8):
            v0[s, rows, :] = vals[s] * inv
        return carry

    lax.fori_loop(0, 4, first, 0)

    def pack(v, xs_buf, zs_buf, extra):
        for i, s in enumerate(B0):
            xs_buf[0, extra + i] = v[s, pl.ds(0, 16, stride=8), :]
            xs_buf[1, extra + i] = v[s, pl.ds(7, 16, stride=8), :]
        for i, s in enumerate(A0):
            zs_buf[0, extra + i] = v[s, 0:8, :]
            zs_buf[1, extra + i] = v[s, 120:128, :]

    def exchange(xs_buf, xr_buf, zs_buf, zr_buf, base):
        copies = []
        for j, (src, dst, slot, who) in enumerate((
            (xs_buf.at[1], xr_buf.at[0], 0, up_x), (xs_buf.at[0], xr_buf.at[1], 1, down_x),
            (zs_buf.at[1], zr_buf.at[0], 2, up_z), (zs_buf.at[0], zr_buf.at[1], 3, down_z),
        )):
            copies.append(pltpu.make_async_remote_copy(
                src_ref=src, dst_ref=dst, send_sem=halo_s.at[base + j], recv_sem=halo_r.at[base + slot],
                device_id=who, device_id_type=MESH))
        for copy in copies:
            copy.start()
        return copies

    pack(v0, hxs, hzs, 1)
    hxs[0, 0] = kk[pl.ds(0, 16, stride=8), :]
    hxs[1, 0] = kk[pl.ds(7, 16, stride=8), :]
    hzs[0, 0] = kk[0:8, :]
    hzs[1, 0] = kk[120:128, :]

    pl.semaphore_wait(barrier, len(partners))
    sent = exchange(hxs, hxr, hzs, hzr, 0)

    loads[3].wait()
    loads[4].wait()
    label = blk[0, 0:1, :]
    for u, (j, r) in enumerate(((0, 0), (0, 4), (1, 0), (1, 4), (2, 0), (2, 4))):
        label = jnp.where(m1[0:1] == u, blk[j, r:r + 1, :], label)
    t_rows = tab.shape[0]
    l_hi, l_lo = label >> 7, label & 127
    w_iota = lax.broadcasted_iota(I32, (128, 128), 0)
    pick = jnp.where(w_iota == l_lo, 1.0, 0.0).astype(BF16)
    ranks = tab[...]
    parts = jnp.concatenate([(ranks >> 7).astype(F32), (ranks & 127).astype(F32)], axis=0).astype(BF16)
    looked = jnp.dot(parts, pick, preferred_element_type=F32)
    t_iota = lax.broadcasted_iota(I32, (t_rows, 128), 0)
    looked = looked[:t_rows] * 128.0 + looked[t_rows:]
    rank = jnp.sum(jnp.where(t_iota == l_hi, looked, 0.0), axis=0, keepdims=True)
    rank = jnp.where(m1[0:1] < 6, rank, -1.0).astype(I32)
    rks[...] = rank
    rkr[0] = rank
    rank_copies = []
    for r in range(1, gn):
        rank_copies.append(pltpu.make_async_remote_copy(
            src_ref=rks, dst_ref=rkr.at[g_inv(r)], send_sem=rk_s.at[r], recv_sem=rk_r.at[g_inv(r)],
            device_id=g_peer(r), device_id_type=MESH))
        rank_copies[-1].start()

    TYM, TYP, TYM1, TYP1, TXM, TXP, TXB, TZM, TZP, RD = range(10)
    k3 = kk[...]
    lane3 = lax.broadcasted_iota(I32, (128, 128), 1)
    x3 = lax.broadcasted_iota(I32, (128, 128), 0) % 8
    m3 = lane3 % 8
    tym = jnp.where(lane3 == 0, 0.0, harmonic(k3, roll_y(k3, 1)))
    typ = roll_y(tym, 127)
    tc[TYM] = tym
    tc[TYP] = typ
    tc[TYM1] = jnp.where(m3 == 4, 0.0, tym)
    tc[TYP1] = jnp.where(m3 == 3, 0.0, typ)
    txm = jnp.where(x3 == 0, 0.0, harmonic(k3, roll_x(k3, 1)))
    tc[TXM] = txm
    tc[TXP] = roll_x(txm, 7)
    tz = harmonic(k3[8:], k3[:-8])
    tc[TZM, 8:128, :] = tz
    tc[TZP, 0:120, :] = tz
    tc[TXB] = jnp.zeros((128, 128), F32)

    def inner(v):
        for g in range(4):
            lo, hi = 32 * g, 32 * g + 32
            rows = slice(lo, hi)
            coef = [tc[i, rows, :] for i in range(9)]
            vals = [v[s, rows, :] for s in range(8)]
            for s in range(8):
                here = vals[s]
                tm, tp = (coef[TYM1], coef[TYP1]) if s & 1 else (coef[TYM], coef[TYP])
                acc = tm * roll_y(jnp.where(is_m[7], vals[s ^ 1], here), 1)
                acc += tp * roll_y(jnp.where(is_m[0], vals[s ^ 1], here), 127)
                acc += coef[TXM] * roll_x(jnp.where(is_x[3], vals[s ^ 2], here), 1)
                acc += coef[TXP] * roll_x(jnp.where(is_x[4], vals[s ^ 2], here), 7)
                zero = jnp.zeros((8, 128), F32)
                if g in (1, 3):
                    below = coef[TZM][0:8] * v[s ^ 4, lo - 8:lo, :]
                elif g == 2 and s < 4:
                    below = coef[TZM][0:8] * v[s, lo - 8:lo, :]
                else:
                    below = zero
                if g in (0, 2):
                    above = coef[TZP][24:32] * v[s ^ 4, hi:hi + 8, :]
                elif g == 1 and s < 4:
                    above = coef[TZP][24:32] * v[s, hi:hi + 8, :]
                else:
                    above = zero
                acc += jnp.concatenate([below, coef[TZM][8:32] * here[0:24]], axis=0)
                acc += jnp.concatenate([coef[TZP][0:24] * here[8:32], above], axis=0)
                nn[s, rows, :] = acc

    def outer(v, new, zr_buf, extra):
        for g in range(4):
            rows = slice(32 * g, 32 * g + 32)
            rd, txb = tc[RD, rows, :], tc[TXB, rows, :]
            vals = []
            for s in range(8):
                near = nn[s, rows, :]
                if s in B0:
                    near += txb * hx[B0.index(s), rows, :]
                if s in A0 and g == 0:
                    near = jnp.concatenate(
                        [near[0:8] + tc[TZM, 0:8, :] * zr_buf[0, extra + s], near[8:32]], axis=0)
                if s in A0 and g == 3:
                    near = jnp.concatenate(
                        [near[0:24], near[24:32] + tc[TZP, 120:128, :] * zr_buf[1, extra + s]], axis=0)
                vals.append((v[s, rows, :] * THIRD + rd * near) * sf[s, rows, :])
            total = sum(vals[1:], vals[0])
            inv = 1.0 / total
            for s in range(8):
                new[s, rows, :] = vals[s] * inv

    def place_x(xr_buf, extra):
        for i in range(4):
            hx[i, pl.ds(0, 16, stride=8), :] = xr_buf[0, extra + i]
            hx[i, pl.ds(7, 16, stride=8), :] = xr_buf[1, extra + i]

    inner(v0)

    for load in loads[5:]:
        load.wait()
    for copy in sent:
        copy.wait_recv()

    k_first, k_last = kk[pl.ds(0, 16, stride=8), :], kk[pl.ds(7, 16, stride=8), :]
    tc[TXB, pl.ds(0, 16, stride=8), :] = jnp.where(mp > 0, harmonic(k_first, hxr[0, 0]), 0.0)
    tc[TXB, pl.ds(7, 16, stride=8), :] = jnp.where(mp < plane - 1, harmonic(k_last, hxr[1, 0]), 0.0)
    tc[TZM, 0:8, :] = jnp.where(ml > 0, harmonic(kk[0:8, :], hzr[0, 0]), 0.0)
    tc[TZP, 120:128, :] = jnp.where(ml < lx - 1, harmonic(kk[120:128, :], hzr[1, 0]), 0.0)
    diag = aa[...] + tc[TYM] + tc[TYP] + tc[TXM] + tc[TXP] + tc[TXB] + tc[TZM] + tc[TZP]
    tc[RD] = TWO_THIRDS / diag

    place_x(hxr, 1)
    outer(v0, v1, hzr, 1)

    pack(v1, hxs2, hzs2, 0)
    sent2 = exchange(hxs2, hxr2, hzs2, hzr2, 4)
    inner(v1)

    n_idx = hn * width
    idx = lax.broadcasted_iota(I32, (n_idx, 128), 0)
    peer = jnp.zeros_like(idx)
    for t in range(1, hn):
        peer += jnp.where(idx >= t * width, 1, 0)
    col = idx - peer * width
    dz, dc = peer // CC, peer % CC
    pz, pc = mz + dz, mc + dc
    pz = jnp.where(pz >= zc, pz - zc, pz)
    pc = jnp.where(pc >= CC, pc - CC, pc)
    dev = ml * plane + (my * zc + pz) * CC + pc
    want = dev * own + col
    wants = [jnp.where(col + q * width < own, want + q * width, -7) for q in range(4)]
    for copy in rank_copies:
        copy.wait_recv()

    def build(r, carry):
        lanes = pl.ds(pl.multiple_of(r * 128, 128), 128)
        have = rkr[r]
        for q in range(4):
            oh[q * n_idx:(q + 1) * n_idx, lanes] = jnp.where(wants[q] == have, 1.0, 0.0).astype(BF16)
        return carry

    lax.fori_loop(0, gn, build, 0)

    for copy in sent2:
        copy.wait_recv()
    place_x(hxr2, 0)
    outer(v1, v0, hzr2, 0)
    store = pltpu.make_async_copy(v0, v_out, out_sem.at[0])
    store.start()

    r_sum = [[None] * 4 for _ in range(9)]
    qx = [[None] * 4 for _ in range(9)]
    qy = [[None] * 4 for _ in range(9)]
    for g in range(4):
        lo = 32 * g
        rows = slice(lo, lo + 32)
        tym, typ, txm, txp = (tc[i, rows, :] for i in (TYM, TYP, TXM, TXP))
        sx0 = jnp.where(is_x[3], txp, 0.0) + jnp.where(is_x[4], txm, 0.0)
        sx1 = sx0 + tc[TXB, rows, :]
        sy0 = jnp.where(is_m[7], typ, 0.0) + jnp.where(is_m[0], tym, 0.0)
        sy1 = sy0 + jnp.where(is_m[3], typ, 0.0) + jnp.where(is_m[4], tym, 0.0)
        zero = jnp.zeros((24, 128), F32)
        lower, upper = tc[TZM, lo:lo + 8, :], tc[TZP, lo + 24:lo + 32, :]
        acc = aa[rows, :]
        if g in (0, 2):
            swap_t, far = upper, slice(lo + 32, lo + 40)
            az0 = acc + jnp.concatenate([zero, upper], axis=0)
            az1 = az0 + jnp.concatenate([lower, zero], axis=0)
        else:
            swap_t, far = lower, slice(lo - 8, lo)
            az0 = acc + jnp.concatenate([lower, zero], axis=0)
            az1 = az0 + jnp.concatenate([zero, upper], axis=0)
        dxy = [[az + sx for sx in (sx0, sx1)] for az in (az0, az1)]
        for s in range(8):
            a, b, c = s >> 2, (s >> 1) & 1, s & 1
            here = v0[s, rows, :]
            d = dxy[a][b] + (sy1 if c else sy0)
            r_sum[s][g] = plane_sum(d * here) - swap_t * v0[s ^ 4, far, :]
            qx[s][g] = plane_sum(sx0 * here)
            qy[s][g] = plane_sum(sy0 * here)
        here = pp[rows, :]
        d = dxy[0][0] + sy0
        r_sum[8][g] = plane_sum(d * here - ss[rows, :]) - swap_t * pp[far, :]
        qx[8][g] = plane_sum(sx0 * here)
        qy[8][g] = plane_sum(sy0 * here)

    def x_swap(q):
        return jnp.where(x1 == 3, roll_x(q, 7), jnp.where(x1 == 4, roll_x(q, 1), 0.0))

    def y_swap(q):
        return jnp.where(m1 == 7, roll_y(q, 127), jnp.where(m1 == 0, roll_y(q, 1), 0.0))

    full = [[None] * 4 for _ in range(9)]
    for s in range(9):
        for g in range(4):
            sx, sy = (s ^ 2, s ^ 1) if s < 8 else (8, 8)
            full[s][g] = r_sum[s][g] - x_swap(qx[sx][g]) - y_swap(qy[sy][g])

    nil = jnp.zeros((8, 128), F32)
    for j in range(3):
        for b in (1, 0):
            for pz in range(3):
                if pz == 1:
                    groups, a = ((0,), (1, 2), (3,))[j], 0
                elif pz == 0:
                    groups, a = ((), (1,), (3,))[j], 1
                else:
                    groups, a = ((0,), (2,), ())[j], 1
                for py in range(3):
                    s = 4 * a + 2 * b + (0 if py == 1 else 1)
                    term = nil
                    for i, g in enumerate(groups):
                        term = full[s][g] if i == 0 else term + full[s][g]
                    if py == 0:
                        term = jnp.where(m1 < 4, term, 0.0)
                    elif py == 2:
                        term = jnp.where(m1 >= 4, term, 0.0)
                    at = (1 - b) * 9 + 3 * pz + py
                    es[j, 8 * at:8 * at + 8, :] = term
        groups = ((0,), (1, 2), (3,))[j]
        term = full[8][groups[0]]
        for g in groups[1:]:
            term += full[8][g]
        es[j, 144:152, :] = -term
        es[j, 152:192, :] = jnp.zeros((40, 128), F32)

    m24 = lax.broadcasted_iota(I32, (24, 128), 1) % 8
    rows_out = jnp.zeros((24, 128), F32)
    for j in range(3):
        for xi in range(2):
            t = es[j, pl.ds(4 * xi, 24, stride=8), :]
            for i in range(1, 4):
                t += es[j, pl.ds(4 * xi + i, 24, stride=8), :]
            t += roll_y(t, 127)
            t += roll_y(t, 126)
            t += roll_y(t, 124)
            u = 2 * j + xi
            rows_out = jnp.where(m24 == u, roll_y(t, u) if u else t, rows_out)
    cs[...] = rows_out[0:20]
    crv[0] = rows_out[0:20]

    g_copies = []
    for r in range(1, gn):
        g_copies.append(pltpu.make_async_remote_copy(
            src_ref=cs, dst_ref=crv.at[g_inv(r)], send_sem=g_s.at[r], recv_sem=g_r.at[g_inv(r)],
            device_id=g_peer(r), device_id_type=MESH))
        g_copies[-1].start()

    xs[...] = jnp.zeros_like(xs)
    xb[64:128, :] = jnp.zeros((64, gn * 128), BF16)
    row20 = lax.broadcasted_iota(I32, (20, 128), 0)
    odd20 = lax.broadcasted_iota(I32, (20, 128), 1) % 2 == 1
    odd9 = lax.broadcasted_iota(I32, (9, 128), 1) % 2 == 1
    drop = (row20 < 9) & odd20
    for copy in g_copies:
        copy.wait_recv()

    def spread(r, carry):
        lanes = pl.ds(pl.multiple_of(r * 128, 128), 128)
        got = crv[r]
        xs[0:20, :] = jnp.where(drop, 0.0, got)
        xs[19:28, :] = jnp.where(odd9, got[0:9], 0.0)
        vals = xs[...]
        high = vals.astype(BF16)
        xb[0:32, lanes] = high
        xb[32:64, lanes] = (vals - high.astype(F32)).astype(BF16)
        return carry

    lax.fori_loop(0, gn, spread, 0)
    routed = lax.dot_general(
        oh[...], xb[...], (((1,), (1,)), ((), ())), preferred_element_type=F32)
    lane_n = lax.broadcasted_iota(I32, (n_idx, 128), 1)
    packed = jnp.zeros((n_idx, 128), F32)
    for q in range(4):
        part = routed[q * n_idx:(q + 1) * n_idx]
        both = jnp.where(lane_n < 32, part + roll_y(part, 96), 0.0)
        packed += roll_y(both, 32 * q) if q else both
    for r in range(hn):
        hs[r] = packed[r * width:(r + 1) * width]

    h_copies = []
    for r in range(1, hn):
        h_copies.append(pltpu.make_async_remote_copy(
            src_ref=hs.at[r], dst_ref=hr.at[h_inv(r)], send_sem=h_s.at[r], recv_sem=h_r.at[h_inv(r)],
            device_id=h_peer(r), device_id_type=MESH))
        h_copies[-1].start()
    ft[...] = jnp.zeros_like(ft)
    for copy in h_copies:
        copy.wait_recv()
    final = hs[0]
    for r in range(1, hn):
        final += hr[r]
    ft[0:width, :] = final
    turned = ft[...].T
    lane_f = lax.broadcasted_iota(I32, (32, 128), 1)
    done = jnp.zeros((32, 128), F32)
    for q in range(4):
        part = turned[32 * q:32 * q + 32]
        here = (lane_f >= q * width) & (lane_f < (q + 1) * width)
        done = jnp.where(here, roll_y(part, q * width) if q else part, done)
    for pz in range(3):
        for px, base in ((0, 19), (1, 9), (2, 0)):
            k = 9 * pz + 3 * px
            cm_out[k:k + 3, :] = done[base + 3 * pz:base + 3 * pz + 3, 0:own]
    cr_out[...] = done[18:19, 0:own]

    store.wait()
    for copy in sent + sent2 + rank_copies + g_copies + h_copies:
        copy.wait_send()


def per_device(sizes, basis_init, permeability, accumulation, pressure, source, support, block_of, curve_rank):
    lx, plane = sizes
    zc = plane // (YC * CC)
    gn, hn = lx * YC, zc * CC
    devices = lx * plane
    own = (curve_rank.shape[0] + devices - 1) // devices
    width = (own + 3) // 4
    flat = lambda v: v.reshape(v.shape[:-3] + (128, 128))
    t_rows = -(-curve_rank.shape[0] // 2048) * 16
    table = jnp.pad(curve_rank, (0, t_rows * 128 - curve_rank.shape[0])).reshape(t_rows, 128)
    labels = jnp.stack([block_of[0], block_of[4], block_of[12]])
    anywhere = pl.BlockSpec(memory_space=pl.ANY)
    vmem = pl.BlockSpec(memory_space=pltpu.VMEM)
    dma = pltpu.SemaphoreType.DMA
    cells = lambda *lead: pltpu.VMEM(lead + (128, 128), F32)
    basis, matrix, residual = pl.pallas_call(
        functools.partial(kernel, (lx, plane, zc, own, width)),
        out_shape=(
            jax.ShapeDtypeStruct((8, 128, 128), F32),
            jax.ShapeDtypeStruct((27, own), F32),
            jax.ShapeDtypeStruct((1, own), F32),
        ),
        in_specs=[anywhere] * 8,
        out_specs=(anywhere, vmem, vmem),
        scratch_shapes=[
            cells(8), pltpu.VMEM((8, 128, 128), I32), cells(), cells(), cells(), cells(),
            pltpu.VMEM((3, 8, 128), I32), pltpu.VMEM((t_rows, 128), I32),
            cells(8), cells(8), cells(8), cells(8), cells(10), cells(4),
            pltpu.VMEM((2, 5, 16, 128), F32), pltpu.VMEM((2, 5, 16, 128), F32),
            pltpu.VMEM((2, 5, 8, 128), F32), pltpu.VMEM((2, 5, 8, 128), F32),
            pltpu.VMEM((2, 4, 16, 128), F32), pltpu.VMEM((2, 4, 16, 128), F32),
            pltpu.VMEM((2, 4, 8, 128), F32), pltpu.VMEM((2, 4, 8, 128), F32),
            pltpu.VMEM((1, 128), I32), pltpu.VMEM((gn, 1, 128), I32),
            pltpu.VMEM((4 * hn * width, gn * 128), BF16),
            pltpu.VMEM((32, 128), F32), pltpu.VMEM((128, gn * 128), BF16),
            pltpu.VMEM((3, 192, 128), F32),
            pltpu.VMEM((20, 128), F32), pltpu.VMEM((gn, 20, 128), F32),
            pltpu.VMEM((hn, width, 128), F32), pltpu.VMEM((hn, width, 128), F32),
            pltpu.VMEM((128, 128), F32),
            dma((8,)), dma((1,)), dma((8,)), dma((8,)),
            dma((gn,)), dma((gn,)), dma((gn,)), dma((gn,)), dma((hn,)), dma((hn,)),
        ],
        compiler_params=pltpu.CompilerParams(
            collective_id=0, has_side_effects=True, vmem_limit_bytes=40 * 1024 * 1024),
        cost_estimate=pl.CostEstimate(flops=20_000_000, bytes_accessed=2_000_000, transcendentals=0),
    )(
        flat(basis_init), flat(permeability), flat(accumulation), flat(pressure), flat(source),
        flat(support), labels, table,
    )
    return basis.reshape(basis_init.shape), matrix, residual.reshape(own)


def solution(mesh):
    return jax.shard_map(
        functools.partial(per_device, (mesh.shape["layer"], mesh.shape["plane"])),
        mesh=mesh,
        in_specs=(
            P(None, "layer", "plane", None),
            P("layer", "plane", None),
            P("layer", "plane", None),
            P("layer", "plane", None),
            P("layer", "plane", None),
            P(None, "layer", "plane", None),
            P("layer", "plane", None),
            P(),
        ),
        out_specs=(
            P(None, "layer", "plane", None),
            P(None, ("layer", "plane")),
            P(("layer", "plane")),
        ),
        check_vma=False,
    )
```

time: 408 us -> 39.8 us (0.10)
  waiting for transfers between devices: 284 us -> 0 us
  starting transfers between devices: 50.1 us -> 0 us
  Pallas kernels: 0 us -> 31.5 us
  other arithmetic: 26.6 us -> 0.01 us
  local copies, waits for them, and re-layouts: 29.9 us -> 7.21 us
  between operations: 15.1 us -> 0.67 us
    unnamed x2 -> x0, waiting for transfers between devices: 278 us -> none
    ppermute x16 -> x0, starting transfers between devices: 50.1 us -> none  [the longest x8 33.2 us: with_halo(): before = lax.ppermute(last, axis, up)]
    pallas_call x0 -> x1, Pallas kernels: none -> 31.5 us  [per_device(): pl.pallas_call(functools.partial(kernel, (lx, plane, zc, own, width)), ou...]
    reduce_sum x4 -> x0, other arithmetic: 14.5 us -> none  [the longest x1 9.46 us: sum_blocks(): return grouped.sum(axis=(2, 4, 6)).reshape(count, -1)]
    pad x1 -> x0, local copies, waits for them, and re-layouts: 12.2 us -> none  [sum_blocks(): padded = jnp.pad(terms, ((0, 0), (4, 4), (4, 4), (0, 0)))]
    ppermute x16 -> x0, waiting for transfers between devices: 5.96 us -> none  [the longest x8 5.93 us: with_halo(): before = lax.ppermute(last, axis, up)]
    concatenate x9 -> x0, other arithmetic: 4.47 us -> none  [the longest x4 4.24 us: with_halo(): shard = jnp.concatenate([before, shard, after], axis=dim)]
  transfers between devices with their start and end apart: 17 -> 0, of which waited for: 6 -> 0; matrix products, arithmetic and copies ran while one was open for 2% -> 0% of each run, Pallas kernels for 0% -> 0%
where the time goes in v1:
time: 39.8 us; the launch traced here: 39.4 us
  Pallas kernels  31.5 us (79%)
  local copies, waits for them, and re-layouts  7.21 us (18%)
  between operations  0.67 us (2%)
    pallas_call x1, Pallas kernels, per_device(): pl.pallas_call(functools.partial(kernel, (lx, plane, zc, own, width)), ou...  31.5 us
    unnamed x15, local copies, waits for them, and re-layouts  5.68 us

profile of v1, /device:TPU:1, one launch (start us, length us, event | category | flops | bytes accessed | tf_op | source)
XLA Modules:
  0.0 39.4 jit_solution(16988376272774972747)
XLA Ops:
  0.6 0.0 copy-start.2
  0.6 0.0 copy-start.3
  0.7 0.8 %fusion = (s32[1,8,128]{2,1,0:T(8,128)S(1)}, s32[1,8,128]{2,1,0:T(8,128)S(1)}, s32[1,8,128]{2,1,0:T(8,128)S(1)}) fusion(s32[16,8,128]{2,1,0:T(8,128)} %param.14), kind=kLoop, calls=%fused_computation.2 | loop fusion | bytes 24576 | tf_op jit(solution)/shard_map/slice | solution.py:469
  1.4 0.8 %pad_bitcast_fusion.tab_hbm = s32[80,128]{1,0:T(8,128)S(1)} fusion(s32[9360]{0:T(1024)} %param.15), kind=kLoop, calls=%fused_computation | loop fusion | bytes 78400 | tf_op jit(solution)/shard_map/reshape | solution.py:468
  2.2 0.0 copy-done.2
  2.2 0.0 copy-done.3
  2.2 0.0 copy-start
  2.2 1.0 %copy-done = f32[8,16,8,128]{3,2,1,0:T(8,128)S(1)} copy-done((f32[8,16,8,128]{3,2,1,0:T(8,128)S(1)}, f32[8,16,8,128]{3,2,1,0:T(8,128)}, u32[]{:S(2)}) %copy-start) | copy-done | bytes 524312
  3.2 0.0 copy-start.1
  3.3 1.0 %copy-done.1 = s32[8,16,8,128]{3,2,1,0:T(8,128)S(1)} copy-done((s32[8,16,8,128]{3,2,1,0:T(8,128)S(1)}, s32[8,16,8,128]{3,2,1,0:T(8,128)}, u32[]{:S(2)}) %copy-start.1) | copy-done | bytes 524312
  4.3 0.0 copy-start.4
  4.3 0.8 %copy-done.4 = f32[16,8,128]{2,1,0:T(8,128)S(1)} copy-done((f32[16,8,128]{2,1,0:T(8,128)S(1)}, f32[16,8,128]{2,1,0:T(8,128)}, u32[]{:S(2)}) %copy-start.4) | copy-done | bytes 65560
  5.1 0.0 copy-start.5
  5.1 0.8 %copy-done.5 = f32[16,8,128]{2,1,0:T(8,128)S(1)} copy-done((f32[16,8,128]{2,1,0:T(8,128)S(1)}, f32[16,8,128]{2,1,0:T(8,128)}, u32[]{:S(2)}) %copy-start.5) | copy-done | bytes 65560
  6.0 31.5 %shard_map.103 = (f32[8,128,128]{2,1,0:T(8,128)S(1)}, f32[27,37]{1,0:T(8,128)S(1)}, f32[1,37]{1,0:T(1,128)S(1)}) custom-call(f32[8,128,128]{2,1,0:T(8,128)S(1)} %bitcast.11, f32[128,128]{1,0:T(8,128)S(1)} %bitcast.13, f32[128,128]{1,0:T(8,128)S(1)} %bitcast.14, f32[128,128]{1,0:T(8,128)S(1)} %bitcast.15, f32[128,128]{1,0:T(8,128)S(1)} %bitcast.16, ...), custom_call_target="tpu_custom_call" | custom-call | flops 20000000 | bytes 2000000 | tf_op jit(solution)/shard_map/pallas_call | solution.py:474
  37.5 0.8 %copy.14 = f32[8,16,8,128]{3,2,1,0:T(8,128)} copy(f32[8,16,8,128]{3,2,1,0:T(8,128)S(1)} %bitcast.10) | data formatting | bytes 1048576
  38.3 0.6 %copy.15 = f32[27,37]{1,0:T(8,128)} copy(f32[27,37]{1,0:T(8,128)S(1)} %get-tuple-element.16) | data formatting | bytes 7992
  38.9 0.5 %copy.16 = f32[37]{0:T(128)} copy(f32[37]{0:T(128)S(1)} %bitcast.17) | data formatting | bytes 296
  (1 shorter events, 0.0 us)
Async XLA Ops:
  0.6 1.6 %copy-start.2 = (f32[16,8,128]{2,1,0:T(8,128)S(1)}, f32[16,8,128]{2,1,0:T(8,128)}, u32[]{:S(2)}) copy-start(f32[16,8,128]{2,1,0:T(8,128)} %param.9) | copy-start | bytes 196612
  0.6 1.6 %copy-start.3 = (f32[16,8,128]{2,1,0:T(8,128)S(1)}, f32[16,8,128]{2,1,0:T(8,128)}, u32[]{:S(2)}) copy-start(f32[16,8,128]{2,1,0:T(8,128)} %param.10) | copy-start | bytes 196612
  2.2 1.0 %copy-start = (f32[8,16,8,128]{3,2,1,0:T(8,128)S(1)}, f32[8,16,8,128]{3,2,1,0:T(8,128)}, u32[]{:S(2)}) copy-start(f32[8,16,8,128]{3,2,1,0:T(8,128)} %param.8) | copy-start | bytes 1572868
  3.2 1.0 %copy-start.1 = (s32[8,16,8,128]{3,2,1,0:T(8,128)S(1)}, s32[8,16,8,128]{3,2,1,0:T(8,128)}, u32[]{:S(2)}) copy-start(s32[8,16,8,128]{3,2,1,0:T(8,128)} %param.13) | copy-start | bytes 1572868
  4.3 0.8 %copy-start.4 = (f32[16,8,128]{2,1,0:T(8,128)S(1)}, f32[16,8,128]{2,1,0:T(8,128)}, u32[]{:S(2)}) copy-start(f32[16,8,128]{2,1,0:T(8,128)} %param.11) | copy-start | bytes 196612
  5.1 0.8 %copy-start.5 = (f32[16,8,128]{2,1,0:T(8,128)S(1)}, f32[16,8,128]{2,1,0:T(8,128)}, u32[]{:S(2)}) copy-start(f32[16,8,128]{2,1,0:T(8,128)} %param.12) | copy-start | bytes 196612

commit v2 on v1

--- a/solution.py
+++ b/solution.py
@@ -11,6 +11,7 @@
 F32, BF16, I32 = jnp.float32, jnp.bfloat16, jnp.int32
 
 YC, CC = 4, 2
+VMEM_GRANT = 60 * 1024 * 1024
 THIRD, TWO_THIRDS = 1.0 / 3.0, 2.0 / 3.0
 B0 = (0, 1, 4, 5)
 A0 = (0, 1, 2, 3)
@@ -35,11 +36,11 @@
 
 def kernel(
     dims,
-    bi_hbm, k_hbm, a_hbm, p_hbm, s_hbm, sup_hbm, blk_hbm, tab_hbm,
-    v_out, cm_out, cr_out,
-    bi, sup, kk, aa, pp, ss, blk, tab,
-    v0, v1, sf, nn, tc, hx, hxs, hxr, hzs, hzr, hxs2, hxr2, hzs2, hzr2,
-    rks, rkr, oh, xs, xb, es, cs, crv, hs, hr, ft,
+    bi_hbm, k_hbm, a_hbm, p_hbm, s_hbm, sup_hbm, blk_hbm, cr_hbm,
+    v_out, f_out,
+    bi, sup, kk, aa, pp, ss, blk, cr1, tab,
+    v0, v1, sf, nn, tc, ec, hx, hxs, hxr, hzs, hzr, hxs2, hxr2, hzs2, hzr2,
+    rks, rkr, oh, xb, es, cs, crv, hs, hr,
     in_sem, out_sem, halo_s, halo_r, rk_s, rk_r, g_s, g_r, h_s, h_r,
 ):
     lx, plane, zc, own, width = dims
@@ -68,12 +69,13 @@
         pltpu.make_async_copy(k_hbm, kk, in_sem.at[0]),
         pltpu.make_async_copy(bi_hbm, bi, in_sem.at[1]),
         pltpu.make_async_copy(sup_hbm, sup, in_sem.at[2]),
-        pltpu.make_async_copy(blk_hbm, blk, in_sem.at[3]),
-        pltpu.make_async_copy(tab_hbm, tab, in_sem.at[4]),
-        pltpu.make_async_copy(a_hbm, aa, in_sem.at[5]),
-        pltpu.make_async_copy(p_hbm, pp, in_sem.at[6]),
-        pltpu.make_async_copy(s_hbm, ss, in_sem.at[7]),
+        pltpu.make_async_copy(a_hbm, aa, in_sem.at[3]),
+        pltpu.make_async_copy(cr_hbm, cr1, in_sem.at[4]),
+        pltpu.make_async_copy(p_hbm, pp, in_sem.at[5]),
+        pltpu.make_async_copy(s_hbm, ss, in_sem.at[6]),
     ]
+    for j, z in enumerate((0, 4, 12)):
+        loads.append(pltpu.make_async_copy(blk_hbm.at[pl.ds(8 * z, 8)], blk.at[j], in_sem.at[7 + j]))
     for load in loads:
         load.start()
 
@@ -93,78 +95,6 @@
     is_x = [x == i for i in range(8)]
 
     loads[0].wait()
-    loads[1].wait()
-    loads[2].wait()
-
-    def first(g, carry):
-        rows = pl.ds(pl.multiple_of(g * 32, 32), 32)
-        vals = []
-        for s in range(8):
-            on = sup[s, rows, :].astype(F32)
-            sf[s, rows, :] = on
-            vals.append(bi[s, rows, :] * on)
-        total = sum(vals[1:], vals[0])
-        inv = 1.0 / total
-        for s in range(8):
-            v0[s, rows, :] = vals[s] * inv
-        return carry
-
-    lax.fori_loop(0, 4, first, 0)
-
-    def pack(v, xs_buf, zs_buf, extra):
-        for i, s in enumerate(B0):
-            xs_buf[0, extra + i] = v[s, pl.ds(0, 16, stride=8), :]
-            xs_buf[1, extra + i] = v[s, pl.ds(7, 16, stride=8), :]
-        for i, s in enumerate(A0):
-            zs_buf[0, extra + i] = v[s, 0:8, :]
-            zs_buf[1, extra + i] = v[s, 120:128, :]
-
-    def exchange(xs_buf, xr_buf, zs_buf, zr_buf, base):
-        copies = []
-        for j, (src, dst, slot, who) in enumerate((
-            (xs_buf.at[1], xr_buf.at[0], 0, up_x), (xs_buf.at[0], xr_buf.at[1], 1, down_x),
-            (zs_buf.at[1], zr_buf.at[0], 2, up_z), (zs_buf.at[0], zr_buf.at[1], 3, down_z),
-        )):
-            copies.append(pltpu.make_async_remote_copy(
-                src_ref=src, dst_ref=dst, send_sem=halo_s.at[base + j], recv_sem=halo_r.at[base + slot],
-                device_id=who, device_id_type=MESH))
-        for copy in copies:
-            copy.start()
-        return copies
-
-    pack(v0, hxs, hzs, 1)
-    hxs[0, 0] = kk[pl.ds(0, 16, stride=8), :]
-    hxs[1, 0] = kk[pl.ds(7, 16, stride=8), :]
-    hzs[0, 0] = kk[0:8, :]
-    hzs[1, 0] = kk[120:128, :]
-
-    pl.semaphore_wait(barrier, len(partners))
-    sent = exchange(hxs, hxr, hzs, hzr, 0)
-
-    loads[3].wait()
-    loads[4].wait()
-    label = blk[0, 0:1, :]
-    for u, (j, r) in enumerate(((0, 0), (0, 4), (1, 0), (1, 4), (2, 0), (2, 4))):
-        label = jnp.where(m1[0:1] == u, blk[j, r:r + 1, :], label)
-    t_rows = tab.shape[0]
-    l_hi, l_lo = label >> 7, label & 127
-    w_iota = lax.broadcasted_iota(I32, (128, 128), 0)
-    pick = jnp.where(w_iota == l_lo, 1.0, 0.0).astype(BF16)
-    ranks = tab[...]
-    parts = jnp.concatenate([(ranks >> 7).astype(F32), (ranks & 127).astype(F32)], axis=0).astype(BF16)
-    looked = jnp.dot(parts, pick, preferred_element_type=F32)
-    t_iota = lax.broadcasted_iota(I32, (t_rows, 128), 0)
-    looked = looked[:t_rows] * 128.0 + looked[t_rows:]
-    rank = jnp.sum(jnp.where(t_iota == l_hi, looked, 0.0), axis=0, keepdims=True)
-    rank = jnp.where(m1[0:1] < 6, rank, -1.0).astype(I32)
-    rks[...] = rank
-    rkr[0] = rank
-    rank_copies = []
-    for r in range(1, gn):
-        rank_copies.append(pltpu.make_async_remote_copy(
-            src_ref=rks, dst_ref=rkr.at[g_inv(r)], send_sem=rk_s.at[r], recv_sem=rk_r.at[g_inv(r)],
-            device_id=g_peer(r), device_id_type=MESH))
-        rank_copies[-1].start()
 
     TYM, TYP, TYM1, TYP1, TXM, TXP, TXB, TZM, TZP, RD = range(10)
     k3 = kk[...]
@@ -184,6 +114,51 @@
     tc[TZM, 8:128, :] = tz
     tc[TZP, 0:120, :] = tz
     tc[TXB] = jnp.zeros((128, 128), F32)
+
+    loads[1].wait()
+    loads[2].wait()
+
+    for g in range(4):
+        rows = slice(32 * g, 32 * g + 32)
+        vals = []
+        for s in range(8):
+            on = sup[s, rows, :].astype(F32)
+            sf[s, rows, :] = on
+            vals.append(bi[s, rows, :] * on)
+        total = sum(vals[1:], vals[0])
+        inv = 1.0 / total
+        for s in range(8):
+            v0[s, rows, :] = vals[s] * inv
+
+    def pack(v, xs_buf, zs_buf, extra):
+        for i, s in enumerate(B0):
+            xs_buf[0, extra + i] = v[s, pl.ds(0, 16, stride=8), :]
+            xs_buf[1, extra + i] = v[s, pl.ds(7, 16, stride=8), :]
+        for i, s in enumerate(A0):
+            zs_buf[0, extra + i] = v[s, 0:8, :]
+            zs_buf[1, extra + i] = v[s, 120:128, :]
+
+    def exchange(xs_buf, xr_buf, zs_buf, zr_buf, base):
+        copies = []
+        for j, (src, dst, slot, who) in enumerate((
+            (xs_buf.at[1], xr_buf.at[0], 0, up_x), (xs_buf.at[0], xr_buf.at[1], 1, down_x),
+            (zs_buf.at[1], zr_buf.at[0], 2, up_z), (zs_buf.at[0], zr_buf.at[1], 3, down_z),
+        )):
+            copies.append(pltpu.make_async_remote_copy(
+                src_ref=src, dst_ref=dst, send_sem=halo_s.at[base + j], recv_sem=halo_r.at[base + slot],
+                device_id=who, device_id_type=MESH))
+        for copy in copies:
+            copy.start()
+        return copies
+
+    pack(v0, hxs, hzs, 1)
+    hxs[0, 0] = kk[pl.ds(0, 16, stride=8), :]
+    hxs[1, 0] = kk[pl.ds(7, 16, stride=8), :]
+    hzs[0, 0] = kk[0:8, :]
+    hzs[1, 0] = kk[120:128, :]
+
+    pl.semaphore_wait(barrier, len(partners))
+    sent = exchange(hxs, hxr, hzs, hzr, 0)
 
     def inner(v):
         for g in range(4):
@@ -243,7 +218,7 @@
 
     inner(v0)
 
-    for load in loads[5:]:
+    for load in loads[3:]:
         load.wait()
     for copy in sent:
         copy.wait_recv()
@@ -263,41 +238,46 @@
     sent2 = exchange(hxs2, hxr2, hzs2, hzr2, 4)
     inner(v1)
 
-    n_idx = hn * width
-    idx = lax.broadcasted_iota(I32, (n_idx, 128), 0)
-    peer = jnp.zeros_like(idx)
-    for t in range(1, hn):
-        peer += jnp.where(idx >= t * width, 1, 0)
-    col = idx - peer * width
-    dz, dc = peer // CC, peer % CC
-    pz, pc = mz + dz, mc + dc
-    pz = jnp.where(pz >= zc, pz - zc, pz)
-    pc = jnp.where(pc >= CC, pc - CC, pc)
-    dev = ml * plane + (my * zc + pz) * CC + pc
-    want = dev * own + col
-    wants = [jnp.where(col + q * width < own, want + q * width, -7) for q in range(4)]
-    for copy in rank_copies:
-        copy.wait_recv()
-
-    def build(r, carry):
-        lanes = pl.ds(pl.multiple_of(r * 128, 128), 128)
-        have = rkr[r]
-        for q in range(4):
-            oh[q * n_idx:(q + 1) * n_idx, lanes] = jnp.where(wants[q] == have, 1.0, 0.0).astype(BF16)
-        return carry
-
-    lax.fori_loop(0, gn, build, 0)
-
-    for copy in sent2:
-        copy.wait_recv()
-    place_x(hxr2, 0)
-    outer(v1, v0, hzr2, 0)
-    store = pltpu.make_async_copy(v0, v_out, out_sem.at[0])
-    store.start()
+    label = blk[0, 0:1, :]
+    for u, (j, r) in enumerate(((0, 0), (0, 4), (1, 0), (1, 4), (2, 0), (2, 4))):
+        label = jnp.where(m1[0:1] == u, blk[j, r:r + 1, :], label)
+    t_rows = tab.shape[0]
+    labels = cr1.shape[0]
+    tab[labels // 128:, :] = jnp.zeros((t_rows - labels // 128, 128), I32)
+    for t in range(labels // 128):
+        tab[t:t + 1, :] = cr1[pl.ds(t * 128, 128)].reshape(1, 128)
+    if labels % 128:
+        t = labels // 128
+        tab[t:t + 1, 0:labels % 128] = cr1[pl.ds(t * 128, labels % 128)].reshape(1, labels % 128)
+    l_hi, l_lo = label >> 7, label & 127
+    w_iota = lax.broadcasted_iota(I32, (128, 128), 0)
+    pick = jnp.where(w_iota == l_lo, 1.0, 0.0).astype(BF16)
+    ranks = tab[...]
+    parts = jnp.concatenate([(ranks >> 7).astype(F32), (ranks & 127).astype(F32)], axis=0).astype(BF16)
+    looked = jnp.dot(parts, pick, preferred_element_type=F32)
+    t_iota = lax.broadcasted_iota(I32, (t_rows, 128), 0)
+    looked = looked[:t_rows] * 128.0 + looked[t_rows:]
+    rank = jnp.sum(jnp.where(t_iota == l_hi, looked, 0.0), axis=0, keepdims=True)
+    rank = jnp.where(m1[0:1] < 6, rank, -1.0).astype(I32)
+    rks[...] = rank
+    rkr[0] = rank
+    rank_copies = []
+    for r in range(1, gn):
+        rank_copies.append(pltpu.make_async_remote_copy(
+            src_ref=rks, dst_ref=rkr.at[g_inv(r)], send_sem=rk_s.at[r], recv_sem=rk_r.at[g_inv(r)],
+            device_id=g_peer(r), device_id_type=MESH))
+        rank_copies[-1].start()
+
+    def swaps(g):
+        lo = 32 * g
+        if g in (0, 2):
+            return tc[TZP, lo + 24:lo + 32, :], slice(lo + 32, lo + 40)
+        return tc[TZM, lo:lo + 8, :], slice(lo - 8, lo)
 
     r_sum = [[None] * 4 for _ in range(9)]
     qx = [[None] * 4 for _ in range(9)]
     qy = [[None] * 4 for _ in range(9)]
+    zero = jnp.zeros((24, 128), F32)
     for g in range(4):
         lo = 32 * g
         rows = slice(lo, lo + 32)
@@ -306,30 +286,41 @@
         sx1 = sx0 + tc[TXB, rows, :]
         sy0 = jnp.where(is_m[7], typ, 0.0) + jnp.where(is_m[0], tym, 0.0)
         sy1 = sy0 + jnp.where(is_m[3], typ, 0.0) + jnp.where(is_m[4], tym, 0.0)
-        zero = jnp.zeros((24, 128), F32)
         lower, upper = tc[TZM, lo:lo + 8, :], tc[TZP, lo + 24:lo + 32, :]
         acc = aa[rows, :]
         if g in (0, 2):
-            swap_t, far = upper, slice(lo + 32, lo + 40)
             az0 = acc + jnp.concatenate([zero, upper], axis=0)
             az1 = az0 + jnp.concatenate([lower, zero], axis=0)
         else:
-            swap_t, far = lower, slice(lo - 8, lo)
             az0 = acc + jnp.concatenate([lower, zero], axis=0)
             az1 = az0 + jnp.concatenate([zero, upper], axis=0)
-        dxy = [[az + sx for sx in (sx0, sx1)] for az in (az0, az1)]
         for s in range(8):
-            a, b, c = s >> 2, (s >> 1) & 1, s & 1
+            ec[s, rows, :] = (az1 if s & 4 else az0) + (sx1 if s & 2 else sx0) + (sy1 if s & 1 else sy0)
+        ec[8, rows, :] = sx0
+        ec[9, rows, :] = sy0
+        here = pp[rows, :]
+        swap_t, far = swaps(g)
+        r_sum[8][g] = plane_sum((az0 + sx0 + sy0) * here - ss[rows, :]) - swap_t * pp[far, :]
+        qx[8][g] = plane_sum(sx0 * here)
+        qy[8][g] = plane_sum(sy0 * here)
+
+    for copy in sent2:
+        copy.wait_recv()
+    place_x(hxr2, 0)
+    outer(v1, v0, hzr2, 0)
+    store = pltpu.make_async_copy(v0, v_out, out_sem.at[0])
+    store.start()
+
+    for g in range(4):
+        lo = 32 * g
+        rows = slice(lo, lo + 32)
+        sx0, sy0 = ec[8, rows, :], ec[9, rows, :]
+        swap_t, far = swaps(g)
+        for s in range(8):
             here = v0[s, rows, :]
-            d = dxy[a][b] + (sy1 if c else sy0)
-            r_sum[s][g] = plane_sum(d * here) - swap_t * v0[s ^ 4, far, :]
+            r_sum[s][g] = plane_sum(ec[s, rows, :] * here) - swap_t * v0[s ^ 4, far, :]
             qx[s][g] = plane_sum(sx0 * here)
             qy[s][g] = plane_sum(sy0 * here)
-        here = pp[rows, :]
-        d = dxy[0][0] + sy0
-        r_sum[8][g] = plane_sum(d * here - ss[rows, :]) - swap_t * pp[far, :]
-        qx[8][g] = plane_sum(sx0 * here)
-        qy[8][g] = plane_sum(sy0 * here)
 
     def x_swap(q):
         return jnp.where(x1 == 3, roll_x(q, 7), jnp.where(x1 == 4, roll_x(q, 1), 0.0))
@@ -383,8 +374,8 @@
             t += roll_y(t, 124)
             u = 2 * j + xi
             rows_out = jnp.where(m24 == u, roll_y(t, u) if u else t, rows_out)
-    cs[...] = rows_out[0:20]
-    crv[0] = rows_out[0:20]
+    cs[...] = rows_out
+    crv[0] = rows_out
 
     g_copies = []
     for r in range(1, gn):
@@ -393,27 +384,45 @@
             device_id=g_peer(r), device_id_type=MESH))
         g_copies[-1].start()
 
-    xs[...] = jnp.zeros_like(xs)
+    n_idx = hn * width
+    idx = lax.broadcasted_iota(I32, (n_idx, 128), 0)
+    peer = jnp.zeros_like(idx)
+    for t in range(1, hn):
+        peer += jnp.where(idx >= t * width, 1, 0)
+    col = idx - peer * width
+    dz, dc = peer // CC, peer % CC
+    pz, pc = mz + dz, mc + dc
+    pz = jnp.where(pz >= zc, pz - zc, pz)
+    pc = jnp.where(pc >= CC, pc - CC, pc)
+    dev = ml * plane + (my * zc + pz) * CC + pc
+    want = dev * own + col
+    wants = [jnp.where(col + q * width < own, want + q * width, -7) for q in range(4)]
+    for copy in rank_copies:
+        copy.wait_recv()
+
+    def build(r, carry):
+        lanes = pl.ds(pl.multiple_of(r * 128, 128), 128)
+        have = rkr[r]
+        for q in range(4):
+            oh[q * n_idx:(q + 1) * n_idx, lanes] = jnp.where(wants[q] == have, 1.0, 0.0).astype(BF16)
+        return carry
+
+    lax.fori_loop(0, gn, build, 0)
+
     xb[64:128, :] = jnp.zeros((64, gn * 128), BF16)
-    row20 = lax.broadcasted_iota(I32, (20, 128), 0)
-    odd20 = lax.broadcasted_iota(I32, (20, 128), 1) % 2 == 1
-    odd9 = lax.broadcasted_iota(I32, (9, 128), 1) % 2 == 1
-    drop = (row20 < 9) & odd20
+    odd = m1 % 2 == 1
     for copy in g_copies:
         copy.wait_recv()
-
-    def spread(r, carry):
-        lanes = pl.ds(pl.multiple_of(r * 128, 128), 128)
-        got = crv[r]
-        xs[0:20, :] = jnp.where(drop, 0.0, got)
-        xs[19:28, :] = jnp.where(odd9, got[0:9], 0.0)
-        vals = xs[...]
+    for r in range(gn):
+        got = [crv[r, 8 * i:8 * i + 8, :] for i in range(3)]
+        turn = [pltpu.roll(jnp.where(odd, got[i], 0.0), 3, 0) for i in range(2)]
+        vals = jnp.concatenate([
+            jnp.where(odd, 0.0, got[0]), jnp.where(odd & (x1 == 0), 0.0, got[1]),
+            jnp.where(x1 < 3, got[2], turn[0]), jnp.where(x1 < 3, turn[0], turn[1])], axis=0)
         high = vals.astype(BF16)
+        lanes = slice(128 * r, 128 * r + 128)
         xb[0:32, lanes] = high
         xb[32:64, lanes] = (vals - high.astype(F32)).astype(BF16)
-        return carry
-
-    lax.fori_loop(0, gn, spread, 0)
     routed = lax.dot_general(
         oh[...], xb[...], (((1,), (1,)), ((), ())), preferred_element_type=F32)
     lane_n = lax.broadcasted_iota(I32, (n_idx, 128), 1)
@@ -431,29 +440,35 @@
             src_ref=hs.at[r], dst_ref=hr.at[h_inv(r)], send_sem=h_s.at[r], recv_sem=h_r.at[h_inv(r)],
             device_id=h_peer(r), device_id_type=MESH))
         h_copies[-1].start()
-    ft[...] = jnp.zeros_like(ft)
     for copy in h_copies:
         copy.wait_recv()
     final = hs[0]
     for r in range(1, hn):
         final += hr[r]
-    ft[0:width, :] = final
+    f_out[0:width, :] = final
+
+    store.wait()
+    for copy in sent + sent2 + rank_copies + g_copies + h_copies:
+        copy.wait_send()
+
+
+def finish(own, width, v_in, f_in, v_out, cm_out, cr_out, ft, sem):
+    store = pltpu.make_async_copy(v_in, v_out, sem)
+    store.start()
+    ft[0:16, :] = f_in[...]
     turned = ft[...].T
-    lane_f = lax.broadcasted_iota(I32, (32, 128), 1)
+    lane = lax.broadcasted_iota(I32, (32, 128), 1)
     done = jnp.zeros((32, 128), F32)
     for q in range(4):
         part = turned[32 * q:32 * q + 32]
-        here = (lane_f >= q * width) & (lane_f < (q + 1) * width)
-        done = jnp.where(here, roll_y(part, q * width) if q else part, done)
+        here = (lane >= q * width) & (lane < (q + 1) * width)
+        done = jnp.where(here, pltpu.roll(part, q * width, 1) if q else part, done)
     for pz in range(3):
         for px, base in ((0, 19), (1, 9), (2, 0)):
             k = 9 * pz + 3 * px
             cm_out[k:k + 3, :] = done[base + 3 * pz:base + 3 * pz + 3, 0:own]
     cr_out[...] = done[18:19, 0:own]
-
     store.wait()
-    for copy in sent + sent2 + rank_copies + g_copies + h_copies:
-        copy.wait_send()
 
 
 def per_device(sizes, basis_init, permeability, accumulation, pressure, source, support, block_of, curve_rank):
@@ -465,46 +480,54 @@
     width = (own + 3) // 4
     flat = lambda v: v.reshape(v.shape[:-3] + (128, 128))
     t_rows = -(-curve_rank.shape[0] // 2048) * 16
-    table = jnp.pad(curve_rank, (0, t_rows * 128 - curve_rank.shape[0])).reshape(t_rows, 128)
-    labels = jnp.stack([block_of[0], block_of[4], block_of[12]])
     anywhere = pl.BlockSpec(memory_space=pl.ANY)
     vmem = pl.BlockSpec(memory_space=pltpu.VMEM)
     dma = pltpu.SemaphoreType.DMA
     cells = lambda *lead: pltpu.VMEM(lead + (128, 128), F32)
-    basis, matrix, residual = pl.pallas_call(
+    basis, rows = pl.pallas_call(
         functools.partial(kernel, (lx, plane, zc, own, width)),
         out_shape=(
             jax.ShapeDtypeStruct((8, 128, 128), F32),
-            jax.ShapeDtypeStruct((27, own), F32),
-            jax.ShapeDtypeStruct((1, own), F32),
+            jax.ShapeDtypeStruct((16, 128), F32),
         ),
         in_specs=[anywhere] * 8,
-        out_specs=(anywhere, vmem, vmem),
+        out_specs=(anywhere, vmem),
         scratch_shapes=[
             cells(8), pltpu.VMEM((8, 128, 128), I32), cells(), cells(), cells(), cells(),
-            pltpu.VMEM((3, 8, 128), I32), pltpu.VMEM((t_rows, 128), I32),
-            cells(8), cells(8), cells(8), cells(8), cells(10), cells(4),
+            pltpu.VMEM((3, 8, 128), I32), pltpu.VMEM(curve_rank.shape, I32), pltpu.VMEM((t_rows, 128), I32),
+            cells(8), cells(8), cells(8), cells(8), cells(10), cells(10), cells(4),
             pltpu.VMEM((2, 5, 16, 128), F32), pltpu.VMEM((2, 5, 16, 128), F32),
             pltpu.VMEM((2, 5, 8, 128), F32), pltpu.VMEM((2, 5, 8, 128), F32),
             pltpu.VMEM((2, 4, 16, 128), F32), pltpu.VMEM((2, 4, 16, 128), F32),
             pltpu.VMEM((2, 4, 8, 128), F32), pltpu.VMEM((2, 4, 8, 128), F32),
             pltpu.VMEM((1, 128), I32), pltpu.VMEM((gn, 1, 128), I32),
             pltpu.VMEM((4 * hn * width, gn * 128), BF16),
-            pltpu.VMEM((32, 128), F32), pltpu.VMEM((128, gn * 128), BF16),
+            pltpu.VMEM((128, gn * 128), BF16),
             pltpu.VMEM((3, 192, 128), F32),
-            pltpu.VMEM((20, 128), F32), pltpu.VMEM((gn, 20, 128), F32),
+            pltpu.VMEM((24, 128), F32), pltpu.VMEM((gn, 24, 128), F32),
             pltpu.VMEM((hn, width, 128), F32), pltpu.VMEM((hn, width, 128), F32),
-            pltpu.VMEM((128, 128), F32),
-            dma((8,)), dma((1,)), dma((8,)), dma((8,)),
+            dma((10,)), dma((1,)), dma((8,)), dma((8,)),
             dma((gn,)), dma((gn,)), dma((gn,)), dma((gn,)), dma((hn,)), dma((hn,)),
         ],
         compiler_params=pltpu.CompilerParams(
-            collective_id=0, has_side_effects=True, vmem_limit_bytes=40 * 1024 * 1024),
+            collective_id=0, has_side_effects=True, vmem_limit_bytes=VMEM_GRANT),
         cost_estimate=pl.CostEstimate(flops=20_000_000, bytes_accessed=2_000_000, transcendentals=0),
     )(
         flat(basis_init), flat(permeability), flat(accumulation), flat(pressure), flat(source),
-        flat(support), labels, table,
+        flat(support), flat(block_of), curve_rank,
     )
+    basis, matrix, residual = pl.pallas_call(
+        functools.partial(finish, own, width),
+        out_shape=(
+            jax.ShapeDtypeStruct((8, 128, 128), F32),
+            jax.ShapeDtypeStruct((27, own), F32),
+            jax.ShapeDtypeStruct((1, own), F32),
+        ),
+        in_specs=[anywhere, vmem],
+        out_specs=(anywhere, vmem, vmem),
+        scratch_shapes=[pltpu.VMEM((128, 128), F32), dma],
+        compiler_params=pltpu.CompilerParams(vmem_limit_bytes=VMEM_GRANT),
+    )(basis, rows)
     return basis.reshape(basis_init.shape), matrix, residual.reshape(own)
 
 

time: 39.8 us -> 50.5 us (1.27)
  Pallas kernels: 31.5 us -> 49.7 us
  local copies, waits for them, and re-layouts: 7.21 us -> 0 us
    pallas_call x0 -> x1, Pallas kernels: none -> 18.3 us  [per_device(): pl.pallas_call(functools.partial(finish, own, width), out_shape=(jax.Shap...]
    unnamed x15 -> x0, local copies, waits for them, and re-layouts: 5.68 us -> none
    reshape x1 -> x0, local copies, waits for them, and re-layouts: 0.78 us -> none  [per_device(): jnp.pad(curve_rank, (0, t_rows * 128 - curve_rank.shape[0]))]
    slice x1 -> x0, local copies, waits for them, and re-layouts: 0.76 us -> none  [per_device(): labels = jnp.stack([block_of[0], block_of[4], block_of[12]])]
where the time goes in v2:
time: 50.5 us; the launch traced here: 50.3 us
  Pallas kernels  49.7 us (98%)
  between operations  0.64 us (1%)
    pallas_call x1, Pallas kernels, per_device(): pl.pallas_call(functools.partial(kernel, (lx, plane, zc, own, width)), ou...  31.4 us
    pallas_call x1, Pallas kernels, per_device(): pl.pallas_call(functools.partial(finish, own, width), out_shape=(jax.Shap...  18.3 us

profile of v2, /device:TPU:1, one launch (start us, length us, event | category | flops | bytes accessed | tf_op | source)
XLA Modules:
  0.0 50.3 jit_solution(9637892108693145429)
XLA Ops:
  0.6 31.4 %shard_map.103 = (f32[8,128,128]{2,1,0:T(8,128)}, f32[16,128]{1,0:T(8,128)}) custom-call(f32[8,128,128]{2,1,0:T(8,128)} %bitcast.9, f32[128,128]{1,0:T(8,128)} %bitcast.11, f32[128,128]{1,0:T(8,128)} %bitcast.12, f32[128,128]{1,0:T(8,128)} %bitcast.13, f32[128,128]{1,0:T(8,128)} %bitcast.14, s32[8,128,128]{2,1,0:T(8,128)} %bitcast.10, s32[128,128]{1,0:T(8,128)} %bitcast.15, ...), custom_call_target="tpu_custom_call" | custom-call | flops 20000000 | bytes 2000000 | tf_op jit(solution)/shard_map/pallas_call | solution.py:487
  32.0 18.3 %shard_map.104 = (f32[8,128,128]{2,1,0:T(8,128)}, f32[27,37]{1,0:T(8,128)}, f32[1,37]{1,0:T(1,128)}) custom-call(f32[8,128,128]{2,1,0:T(8,128)} %get-tuple-element.8.v_in, f32[16,128]{1,0:T(8,128)} %get-tuple-element.9.f_in), custom_call_target="tpu_custom_call" | custom-call | tf_op jit(solution)/shard_map/pallas_call | solution.py:519

commit v3 on v2

v3 whole, which is shorter than its diff:
```python
import functools

import jax
import jax.numpy as jnp
from jax import lax
from jax.experimental import pallas as pl
from jax.experimental.pallas import tpu as pltpu
from jax.sharding import PartitionSpec as P

MESH = pl.DeviceIdType.MESH
F32, BF16, I32 = jnp.float32, jnp.bfloat16, jnp.int32

YC, CC = 4, 2
VMEM_GRANT = 60 * 1024 * 1024
THIRD, TWO_THIRDS = 1.0 / 3.0, 2.0 / 3.0
B0 = (0, 1, 4, 5)
A0 = (0, 1, 2, 3)


def roll_x(v, shift):
    rows = v.shape[0]
    return pltpu.roll(v.reshape(rows // 8, 8, 128), shift, 1).reshape(rows, 128)


def roll_y(v, shift):
    return pltpu.roll(v, shift, 1)


def harmonic(k, n):
    return 2.0 * k * n / (k + n)


def plane_sum(v):
    return v.reshape(-1, 8, 128).sum(axis=0)


TYM, TYP, TYM1, TYP1, TXM, TXP, TZM, TZP, TZM1, TZP1, TXB, RD = range(12)


def kernel(
    dims,
    bi_hbm, k_hbm, a_hbm, p_hbm, s_hbm, sup_hbm, blk_hbm, cr_hbm,
    v_out, f_out,
    bi, sup, aa, pp, ss, blk, cr1, tab,
    va, vb, sf, nn, tc, tzb, ec, sw, fl, hx, hxs, hxr, hzr, hxs2, hxr2, hzr2,
    rks, rkr, wt, oh, xb, es, cs, crv, acc, hs, hr,
    in_sem, out_sem, halo_s, halo_r, rk_s, rk_r, g_s, g_r, h_s, h_r,
):
    lx, plane, zc, own, width = dims
    gn, hn = lx * YC, zc * CC
    n_idx = hn * width
    ml, mp = lax.axis_index("layer"), lax.axis_index("plane")
    my, mz, mc = mp // (zc * CC), (mp // CC) % zc, mp % CC

    def g_peer(r):
        dx, dy = r // YC, r % YC
        return ((ml + dx) % lx, (((my + dy) % YC) * zc + mz) * CC + mc)

    def g_inv(r):
        return ((lx - r // YC) % lx) * YC + (YC - r % YC) % YC

    def h_peer(r):
        dz, dc = r // CC, r % CC
        return (ml, (my * zc + (mz + dz) % zc) * CC + (mc + dc) % CC)

    def h_inv(r):
        return ((zc - r // CC) % zc) * CC + (CC - r % CC) % CC

    up_x, down_x = (ml, (mp + 1) % plane), (ml, (mp + plane - 1) % plane)
    up_z, down_z = ((ml + 1) % lx, mp), ((ml + lx - 1) % lx, mp)

    def loop(n, body, start=0):
        def step(i, carry):
            body(i)
            return carry

        lax.fori_loop(start, n, step, 0)

    def group(g):
        return pl.ds(pl.multiple_of(g * 32, 32), 32)

    def one_plane(z):
        return pl.ds(pl.multiple_of(z * 8, 8), 8)

    loads = [
        pltpu.make_async_copy(k_hbm, va.at[0], in_sem.at[0]),
        pltpu.make_async_copy(bi_hbm, bi, in_sem.at[1]),
        pltpu.make_async_copy(sup_hbm, sup, in_sem.at[2]),
        pltpu.make_async_copy(a_hbm, aa, in_sem.at[3]),
        pltpu.make_async_copy(cr_hbm, cr1, in_sem.at[4]),
        pltpu.make_async_copy(p_hbm, pp, in_sem.at[5]),
        pltpu.make_async_copy(s_hbm, ss, in_sem.at[6]),
    ]
    for j, z in enumerate((0, 4, 12)):
        loads.append(pltpu.make_async_copy(blk_hbm.at[pl.ds(8 * z, 8)], blk.at[j], in_sem.at[7 + j]))
    for load in loads:
        load.start()

    barrier = pltpu.get_barrier_semaphore()

    def greet(who):
        pl.semaphore_signal(barrier, inc=1, device_id=who, device_id_type=MESH)

    greet(up_x)
    greet(down_x)
    loop(gn, lambda r: greet(g_peer(r)), 1)
    loop(hn, lambda r: greet(h_peer(r)), 1)

    lane = lax.broadcasted_iota(I32, (32, 128), 1)
    m, x = lane % 8, lax.broadcasted_iota(I32, (32, 128), 0) % 8
    m1, x1 = m[:8], x[:8]
    lane1, row1 = lane[:8], x[:8]
    is_m = {i: m == i for i in (0, 3, 4, 7)}
    is_x = {i: x == i for i in (3, 4)}

    hx[...] = jnp.zeros_like(hx)
    es[...] = jnp.zeros_like(es)
    tc[TXB] = jnp.zeros((128, 128), F32)

    def blank(i):
        xb[i, 64:128, :] = jnp.zeros((64, 256), BF16)

    loop(gn // 2, blank)

    def wanted(i):
        idx = row1 + i * 8
        peer = jnp.zeros_like(idx)
        for t in range(1, hn):
            peer += jnp.where(idx >= t * width, 1, 0)
        col = idx - peer * width
        pz, pc = mz + (peer >> (CC - 1)), mc + (peer & (CC - 1))
        pz = jnp.where(pz >= zc, pz - zc, pz)
        pc = jnp.where(pc >= CC, pc - CC, pc)
        want = (ml * plane + (my * zc + pz) * CC + pc) * own + col
        for q in range(4):
            wt[one_plane(i + q * (n_idx // 8)), :] = jnp.where(col + q * width < own, want + q * width, -7)

    loop(n_idx // 8, wanted)

    loads[0].wait()

    def faces(g):
        rows, below = group(g), one_plane((4 * g + 15) % 16)
        k = va[0, rows, :]
        tym = jnp.where(lane == 0, 0.0, harmonic(k, roll_y(k, 1)))
        typ = roll_y(tym, 127)
        tc[TYM, rows, :] = tym
        tc[TYP, rows, :] = typ
        tc[TYM1, rows, :] = jnp.where(is_m[4], 0.0, tym)
        tc[TYP1, rows, :] = jnp.where(is_m[3], 0.0, typ)
        txm = jnp.where(x == 0, 0.0, harmonic(k, roll_x(k, 1)))
        tc[TXM, rows, :] = txm
        tc[TXP, rows, :] = roll_x(txm, 7)
        tz = harmonic(k, jnp.concatenate([va[0, below, :], k[0:24]], axis=0))
        tc[TZM, rows, :] = tz
        tc[TZP, below, :] = tz[0:8]
        tc[TZP, pl.ds(pl.multiple_of(g * 32, 32), 24), :] = tz[8:32]
        tc[TZM1, rows, :] = tz
        tc[TZP1, below, :] = tz[0:8]
        tc[TZP1, pl.ds(pl.multiple_of(g * 32, 32), 24), :] = tz[8:32]

    loop(4, faces)
    nil = jnp.zeros((8, 128), F32)
    tc[TZM, 0:8, :] = nil
    tc[TZP, 120:128, :] = nil
    tc[TZM1, 0:8, :] = nil
    tc[TZP1, 120:128, :] = nil
    tc[TZM1, 64:72, :] = nil
    tc[TZP1, 56:64, :] = nil
    for i, (t, z) in enumerate(((TZP, 3), (TZM, 4), (TZP, 11), (TZM, 12))):
        sw[i] = tc[t, 8 * z:8 * z + 8, :]

    loads[1].wait()
    loads[2].wait()

    def first(g):
        rows = group(g)
        vals = []
        for s in range(8):
            on = sup[s, rows, :].astype(F32)
            sf[s, rows, :] = on
            vals.append(bi[s, rows, :] * on)
        inv = 1.0 / sum(vals[1:], vals[0])
        for s in range(8):
            va[1 + s, rows, :] = vals[s] * inv

    loop(4, first)

    def exchange(v, off, xs_buf, xr_buf, zr_buf, base):
        for i, s in enumerate(B0):
            xs_buf[0, off + i] = v[off + s, pl.ds(0, 16, stride=8), :]
            xs_buf[1, off + i] = v[off + s, pl.ds(7, 16, stride=8), :]
        if off:
            xs_buf[0, 0] = v[0, pl.ds(0, 16, stride=8), :]
            xs_buf[1, 0] = v[0, pl.ds(7, 16, stride=8), :]
            pl.semaphore_wait(barrier, gn + hn)
        last, lead = v.at[pl.ds(0, off + 4), pl.ds(120, 8)], v.at[pl.ds(0, off + 4), pl.ds(0, 8)]
        copies = []
        for j, (src, dst, who) in enumerate((
            (xs_buf.at[1], xr_buf.at[0], up_x), (xs_buf.at[0], xr_buf.at[1], down_x),
            (last, zr_buf.at[0], up_z), (lead, zr_buf.at[1], down_z),
        )):
            copies.append(pltpu.make_async_remote_copy(
                src_ref=src, dst_ref=dst, send_sem=halo_s.at[base + j], recv_sem=halo_r.at[base + j],
                device_id=who, device_id_type=MESH))
        for copy in copies:
            copy.start()
        return copies

    def inner(v, off):
        def part(g):
            rows = group(g)
            odd = g % 2
            below, above = one_plane((4 * g + 15) % 16), one_plane((4 * g + 4) % 16)
            coef = [tc[i, rows, :] for i in range(10)]
            vals = [v[off + s, rows, :] for s in range(8)]
            for s in range(8):
                here, turn = vals[s], 4 - (s & 4) * 2
                tm, tp = (coef[TYM1], coef[TYP1]) if s & 1 else (coef[TYM], coef[TYP])
                zm, zp = (coef[TZM1], coef[TZP1]) if s & 4 else (coef[TZM], coef[TZP])
                near = tm * roll_y(jnp.where(is_m[7], vals[s ^ 1], here), 1)
                near += tp * roll_y(jnp.where(is_m[0], vals[s ^ 1], here), 127)
                near += coef[TXM] * roll_x(jnp.where(is_x[3], vals[s ^ 2], here), 1)
                near += coef[TXP] * roll_x(jnp.where(is_x[4], vals[s ^ 2], here), 7)
                lo, hi = v[off + s + turn * odd, below, :], v[off + s + turn * (1 - odd), above, :]
                near += zm * jnp.concatenate([lo, here[0:24]], axis=0)
                near += zp * jnp.concatenate([here[8:32], hi], axis=0)
                nn[s, rows, :] = near

        loop(4, part)

    def outer(v, off, new, off2, xr_buf, zr_buf, extra):
        for i in range(4):
            hx[i, pl.ds(0, 16, stride=8), :] = xr_buf[0, extra + i]
            hx[i, pl.ds(7, 16, stride=8), :] = xr_buf[1, extra + i]
            nn[i, 0:8, :] += tzb[0] * zr_buf[0, extra + i]
            nn[i, 120:128, :] += tzb[1] * zr_buf[1, extra + i]

        def part(g):
            rows = group(g)
            rd, txb = tc[RD, rows, :], tc[TXB, rows, :]
            vals = []
            for s in range(8):
                near = nn[s, rows, :]
                if s in B0:
                    near += txb * hx[B0.index(s), rows, :]
                vals.append((v[off + s, rows, :] * THIRD + rd * near) * sf[s, rows, :])
            inv = 1.0 / sum(vals[1:], vals[0])
            for s in range(8):
                new[off2 + s, rows, :] = vals[s] * inv

        loop(4, part)

    sent = exchange(va, 1, hxs, hxr, hzr, 0)
    inner(va, 1)
    loads[3].wait()
    for copy in sent:
        copy.wait_recv()

    tc[TXB, pl.ds(0, 16, stride=8), :] = jnp.where(mp > 0, harmonic(hxs[0, 0], hxr[0, 0]), 0.0)
    tc[TXB, pl.ds(7, 16, stride=8), :] = jnp.where(mp < plane - 1, harmonic(hxs[1, 0], hxr[1, 0]), 0.0)
    tzb[0] = jnp.where(ml > 0, harmonic(va[0, 0:8, :], hzr[0, 0]), 0.0)
    tzb[1] = jnp.where(ml < lx - 1, harmonic(va[0, 120:128, :], hzr[1, 0]), 0.0)

    def scale(g):
        rows = group(g)
        diag = aa[rows, :]
        for t in (TYM, TYP, TXM, TXP, TXB, TZM, TZP):
            diag += tc[t, rows, :]
        tc[RD, rows, :] = diag

    loop(4, scale)
    tc[RD, 0:8, :] += tzb[0]
    tc[RD, 120:128, :] += tzb[1]
    tc[RD] = TWO_THIRDS / tc[RD]

    outer(va, 1, vb, 0, hxr, hzr, 1)
    sent2 = exchange(vb, 0, hxs2, hxr2, hzr2, 4)

    for load in loads[4:]:
        load.wait()
    label = blk[0, 0:1, :]
    for u, (j, r) in enumerate(((0, 0), (0, 4), (1, 0), (1, 4), (2, 0), (2, 4))):
        label = jnp.where(m1[0:1] == u, blk[j, r:r + 1, :], label)
    t_rows, labels = tab.shape[0], cr1.shape[0]
    tab[labels // 128:, :] = jnp.zeros((t_rows - labels // 128, 128), I32)

    def table(t):
        tab[pl.ds(t, 1), :] = cr1[pl.ds(pl.multiple_of(t * 128, 128), 128)].reshape(1, 128)

    loop(labels // 128, table)
    if labels % 128:
        t = labels // 128
        tab[t:t + 1, 0:labels % 128] = cr1[pl.ds(t * 128, labels % 128)].reshape(1, labels % 128)
    l_hi, l_lo = label >> 7, label & 127
    w_iota = lax.broadcasted_iota(I32, (128, 128), 0)
    pick = jnp.where(w_iota == l_lo, 1.0, 0.0).astype(BF16)
    ranks = tab[...]
    parts = jnp.concatenate([(ranks >> 7).astype(F32), (ranks & 127).astype(F32)], axis=0).astype(BF16)
    looked = jnp.dot(parts, pick, preferred_element_type=F32)
    t_iota = lax.broadcasted_iota(I32, (t_rows, 128), 0)
    looked = looked[:t_rows] * 128.0 + looked[t_rows:]
    rank = jnp.sum(jnp.where(t_iota == l_hi, looked, 0.0), axis=0, keepdims=True)
    rank = jnp.where(m1[0:1] < 6, rank, -1.0).astype(I32)
    rks[...] = rank
    rkr[0] = rank

    def rank_copy(r):
        return pltpu.make_async_remote_copy(
            src_ref=rks, dst_ref=rkr.at[g_inv(r)], send_sem=rk_s.at[r], recv_sem=rk_r.at[g_inv(r)],
            device_id=g_peer(r), device_id_type=MESH)

    loop(gn, lambda r: rank_copy(r).start(), 1)

    inner(vb, 0)

    def weigh(g):
        rows = group(g)
        tym, typ, txm, txp = (tc[i, rows, :] for i in (TYM, TYP, TXM, TXP))
        sx0 = jnp.where(is_x[3], txp, 0.0) + jnp.where(is_x[4], txm, 0.0)
        sx1 = sx0 + tc[TXB, rows, :]
        sy0 = jnp.where(is_m[7], typ, 0.0) + jnp.where(is_m[0], tym, 0.0)
        sy1 = sy0 + jnp.where(is_m[3], typ, 0.0) + jnp.where(is_m[4], tym, 0.0)
        for s in range(4):
            d = aa[rows, :] + (sx1 if s & 2 else sx0) + (sy1 if s & 1 else sy0)
            ec[s, rows, :] = d
            ec[4 + s, rows, :] = d
        ec[8, rows, :] = sx0
        ec[9, rows, :] = sy0

    loop(4, weigh)
    for i, z in enumerate((3, 4, 11, 12)):
        for s in range(8):
            ec[s, 8 * z:8 * z + 8, :] += sw[i]
    for t, z in ((tzb[0], 0), (tc[TZP, 56:64, :], 7), (tc[TZM, 64:72, :], 8), (tzb[1], 15)):
        for s in range(4, 8):
            ec[s, 8 * z:8 * z + 8, :] += t

    def x_swap(q):
        return jnp.where(x1 == 3, roll_x(q, 7), jnp.where(x1 == 4, roll_x(q, 1), 0.0))

    def y_swap(q):
        return jnp.where(m1 == 7, roll_y(q, 127), jnp.where(m1 == 0, roll_y(q, 1), 0.0))

    def far(g):
        return one_plane(4 * g + 4 - 5 * (g % 2))

    def rest(g):
        rows = group(g)
        here = pp[rows, :]
        full = plane_sum(ec[0, rows, :] * here - ss[rows, :]) - sw[g] * pp[far(g), :]
        fl[8, one_plane(g), :] = (
            full - x_swap(plane_sum(ec[8, rows, :] * here)) - y_swap(plane_sum(ec[9, rows, :] * here)))

    loop(4, rest)

    for copy in sent2:
        copy.wait_recv()
    for copy in sent:
        copy.wait_send()
    outer(vb, 0, va, 1, hxr2, hzr2, 0)
    store = pltpu.make_async_copy(va.at[pl.ds(1, 8)], v_out, out_sem.at[0])
    store.start()

    def gather(g):
        rows = group(g)
        sx0, sy0 = ec[8, rows, :], ec[9, rows, :]
        vals = [va[1 + s, rows, :] for s in range(8)]
        qx = [x_swap(plane_sum(sx0 * v)) for v in vals]
        qy = [y_swap(plane_sum(sy0 * v)) for v in vals]
        for s in range(8):
            full = plane_sum(ec[s, rows, :] * vals[s]) - sw[g] * va[1 + (s ^ 4), far(g), :]
            fl[s, one_plane(g), :] = full - qx[s ^ 2] - qy[s ^ 1]

    loop(4, gather)

    for j in range(3):
        for pz in range(3):
            if pz == 1:
                groups, a = ((0,), (1, 2), (3,))[j], 0
            elif pz == 0:
                groups, a = ((), (1,), (3,))[j], 1
            else:
                groups, a = ((0,), (2,), ())[j], 1
            if not groups:
                continue
            for b in (1, 0):
                at = 8 * ((1 - b) * 9 + 3 * pz)
                for c in (0, 1):
                    s = 4 * a + 2 * b + c
                    term = fl[s, 8 * groups[0]:8 * groups[0] + 8, :]
                    for g in groups[1:]:
                        term += fl[s, 8 * g:8 * g + 8, :]
                    if c:
                        es[j, at:at + 8, :] = jnp.where(m1 < 4, term, 0.0)
                        es[j, at + 16:at + 24, :] = jnp.where(m1 < 4, 0.0, term)
                    else:
                        es[j, at + 8:at + 16, :] = term
        groups = ((0,), (1, 2), (3,))[j]
        term = fl[8, 8 * groups[0]:8 * groups[0] + 8, :]
        for g in groups[1:]:
            term += fl[8, 8 * g:8 * g + 8, :]
        es[j, 144:152, :] = -term

    m24 = m[:24]
    rows_out = jnp.zeros((24, 128), F32)
    for j in range(3):
        for xi in range(2):
            t = es[j, pl.ds(4 * xi, 24, stride=8), :]
            for i in range(1, 4):
                t += es[j, pl.ds(4 * xi + i, 24, stride=8), :]
            t += roll_y(t, 127)
            t += roll_y(t, 126)
            t += roll_y(t, 124)
            u = 2 * j + xi
            rows_out = jnp.where(m24 == u, roll_y(t, u) if u else t, rows_out)
    cs[...] = rows_out
    crv[0] = rows_out

    def g_copy(r):
        return pltpu.make_async_remote_copy(
            src_ref=cs, dst_ref=crv.at[g_inv(r)], send_sem=g_s.at[r], recv_sem=g_r.at[g_inv(r)],
            device_id=g_peer(r), device_id_type=MESH)

    loop(gn, lambda r: g_copy(r).start(), 1)

    loop(gn, lambda r: rank_copy(r).wait_recv(), 1)

    def build(i):
        at = pl.multiple_of(i * 16, 16)
        want = wt[pl.ds(at, 16), :]
        for r in range(gn):
            oh[r // 2, pl.ds(at, 16), 128 * (r % 2):128 * (r % 2) + 128] = (
                jnp.where(want == rkr[r], 1.0, 0.0).astype(BF16))

    loop(4 * n_idx // 16, build)

    odd = m1 % 2 == 1
    loop(gn, lambda r: g_copy(r).wait_recv(), 1)

    def spread(i):
        for h in range(2):
            got = [crv[2 * i + h, 8 * k:8 * k + 8, :] for k in range(3)]
            turn = [pltpu.roll(jnp.where(odd, got[k], 0.0), 3, 0) for k in range(2)]
            vals = jnp.concatenate([
                jnp.where(odd, 0.0, got[0]), jnp.where(odd & (x1 == 0), 0.0, got[1]),
                jnp.where(x1 < 3, got[2], turn[0]), jnp.where(x1 < 3, turn[0], turn[1])], axis=0)
            high = vals.astype(BF16)
            lanes = slice(128 * h, 128 * h + 128)
            xb[i, 0:32, lanes] = high
            xb[i, 32:64, lanes] = (vals - high.astype(F32)).astype(BF16)

    loop(gn // 2, spread)

    def product(i):
        return lax.dot_general(oh[i], xb[i], (((1,), (1,)), ((), ())), preferred_element_type=F32)

    acc[...] = product(0) + product(1)

    def add_product(i):
        acc[...] += product(2 * i) + product(2 * i + 1)

    loop(gn // 4, add_product, 1)

    low_lanes = lax.broadcasted_iota(I32, (n_idx, 128), 1) < 32
    packed = jnp.zeros((n_idx, 128), F32)
    for q in range(4):
        part = acc[q * n_idx:(q + 1) * n_idx, :]
        both = jnp.where(low_lanes, part + roll_y(part, 96), 0.0)
        packed += roll_y(both, 32 * q) if q else both
    for r in range(hn):
        hs[r] = packed[r * width:(r + 1) * width]

    def h_copy(r):
        return pltpu.make_async_remote_copy(
            src_ref=hs.at[r], dst_ref=hr.at[h_inv(r)], send_sem=h_s.at[r], recv_sem=h_r.at[h_inv(r)],
            device_id=h_peer(r), device_id_type=MESH)

    loop(hn, lambda r: h_copy(r).start(), 1)
    loop(hn, lambda r: h_copy(r).wait_recv(), 1)
    final = hs[0]
    for r in range(1, hn):
        final += hr[r]
    f_out[0:width, :] = final

    store.wait()
    for copy in sent2:
        copy.wait_send()

    def drain(r):
        rank_copy(r).wait_send()
        g_copy(r).wait_send()

    loop(gn, drain, 1)
    loop(hn, lambda r: h_copy(r).wait_send(), 1)


def finish(own, width, v_in, f_in, v_out, cm_out, cr_out, vv, ft, sem):
    fetch = [pltpu.make_async_copy(v_in.at[s], vv.at[s], sem.at[0, s]) for s in range(8)]
    store = [pltpu.make_async_copy(vv.at[s], v_out.at[s], sem.at[1, s]) for s in range(8)]
    for copy in fetch:
        copy.start()
    for s in range(8):
        fetch[s].wait()
        store[s].start()
    ft[0:16, :] = f_in[...]
    turned = ft[...].T
    lane = lax.broadcasted_iota(I32, (32, 128), 1)
    done = jnp.zeros((32, 128), F32)
    for q in range(4):
        part = turned[32 * q:32 * q + 32]
        here = (lane >= q * width) & (lane < (q + 1) * width)
        done = jnp.where(here, pltpu.roll(part, q * width, 1) if q else part, done)
    for pz in range(3):
        for px, base in ((0, 19), (1, 9), (2, 0)):
            k = 9 * pz + 3 * px
            cm_out[k:k + 3, :] = done[base + 3 * pz:base + 3 * pz + 3, 0:own]
    cr_out[...] = done[18:19, 0:own]
    for copy in store:
        copy.wait()


def per_device(sizes, basis_init, permeability, accumulation, pressure, source, support, block_of, curve_rank):
    lx, plane = sizes
    zc = plane // (YC * CC)
    gn, hn = lx * YC, zc * CC
    devices = lx * plane
    own = (curve_rank.shape[0] + devices - 1) // devices
    width = (own + 3) // 4
    flat = lambda v: v.reshape(v.shape[:-3] + (128, 128))
    t_rows = -(-curve_rank.shape[0] // 2048) * 16
    anywhere = pl.BlockSpec(memory_space=pl.ANY)
    vmem = pl.BlockSpec(memory_space=pltpu.VMEM)
    dma = pltpu.SemaphoreType.DMA
    cells = lambda *lead: pltpu.VMEM(lead + (128, 128), F32)
    basis, rows = pl.pallas_call(
        functools.partial(kernel, (lx, plane, zc, own, width)),
        out_shape=(
            jax.ShapeDtypeStruct((8, 128, 128), F32),
            jax.ShapeDtypeStruct((16, 128), F32),
        ),
        in_specs=[anywhere] * 8,
        out_specs=(anywhere, vmem),
        scratch_shapes=[
            cells(8), pltpu.VMEM((8, 128, 128), I32), cells(), cells(), cells(),
            pltpu.VMEM((3, 8, 128), I32), pltpu.VMEM(curve_rank.shape, I32), pltpu.VMEM((t_rows, 128), I32),
            cells(9), cells(8), cells(8), cells(8), cells(12),
            pltpu.VMEM((2, 8, 128), F32), cells(10), pltpu.VMEM((4, 8, 128), F32),
            pltpu.VMEM((9, 32, 128), F32), cells(4),
            pltpu.VMEM((2, 5, 16, 128), F32), pltpu.VMEM((2, 5, 16, 128), F32), pltpu.VMEM((2, 5, 8, 128), F32),
            pltpu.VMEM((2, 4, 16, 128), F32), pltpu.VMEM((2, 4, 16, 128), F32), pltpu.VMEM((2, 4, 8, 128), F32),
            pltpu.VMEM((1, 128), I32), pltpu.VMEM((gn, 1, 128), I32),
            pltpu.VMEM((4 * hn * width, 128), I32), pltpu.VMEM((gn // 2, 4 * hn * width, 256), BF16),
            pltpu.VMEM((gn // 2, 128, 256), BF16), pltpu.VMEM((3, 192, 128), F32),
            pltpu.VMEM((24, 128), F32), pltpu.VMEM((gn, 24, 128), F32),
            pltpu.VMEM((4 * hn * width, 128), F32),
            pltpu.VMEM((hn, width, 128), F32), pltpu.VMEM((hn, width, 128), F32),
            dma((10,)), dma((1,)), dma((8,)), dma((8,)),
            dma((gn,)), dma((gn,)), dma((gn,)), dma((gn,)), dma((hn,)), dma((hn,)),
        ],
        compiler_params=pltpu.CompilerParams(
            collective_id=0, has_side_effects=True, vmem_limit_bytes=VMEM_GRANT),
        cost_estimate=pl.CostEstimate(flops=20_000_000, bytes_accessed=2_000_000, transcendentals=0),
    )(
        flat(basis_init), flat(permeability), flat(accumulation), flat(pressure), flat(source),
        flat(support), flat(block_of), curve_rank,
    )
    basis, matrix, residual = pl.pallas_call(
        functools.partial(finish, own, width),
        out_shape=(
            jax.ShapeDtypeStruct((8, 128, 128), F32),
            jax.ShapeDtypeStruct((27, own), F32),
            jax.ShapeDtypeStruct((1, own), F32),
        ),
        in_specs=[anywhere, vmem],
        out_specs=(anywhere, vmem, vmem),
        scratch_shapes=[cells(8), cells(), dma((2, 8))],
        compiler_params=pltpu.CompilerParams(vmem_limit_bytes=VMEM_GRANT),
    )(basis, rows)
    return basis.reshape(basis_init.shape), matrix, residual.reshape(own)


def solution(mesh):
    return jax.shard_map(
        functools.partial(per_device, (mesh.shape["layer"], mesh.shape["plane"])),
        mesh=mesh,
        in_specs=(
            P(None, "layer", "plane", None),
            P("layer", "plane", None),
            P("layer", "plane", None),
            P("layer", "plane", None),
            P("layer", "plane", None),
            P(None, "layer", "plane", None),
            P("layer", "plane", None),
            P(),
        ),
        out_specs=(
            P(None, "layer", "plane", None),
            P(None, ("layer", "plane")),
            P(("layer", "plane")),
        ),
        check_vma=False,
    )
```

time: 50.5 us -> 37.1 us (0.73)
  Pallas kernels: 49.7 us -> 36.2 us
    pallas_call x1, Pallas kernels: 18.3 us -> 3.13 us  [per_device(): pl.pallas_call(functools.partial(finish, own, width), out_shape=(jax.Shap...]
    pallas_call x1, Pallas kernels: 31.4 us -> 33.1 us  [per_device(): pl.pallas_call(functools.partial(kernel, (lx, plane, zc, own, width)), ou...]
where the time goes in v3:
time: 37.1 us; the launch traced here: 36.9 us
  Pallas kernels  36.2 us (98%)
  between operations  0.64 us (2%)
    pallas_call x1, Pallas kernels, per_device(): pl.pallas_call(functools.partial(kernel, (lx, plane, zc, own, width)), ou...  33.1 us
    pallas_call x1, Pallas kernels, per_device(): pl.pallas_call(functools.partial(finish, own, width), out_shape=(jax.Shap...  3.13 us

profile of v3, /device:TPU:1, one launch (start us, length us, event | category | flops | bytes accessed | tf_op | source)
XLA Modules:
  0.0 36.9 jit_solution(10825795294821449919)
XLA Ops:
  0.6 33.1 %shard_map.103 = (f32[8,128,128]{2,1,0:T(8,128)}, f32[16,128]{1,0:T(8,128)}) custom-call(f32[8,128,128]{2,1,0:T(8,128)} %bitcast.9, f32[128,128]{1,0:T(8,128)} %bitcast.11, f32[128,128]{1,0:T(8,128)} %bitcast.12, f32[128,128]{1,0:T(8,128)} %bitcast.13, f32[128,128]{1,0:T(8,128)} %bitcast.14, s32[8,128,128]{2,1,0:T(8,128)} %bitcast.10, s32[128,128]{1,0:T(8,128)} %bitcast.15, ...), custom_call_target="tpu_custom_call" | custom-call | flops 20000000 | bytes 2000000 | tf_op jit(solution)/shard_map/pallas_call | solution.py:536
  33.7 3.1 %shard_map.104 = (f32[8,128,128]{2,1,0:T(8,128)}, f32[27,37]{1,0:T(8,128)}, f32[1,37]{1,0:T(1,128)}) custom-call(f32[8,128,128]{2,1,0:T(8,128)} %get-tuple-element.8.v_in, f32[16,128]{1,0:T(8,128)} %get-tuple-element.9.f_in), custom_call_target="tpu_custom_call" | custom-call | tf_op jit(solution)/shard_map/pallas_call | solution.py:568

commit v4 on v3

--- a/solution.py
+++ b/solution.py
@@ -10,11 +10,13 @@
 MESH = pl.DeviceIdType.MESH
 F32, BF16, I32 = jnp.float32, jnp.bfloat16, jnp.int32
 
-YC, CC = 4, 2
-VMEM_GRANT = 60 * 1024 * 1024
+G_BITS = (("layer", 1), ("layer", 2), ("plane", 16), ("plane", 32))
+H_BITS = (("plane", 1), ("plane", 2), ("plane", 4), ("plane", 8))
+VMEM_GRANT = 32 * 1024 * 1024
 THIRD, TWO_THIRDS = 1.0 / 3.0, 2.0 / 3.0
 B0 = (0, 1, 4, 5)
 A0 = (0, 1, 2, 3)
+TYM, TYP, TYM1, TYP1, TXM, TXP, TZM, TZP, TZM1, TZP1, TXB, RD = range(12)
 
 
 def roll_x(v, shift):
@@ -32,9 +34,6 @@
 
 def plane_sum(v):
     return v.reshape(-1, 8, 128).sum(axis=0)
-
-
-TYM, TYP, TYM1, TYP1, TXM, TXP, TZM, TZP, TZM1, TZP1, TXB, RD = range(12)
 
 
 def kernel(
@@ -43,44 +42,42 @@
     v_out, f_out,
     bi, sup, aa, pp, ss, blk, cr1, tab,
     va, vb, sf, nn, tc, tzb, ec, sw, fl, hx, hxs, hxr, hzr, hxs2, hxr2, hzr2,
-    rks, rkr, wt, oh, xb, es, cs, crv, acc, hs, hr,
+    rks, rkr, wt, oh, xb, es, cs, crv, hs, hr,
     in_sem, out_sem, halo_s, halo_r, rk_s, rk_r, g_s, g_r, h_s, h_r,
 ):
-    lx, plane, zc, own, width = dims
-    gn, hn = lx * YC, zc * CC
+    lx, plane, own, width = dims
+    gn, hn = 2 ** len(G_BITS), 2 ** len(H_BITS)
     n_idx = hn * width
     ml, mp = lax.axis_index("layer"), lax.axis_index("plane")
-    my, mz, mc = mp // (zc * CC), (mp // CC) % zc, mp % CC
-
-    def g_peer(r):
-        dx, dy = r // YC, r % YC
-        return ((ml + dx) % lx, (((my + dy) % YC) * zc + mz) * CC + mc)
-
-    def g_inv(r):
-        return ((lx - r // YC) % lx) * YC + (YC - r % YC) % YC
-
-    def h_peer(r):
-        dz, dc = r // CC, r % CC
-        return (ml, (my * zc + (mz + dz) % zc) * CC + (mc + dc) % CC)
-
-    def h_inv(r):
-        return ((zc - r // CC) % zc) * CC + (CC - r % CC) % CC
+
+    def flips(bits):
+        steps = []
+        for axis, bit in bits:
+            at = ml if axis == "layer" else mp
+            steps.append((axis == "layer", bit * (1 - 2 * ((at // bit) % 2))))
+        return steps
+
+    g_flips, h_flips = flips(G_BITS), flips(H_BITS)
+
+    def partner(steps, r):
+        to_l, to_p = ml, mp
+        for i, (on_layer, step) in enumerate(steps):
+            if (r >> i) & 1:
+                to_l, to_p = (to_l + step, to_p) if on_layer else (to_l, to_p + step)
+        return (to_l, to_p)
 
     up_x, down_x = (ml, (mp + 1) % plane), (ml, (mp + plane - 1) % plane)
     up_z, down_z = ((ml + 1) % lx, mp), ((ml + lx - 1) % lx, mp)
 
     def loop(n, body, start=0):
-        def step(i, carry):
+        for i in range(start, n):
             body(i)
-            return carry
-
-        lax.fori_loop(start, n, step, 0)
 
     def group(g):
-        return pl.ds(pl.multiple_of(g * 32, 32), 32)
+        return slice(g * 32, g * 32 + 32)
 
     def one_plane(z):
-        return pl.ds(pl.multiple_of(z * 8, 8), 8)
+        return slice(z * 8, z * 8 + 8)
 
     loads = [
         pltpu.make_async_copy(k_hbm, va.at[0], in_sem.at[0]),
@@ -103,8 +100,8 @@
 
     greet(up_x)
     greet(down_x)
-    loop(gn, lambda r: greet(g_peer(r)), 1)
-    loop(hn, lambda r: greet(h_peer(r)), 1)
+    loop(gn, lambda r: greet(partner(g_flips, r)), 1)
+    loop(hn, lambda r: greet(partner(h_flips, r)), 1)
 
     lane = lax.broadcasted_iota(I32, (32, 128), 1)
     m, x = lane % 8, lax.broadcasted_iota(I32, (32, 128), 0) % 8
@@ -116,11 +113,7 @@
     hx[...] = jnp.zeros_like(hx)
     es[...] = jnp.zeros_like(es)
     tc[TXB] = jnp.zeros((128, 128), F32)
-
-    def blank(i):
-        xb[i, 64:128, :] = jnp.zeros((64, 256), BF16)
-
-    loop(gn // 2, blank)
+    xb[64:128, :] = jnp.zeros((64, gn * 128), BF16)
 
     def wanted(i):
         idx = row1 + i * 8
@@ -128,10 +121,10 @@
         for t in range(1, hn):
             peer += jnp.where(idx >= t * width, 1, 0)
         col = idx - peer * width
-        pz, pc = mz + (peer >> (CC - 1)), mc + (peer & (CC - 1))
-        pz = jnp.where(pz >= zc, pz - zc, pz)
-        pc = jnp.where(pc >= CC, pc - CC, pc)
-        want = (ml * plane + (my * zc + pz) * CC + pc) * own + col
+        dev = jnp.zeros_like(idx) + (ml * plane + mp)
+        for b, (on_layer, step) in enumerate(h_flips):
+            dev += ((peer >> b) & 1) * (step * plane if on_layer else step)
+        want = dev * own + col
         for q in range(4):
             wt[one_plane(i + q * (n_idx // 8)), :] = jnp.where(col + q * width < own, want + q * width, -7)
 
@@ -154,10 +147,10 @@
         tz = harmonic(k, jnp.concatenate([va[0, below, :], k[0:24]], axis=0))
         tc[TZM, rows, :] = tz
         tc[TZP, below, :] = tz[0:8]
-        tc[TZP, pl.ds(pl.multiple_of(g * 32, 32), 24), :] = tz[8:32]
+        tc[TZP, slice(g * 32, g * 32 + 24), :] = tz[8:32]
         tc[TZM1, rows, :] = tz
         tc[TZP1, below, :] = tz[0:8]
-        tc[TZP1, pl.ds(pl.multiple_of(g * 32, 32), 24), :] = tz[8:32]
+        tc[TZP1, slice(g * 32, g * 32 + 24), :] = tz[8:32]
 
     loop(4, faces)
     nil = jnp.zeros((8, 128), F32)
@@ -212,16 +205,17 @@
             rows = group(g)
             odd = g % 2
             below, above = one_plane((4 * g + 15) % 16), one_plane((4 * g + 4) % 16)
-            coef = [tc[i, rows, :] for i in range(10)]
-            vals = [v[off + s, rows, :] for s in range(8)]
             for s in range(8):
-                here, turn = vals[s], 4 - (s & 4) * 2
-                tm, tp = (coef[TYM1], coef[TYP1]) if s & 1 else (coef[TYM], coef[TYP])
-                zm, zp = (coef[TZM1], coef[TZP1]) if s & 4 else (coef[TZM], coef[TZP])
-                near = tm * roll_y(jnp.where(is_m[7], vals[s ^ 1], here), 1)
-                near += tp * roll_y(jnp.where(is_m[0], vals[s ^ 1], here), 127)
-                near += coef[TXM] * roll_x(jnp.where(is_x[3], vals[s ^ 2], here), 1)
-                near += coef[TXP] * roll_x(jnp.where(is_x[4], vals[s ^ 2], here), 7)
+                if s % 4 == 0:
+                    vals = [v[off + s + i, rows, :] for i in range(4)]
+                    txm, txp = tc[TXM, rows, :], tc[TXP, rows, :]
+                    tym, typ = [tc[i, rows, :] for i in (TYM, TYM1)], [tc[i, rows, :] for i in (TYP, TYP1)]
+                    zm, zp = tc[TZM1 if s else TZM, rows, :], tc[TZP1 if s else TZP, rows, :]
+                here, by_y, by_x, turn = vals[s % 4], vals[s % 4 ^ 1], vals[s % 4 ^ 2], 4 - (s & 4) * 2
+                near = tym[s & 1] * roll_y(jnp.where(is_m[7], by_y, here), 1)
+                near += typ[s & 1] * roll_y(jnp.where(is_m[0], by_y, here), 127)
+                near += txm * roll_x(jnp.where(is_x[3], by_x, here), 1)
+                near += txp * roll_x(jnp.where(is_x[4], by_x, here), 7)
                 lo, hi = v[off + s + turn * odd, below, :], v[off + s + turn * (1 - odd), above, :]
                 near += zm * jnp.concatenate([lo, here[0:24]], axis=0)
                 near += zp * jnp.concatenate([here[8:32], hi], axis=0)
@@ -280,13 +274,13 @@
     for load in loads[4:]:
         load.wait()
     label = blk[0, 0:1, :]
-    for u, (j, r) in enumerate(((0, 0), (0, 4), (1, 0), (1, 4), (2, 0), (2, 4))):
+    for u, (j, r) in enumerate(((0, 0), (0, 4), (1, 0), (1, 4), (2, 0), (2, 4), (1, 0), (1, 4))):
         label = jnp.where(m1[0:1] == u, blk[j, r:r + 1, :], label)
     t_rows, labels = tab.shape[0], cr1.shape[0]
     tab[labels // 128:, :] = jnp.zeros((t_rows - labels // 128, 128), I32)
 
     def table(t):
-        tab[pl.ds(t, 1), :] = cr1[pl.ds(pl.multiple_of(t * 128, 128), 128)].reshape(1, 128)
+        tab[t:t + 1, :] = cr1[pl.ds(t * 128, 128)].reshape(1, 128)
 
     loop(labels // 128, table)
     if labels % 128:
@@ -301,14 +295,14 @@
     t_iota = lax.broadcasted_iota(I32, (t_rows, 128), 0)
     looked = looked[:t_rows] * 128.0 + looked[t_rows:]
     rank = jnp.sum(jnp.where(t_iota == l_hi, looked, 0.0), axis=0, keepdims=True)
-    rank = jnp.where(m1[0:1] < 6, rank, -1.0).astype(I32)
+    rank = rank.astype(I32)
     rks[...] = rank
     rkr[0] = rank
 
     def rank_copy(r):
         return pltpu.make_async_remote_copy(
-            src_ref=rks, dst_ref=rkr.at[g_inv(r)], send_sem=rk_s.at[r], recv_sem=rk_r.at[g_inv(r)],
-            device_id=g_peer(r), device_id_type=MESH)
+            src_ref=rks, dst_ref=rkr.at[r], send_sem=rk_s.at[r], recv_sem=rk_r.at[r],
+            device_id=partner(g_flips, r), device_id_type=MESH)
 
     loop(gn, lambda r: rank_copy(r).start(), 1)
 
@@ -374,107 +368,98 @@
 
     loop(4, gather)
 
-    for j in range(3):
-        for pz in range(3):
-            if pz == 1:
-                groups, a = ((0,), (1, 2), (3,))[j], 0
-            elif pz == 0:
-                groups, a = ((), (1,), (3,))[j], 1
-            else:
-                groups, a = ((0,), (2,), ())[j], 1
-            if not groups:
-                continue
-            for b in (1, 0):
-                at = 8 * ((1 - b) * 9 + 3 * pz)
-                for c in (0, 1):
-                    s = 4 * a + 2 * b + c
-                    term = fl[s, 8 * groups[0]:8 * groups[0] + 8, :]
-                    for g in groups[1:]:
-                        term += fl[s, 8 * g:8 * g + 8, :]
-                    if c:
-                        es[j, at:at + 8, :] = jnp.where(m1 < 4, term, 0.0)
-                        es[j, at + 16:at + 24, :] = jnp.where(m1 < 4, 0.0, term)
-                    else:
-                        es[j, at + 8:at + 16, :] = term
-        groups = ((0,), (1, 2), (3,))[j]
-        term = fl[8, 8 * groups[0]:8 * groups[0] + 8, :]
+    def z_part(j, pz, s):
+        groups = ((0,), (1, 2), (3,))[j] if pz == 1 else {(1, 0): (1,), (2, 0): (3,), (0, 2): (0,), (1, 2): (2,)}[j, pz]
+        term = fl[s, one_plane(groups[0]), :]
         for g in groups[1:]:
-            term += fl[8, 8 * g:8 * g + 8, :]
-        es[j, 144:152, :] = -term
-
-    m24 = m[:24]
-    rows_out = jnp.zeros((24, 128), F32)
-    for j in range(3):
+            term += fl[s, one_plane(g), :]
+        return term
+
+    for k, (j, halves) in enumerate(((0, (1, 2)), (1, (1, 2)), (2, (1, 0)), (1, (0,)))):
+        for half, pz in enumerate(halves):
+            for b in range(2):
+                at, s = 64 * half + 24 * b, (0 if pz == 1 else 4) + 2 * b
+                side = z_part(j, pz, s + 1)
+                es[k, at:at + 8, :] = jnp.where(m1 < 4, side, 0.0)
+                es[k, at + 8:at + 16, :] = z_part(j, pz, s)
+                es[k, at + 16:at + 24, :] = jnp.where(m1 < 4, 0.0, side)
+        if k < 3:
+            es[k, 48:56, :] = -z_part(j, 1, 8)
+
+    m16 = m[:16]
+    sums = []
+    for k in range(4):
         for xi in range(2):
-            t = es[j, pl.ds(4 * xi, 24, stride=8), :]
+            t = es[k, pl.ds(4 * xi, 16, stride=8), :]
             for i in range(1, 4):
-                t += es[j, pl.ds(4 * xi + i, 24, stride=8), :]
-            t += roll_y(t, 127)
-            t += roll_y(t, 126)
-            t += roll_y(t, 124)
-            u = 2 * j + xi
-            rows_out = jnp.where(m24 == u, roll_y(t, u) if u else t, rows_out)
+                t += es[k, pl.ds(4 * xi + i, 16, stride=8), :]
+            sums.append(t)
+    for bit in (4, 2, 1):
+        high = (m16 & bit) != 0
+        merged = []
+        for u in range(bit):
+            one, two = sums[u], sums[u + bit]
+            move = jnp.where(high, one, two)
+            merged.append(jnp.where(high, two, one) + jnp.where(high, roll_y(move, bit), roll_y(move, 128 - bit)))
+        sums = merged
+    rows_out = sums[0]
     cs[...] = rows_out
     crv[0] = rows_out
 
     def g_copy(r):
         return pltpu.make_async_remote_copy(
-            src_ref=cs, dst_ref=crv.at[g_inv(r)], send_sem=g_s.at[r], recv_sem=g_r.at[g_inv(r)],
-            device_id=g_peer(r), device_id_type=MESH)
+            src_ref=cs, dst_ref=crv.at[r], send_sem=g_s.at[r], recv_sem=g_r.at[r],
+            device_id=partner(g_flips, r), device_id_type=MESH)
 
     loop(gn, lambda r: g_copy(r).start(), 1)
 
     loop(gn, lambda r: rank_copy(r).wait_recv(), 1)
 
-    def build(i):
+    have = [rkr[r] for r in range(gn)]
+
+    def build(i, carry):
         at = pl.multiple_of(i * 16, 16)
         want = wt[pl.ds(at, 16), :]
         for r in range(gn):
-            oh[r // 2, pl.ds(at, 16), 128 * (r % 2):128 * (r % 2) + 128] = (
-                jnp.where(want == rkr[r], 1.0, 0.0).astype(BF16))
-
-    loop(4 * n_idx // 16, build)
+            oh[pl.ds(at, 16), 128 * r:128 * r + 128] = jnp.where(want == have[r], 1.0, 0.0).astype(BF16)
+        return carry
+
+    lax.fori_loop(0, 4 * n_idx // 16, build, 0)
 
     odd = m1 % 2 == 1
+    b1 = (x1 >= 3) & (x1 < 6)
+    b1_odd = b1 & odd
     loop(gn, lambda r: g_copy(r).wait_recv(), 1)
-
-    def spread(i):
-        for h in range(2):
-            got = [crv[2 * i + h, 8 * k:8 * k + 8, :] for k in range(3)]
-            turn = [pltpu.roll(jnp.where(odd, got[k], 0.0), 3, 0) for k in range(2)]
-            vals = jnp.concatenate([
-                jnp.where(odd, 0.0, got[0]), jnp.where(odd & (x1 == 0), 0.0, got[1]),
-                jnp.where(x1 < 3, got[2], turn[0]), jnp.where(x1 < 3, turn[0], turn[1])], axis=0)
-            high = vals.astype(BF16)
-            lanes = slice(128 * h, 128 * h + 128)
-            xb[i, 0:32, lanes] = high
-            xb[i, 32:64, lanes] = (vals - high.astype(F32)).astype(BF16)
-
-    loop(gn // 2, spread)
-
-    def product(i):
-        return lax.dot_general(oh[i], xb[i], (((1,), (1,)), ((), ())), preferred_element_type=F32)
-
-    acc[...] = product(0) + product(1)
-
-    def add_product(i):
-        acc[...] += product(2 * i) + product(2 * i + 1)
-
-    loop(gn // 4, add_product, 1)
-
-    low_lanes = lax.broadcasted_iota(I32, (n_idx, 128), 1) < 32
+    for r in range(gn):
+        got1, got2 = crv[r, 0:8, :], crv[r, 8:16, :]
+        pz1 = jnp.where(m1 < 6, got1, 0.0)
+        pz2 = jnp.where(m1 < 4, got2, 0.0)
+        pz0 = jnp.where(m1 < 4, 0.0, jnp.where(m1 < 6, got2, got1))
+        low1, low2, low0 = (jnp.where(b1_odd, v, 0.0) for v in (pz1, pz2, pz0))
+        last = pltpu.roll(low1, 5, 0) + low2 + jnp.where(x1 >= 6, pltpu.roll(low0, 3, 0), 0.0)
+        vals = jnp.concatenate([
+            pz1 - low1 + jnp.where(x1 == 7, pltpu.roll(low0, 2, 0), 0.0), pz2 - low2, pz0 - low0, last], axis=0)
+        high = vals.astype(BF16)
+        lanes = slice(128 * r, 128 * r + 128)
+        xb[0:32, lanes] = high
+        xb[32:64, lanes] = (vals - high.astype(F32)).astype(BF16)
+
+    routed = lax.dot_general(
+        oh[...], xb[...], (((1,), (1,)), ((), ())), preferred_element_type=F32)
+    quarter = lax.broadcasted_iota(I32, (n_idx, 128), 1) >> 5
     packed = jnp.zeros((n_idx, 128), F32)
     for q in range(4):
-        part = acc[q * n_idx:(q + 1) * n_idx, :]
-        both = jnp.where(low_lanes, part + roll_y(part, 96), 0.0)
-        packed += roll_y(both, 32 * q) if q else both
+        part = routed[q * n_idx:(q + 1) * n_idx]
+        first_half = roll_y(part, 32 * q) if q else part
+        second_half = part if q == 1 else roll_y(part, (32 * q + 96) % 128)
+        packed = jnp.where(quarter == q, first_half + second_half, packed)
     for r in range(hn):
         hs[r] = packed[r * width:(r + 1) * width]
 
     def h_copy(r):
         return pltpu.make_async_remote_copy(
-            src_ref=hs.at[r], dst_ref=hr.at[h_inv(r)], send_sem=h_s.at[r], recv_sem=h_r.at[h_inv(r)],
-            device_id=h_peer(r), device_id_type=MESH)
+            src_ref=hs.at[r], dst_ref=hr.at[r], send_sem=h_s.at[r], recv_sem=h_r.at[r],
+            device_id=partner(h_flips, r), device_id_type=MESH)
 
     loop(hn, lambda r: h_copy(r).start(), 1)
     loop(hn, lambda r: h_copy(r).wait_recv(), 1)
@@ -495,14 +480,9 @@
     loop(hn, lambda r: h_copy(r).wait_send(), 1)
 
 
-def finish(own, width, v_in, f_in, v_out, cm_out, cr_out, vv, ft, sem):
-    fetch = [pltpu.make_async_copy(v_in.at[s], vv.at[s], sem.at[0, s]) for s in range(8)]
-    store = [pltpu.make_async_copy(vv.at[s], v_out.at[s], sem.at[1, s]) for s in range(8)]
-    for copy in fetch:
-        copy.start()
-    for s in range(8):
-        fetch[s].wait()
-        store[s].start()
+def finish(own, width, v_in, f_in, v_out, cm_out, cr_out, ft, sem):
+    store = pltpu.make_async_copy(v_in, v_out, sem)
+    store.start()
     ft[0:16, :] = f_in[...]
     turned = ft[...].T
     lane = lax.broadcasted_iota(I32, (32, 128), 1)
@@ -511,19 +491,19 @@
         part = turned[32 * q:32 * q + 32]
         here = (lane >= q * width) & (lane < (q + 1) * width)
         done = jnp.where(here, pltpu.roll(part, q * width, 1) if q else part, done)
-    for pz in range(3):
-        for px, base in ((0, 19), (1, 9), (2, 0)):
-            k = 9 * pz + 3 * px
-            cm_out[k:k + 3, :] = done[base + 3 * pz:base + 3 * pz + 3, 0:own]
-    cr_out[...] = done[18:19, 0:own]
-    for copy in store:
-        copy.wait()
+    for pz, px, base in (
+        (1, 1, 0), (1, 2, 3), (2, 1, 8), (2, 2, 11), (0, 1, 16), (0, 2, 19), (1, 0, 24), (2, 0, 27)):
+        k = 9 * pz + 3 * px
+        cm_out[k:k + 3, :] = done[base:base + 3, 0:own]
+    cm_out[0:2, :] = done[30:32, 0:own]
+    cm_out[2:3, :] = done[7:8, 0:own]
+    cr_out[...] = done[6:7, 0:own]
+    store.wait()
 
 
 def per_device(sizes, basis_init, permeability, accumulation, pressure, source, support, block_of, curve_rank):
     lx, plane = sizes
-    zc = plane // (YC * CC)
-    gn, hn = lx * YC, zc * CC
+    gn, hn = 2 ** len(G_BITS), 2 ** len(H_BITS)
     devices = lx * plane
     own = (curve_rank.shape[0] + devices - 1) // devices
     width = (own + 3) // 4
@@ -534,7 +514,7 @@
     dma = pltpu.SemaphoreType.DMA
     cells = lambda *lead: pltpu.VMEM(lead + (128, 128), F32)
     basis, rows = pl.pallas_call(
-        functools.partial(kernel, (lx, plane, zc, own, width)),
+        functools.partial(kernel, (lx, plane, own, width)),
         out_shape=(
             jax.ShapeDtypeStruct((8, 128, 128), F32),
             jax.ShapeDtypeStruct((16, 128), F32),
@@ -550,10 +530,9 @@
             pltpu.VMEM((2, 5, 16, 128), F32), pltpu.VMEM((2, 5, 16, 128), F32), pltpu.VMEM((2, 5, 8, 128), F32),
             pltpu.VMEM((2, 4, 16, 128), F32), pltpu.VMEM((2, 4, 16, 128), F32), pltpu.VMEM((2, 4, 8, 128), F32),
             pltpu.VMEM((1, 128), I32), pltpu.VMEM((gn, 1, 128), I32),
-            pltpu.VMEM((4 * hn * width, 128), I32), pltpu.VMEM((gn // 2, 4 * hn * width, 256), BF16),
-            pltpu.VMEM((gn // 2, 128, 256), BF16), pltpu.VMEM((3, 192, 128), F32),
-            pltpu.VMEM((24, 128), F32), pltpu.VMEM((gn, 24, 128), F32),
-            pltpu.VMEM((4 * hn * width, 128), F32),
+            pltpu.VMEM((4 * hn * width, 128), I32), pltpu.VMEM((4 * hn * width, gn * 128), BF16),
+            pltpu.VMEM((128, gn * 128), BF16), pltpu.VMEM((4, 128, 128), F32),
+            pltpu.VMEM((16, 128), F32), pltpu.VMEM((gn, 16, 128), F32),
             pltpu.VMEM((hn, width, 128), F32), pltpu.VMEM((hn, width, 128), F32),
             dma((10,)), dma((1,)), dma((8,)), dma((8,)),
             dma((gn,)), dma((gn,)), dma((gn,)), dma((gn,)), dma((hn,)), dma((hn,)),
@@ -561,10 +540,10 @@
         compiler_params=pltpu.CompilerParams(
             collective_id=0, has_side_effects=True, vmem_limit_bytes=VMEM_GRANT),
         cost_estimate=pl.CostEstimate(flops=20_000_000, bytes_accessed=2_000_000, transcendentals=0),
-    )(
+    )(*(pltpu.with_memory_space_constraint(v, pltpu.HBM) for v in (
         flat(basis_init), flat(permeability), flat(accumulation), flat(pressure), flat(source),
         flat(support), flat(block_of), curve_rank,
-    )
+    )))
     basis, matrix, residual = pl.pallas_call(
         functools.partial(finish, own, width),
         out_shape=(
@@ -574,7 +553,7 @@
         ),
         in_specs=[anywhere, vmem],
         out_specs=(anywhere, vmem, vmem),
-        scratch_shapes=[cells(8), cells(), dma((2, 8))],
+        scratch_shapes=[cells(), dma],
         compiler_params=pltpu.CompilerParams(vmem_limit_bytes=VMEM_GRANT),
     )(basis, rows)
     return basis.reshape(basis_init.shape), matrix, residual.reshape(own)

time: 37.1 us -> 32.5 us (0.88)
  Pallas kernels: 36.2 us -> 31.8 us
    pallas_call x1, Pallas kernels: 33.1 us -> 30.4 us  [per_device(): pl.pallas_call(functools.partial(kernel, (lx, plane, own, width)), out_sh...]
    pallas_call x1, Pallas kernels: 3.13 us -> 1.41 us  [per_device(): pl.pallas_call(functools.partial(finish, own, width), out_shape=(jax.Shap...]
where the time goes in v4:
time: 32.5 us; the launch traced here: 32.4 us
  Pallas kernels  31.8 us (98%)
  between operations  0.64 us (2%)
    pallas_call x1, Pallas kernels, per_device(): pl.pallas_call(functools.partial(kernel, (lx, plane, own, width)), out_sh...  30.4 us
    pallas_call x1, Pallas kernels, per_device(): pl.pallas_call(functools.partial(finish, own, width), out_shape=(jax.Shap...  1.41 us

profile of v4, /device:TPU:1, one launch (start us, length us, event | category | flops | bytes accessed | tf_op | source)
XLA Modules:
  0.0 32.4 jit_solution(2189046748076335625)
XLA Ops:
  0.6 30.4 %shard_map.103 = (f32[8,128,128]{2,1,0:T(8,128)S(1)}, f32[16,128]{1,0:T(8,128)S(1)}) custom-call(f32[8,128,128]{2,1,0:T(8,128)} %bitcast.9, f32[128,128]{1,0:T(8,128)} %bitcast.11, f32[128,128]{1,0:T(8,128)} %bitcast.12, f32[128,128]{1,0:T(8,128)} %bitcast.13, f32[128,128]{1,0:T(8,128)} %bitcast.14, s32[8,128,128]{2,1,0:T(8,128)} %bitcast.10, ...), custom_call_target="tpu_custom_call" | custom-call | flops 20000000 | bytes 2000000 | tf_op jit(solution)/shard_map/pallas_call | solution.py:516
  31.0 1.4 %shard_map.104 = (f32[8,128,128]{2,1,0:T(8,128)}, f32[27,37]{1,0:T(8,128)}, f32[1,37]{1,0:T(1,128)}) custom-call(f32[8,128,128]{2,1,0:T(8,128)S(1)} %get-tuple-element.8.v_in, f32[16,128]{1,0:T(8,128)S(1)} %get-tuple-element.9.f_in), custom_call_target="tpu_custom_call" | custom-call | tf_op jit(solution)/shard_map/pallas_call | solution.py:547

commit v5 on v4

--- a/solution.py
+++ b/solution.py
@@ -90,9 +90,6 @@
     ]
     for j, z in enumerate((0, 4, 12)):
         loads.append(pltpu.make_async_copy(blk_hbm.at[pl.ds(8 * z, 8)], blk.at[j], in_sem.at[7 + j]))
-    for load in loads:
-        load.start()
-
     barrier = pltpu.get_barrier_semaphore()
 
     def greet(who):
@@ -100,8 +97,16 @@
 
     greet(up_x)
     greet(down_x)
-    loop(gn, lambda r: greet(partner(g_flips, r)), 1)
+    g_order = [1, 3, 2][:gn - 1] + list(range(4, gn))
+    for r in g_order[:2]:
+        greet(partner(g_flips, r))
+    for load in loads[:3]:
+        load.start()
+    for r in g_order[2:]:
+        greet(partner(g_flips, r))
     loop(hn, lambda r: greet(partner(h_flips, r)), 1)
+    for load in loads[3:]:
+        load.start()
 
     lane = lax.broadcasted_iota(I32, (32, 128), 1)
     m, x = lane % 8, lax.broadcasted_iota(I32, (32, 128), 0) % 8
@@ -111,24 +116,7 @@
     is_x = {i: x == i for i in (3, 4)}
 
     hx[...] = jnp.zeros_like(hx)
-    es[...] = jnp.zeros_like(es)
     tc[TXB] = jnp.zeros((128, 128), F32)
-    xb[64:128, :] = jnp.zeros((64, gn * 128), BF16)
-
-    def wanted(i):
-        idx = row1 + i * 8
-        peer = jnp.zeros_like(idx)
-        for t in range(1, hn):
-            peer += jnp.where(idx >= t * width, 1, 0)
-        col = idx - peer * width
-        dev = jnp.zeros_like(idx) + (ml * plane + mp)
-        for b, (on_layer, step) in enumerate(h_flips):
-            dev += ((peer >> b) & 1) * (step * plane if on_layer else step)
-        want = dev * own + col
-        for q in range(4):
-            wt[one_plane(i + q * (n_idx // 8)), :] = jnp.where(col + q * width < own, want + q * width, -7)
-
-    loop(n_idx // 8, wanted)
 
     loads[0].wait()
 
@@ -305,6 +293,7 @@
             device_id=partner(g_flips, r), device_id_type=MESH)
 
     loop(gn, lambda r: rank_copy(r).start(), 1)
+    es[...] = jnp.zeros_like(es)
 
     inner(vb, 0)
 
@@ -413,6 +402,23 @@
 
     loop(gn, lambda r: g_copy(r).start(), 1)
 
+    xb[64:128, :] = jnp.zeros((64, gn * 128), BF16)
+
+    def wanted(i):
+        idx = row1 + i * 8
+        peer = jnp.zeros_like(idx)
+        for t in range(1, hn):
+            peer += jnp.where(idx >= t * width, 1, 0)
+        col = idx - peer * width
+        dev = jnp.zeros_like(idx) + (ml * plane + mp)
+        for b, (on_layer, step) in enumerate(h_flips):
+            dev += ((peer >> b) & 1) * (step * plane if on_layer else step)
+        want = dev * own + col
+        for q in range(4):
+            wt[one_plane(i + q * (n_idx // 8)), :] = jnp.where(col + q * width < own, want + q * width, -7)
+
+    loop(n_idx // 8, wanted)
+
     loop(gn, lambda r: rank_copy(r).wait_recv(), 1)
 
     have = [rkr[r] for r in range(gn)]
@@ -429,8 +435,8 @@
     odd = m1 % 2 == 1
     b1 = (x1 >= 3) & (x1 < 6)
     b1_odd = b1 & odd
-    loop(gn, lambda r: g_copy(r).wait_recv(), 1)
-    for r in range(gn):
+
+    def spread(r):
         got1, got2 = crv[r, 0:8, :], crv[r, 8:16, :]
         pz1 = jnp.where(m1 < 6, got1, 0.0)
         pz2 = jnp.where(m1 < 4, got2, 0.0)
@@ -444,8 +450,17 @@
         xb[0:32, lanes] = high
         xb[32:64, lanes] = (vals - high.astype(F32)).astype(BF16)
 
-    routed = lax.dot_general(
-        oh[...], xb[...], (((1,), (1,)), ((), ())), preferred_element_type=F32)
+    def product(part):
+        return lax.dot_general(
+            oh[:, part], xb[:, part], (((1,), (1,)), ((), ())), preferred_element_type=F32)
+
+    half = gn // 2
+    loop(half, lambda r: g_copy(r).wait_recv(), 1)
+    loop(half, spread)
+    routed = product(slice(0, half * 128))
+    loop(gn, lambda r: g_copy(r).wait_recv(), half)
+    loop(gn, spread, half)
+    routed += product(slice(half * 128, gn * 128))
     quarter = lax.broadcasted_iota(I32, (n_idx, 128), 1) >> 5
     packed = jnp.zeros((n_idx, 128), F32)
     for q in range(4):

time: 32.5 us -> 32.5 us (level)
  no operation moved by 1% of the time
where the time goes in v5:
time: 32.5 us; the launch traced here: 32.4 us
  Pallas kernels  31.8 us (98%)
  between operations  0.64 us (2%)
    pallas_call x1, Pallas kernels, per_device(): pl.pallas_call(functools.partial(kernel, (lx, plane, own, width)), out_sh...  30.4 us
    pallas_call x1, Pallas kernels, per_device(): pl.pallas_call(functools.partial(finish, own, width), out_shape=(jax.Shap...  1.41 us

profile of v5, /device:TPU:1, one launch (start us, length us, event | category | flops | bytes accessed | tf_op | source)
XLA Modules:
  0.0 32.4 jit_solution(3603586846497840496)
XLA Ops:
  0.6 30.4 %shard_map.103 = (f32[8,128,128]{2,1,0:T(8,128)S(1)}, f32[16,128]{1,0:T(8,128)S(1)}) custom-call(f32[8,128,128]{2,1,0:T(8,128)} %bitcast.9, f32[128,128]{1,0:T(8,128)} %bitcast.11, f32[128,128]{1,0:T(8,128)} %bitcast.12, f32[128,128]{1,0:T(8,128)} %bitcast.13, f32[128,128]{1,0:T(8,128)} %bitcast.14, s32[8,128,128]{2,1,0:T(8,128)} %bitcast.10, ...), custom_call_target="tpu_custom_call" | custom-call | flops 20000000 | bytes 2000000 | tf_op jit(solution)/shard_map/pallas_call | solution.py:531
  31.0 1.4 %shard_map.104 = (f32[8,128,128]{2,1,0:T(8,128)}, f32[27,37]{1,0:T(8,128)}, f32[1,37]{1,0:T(1,128)}) custom-call(f32[8,128,128]{2,1,0:T(8,128)S(1)} %get-tuple-element.8.v_in, f32[16,128]{1,0:T(8,128)S(1)} %get-tuple-element.9.f_in), custom_call_target="tpu_custom_call" | custom-call | tf_op jit(solution)/shard_map/pallas_call | solution.py:562

commit v6 on v5

--- a/solution.py
+++ b/solution.py
@@ -10,8 +10,8 @@
 MESH = pl.DeviceIdType.MESH
 F32, BF16, I32 = jnp.float32, jnp.bfloat16, jnp.int32
 
-G_BITS = (("layer", 1), ("layer", 2), ("plane", 16), ("plane", 32))
-H_BITS = (("plane", 1), ("plane", 2), ("plane", 4), ("plane", 8))
+G_BITS = (("layer", 1), ("plane", 1), ("plane", 2), ("plane", 16))
+H_BITS = (("layer", 2), ("plane", 4), ("plane", 8), ("plane", 32))
 VMEM_GRANT = 32 * 1024 * 1024
 THIRD, TWO_THIRDS = 1.0 / 3.0, 2.0 / 3.0
 B0 = (0, 1, 4, 5)
@@ -97,13 +97,11 @@
 
     greet(up_x)
     greet(down_x)
-    g_order = [1, 3, 2][:gn - 1] + list(range(4, gn))
-    for r in g_order[:2]:
-        greet(partner(g_flips, r))
+    greet(up_z)
+    greet(down_z)
     for load in loads[:3]:
         load.start()
-    for r in g_order[2:]:
-        greet(partner(g_flips, r))
+    loop(gn, lambda r: greet(partner(g_flips, r)), 1)
     loop(hn, lambda r: greet(partner(h_flips, r)), 1)
     for load in loads[3:]:
         load.start()
@@ -174,7 +172,7 @@
         if off:
             xs_buf[0, 0] = v[0, pl.ds(0, 16, stride=8), :]
             xs_buf[1, 0] = v[0, pl.ds(7, 16, stride=8), :]
-            pl.semaphore_wait(barrier, gn + hn)
+            pl.semaphore_wait(barrier, 2 + gn + hn)
         last, lead = v.at[pl.ds(0, off + 4), pl.ds(120, 8)], v.at[pl.ds(0, off + 4), pl.ds(0, 8)]
         copies = []
         for j, (src, dst, who) in enumerate((

time: 32.5 us -> 36 us (1.11)
  Pallas kernels: 31.8 us -> 35.3 us
    pallas_call x1, Pallas kernels: 30.4 us -> 33.8 us  [per_device(): pl.pallas_call(functools.partial(kernel, (lx, plane, own, width)), out_sh...]
where the time goes in v6:
time: 36 us; the launch traced here: 35.9 us
  Pallas kernels  35.3 us (98%)
  between operations  0.64 us (2%)
    pallas_call x1, Pallas kernels, per_device(): pl.pallas_call(functools.partial(kernel, (lx, plane, own, width)), out_sh...  33.8 us
    pallas_call x1, Pallas kernels, per_device(): pl.pallas_call(functools.partial(finish, own, width), out_shape=(jax.Shap...  1.41 us

profile of v6, /device:TPU:1, one launch (start us, length us, event | category | flops | bytes accessed | tf_op | source)
XLA Modules:
  0.0 35.9 jit_solution(1079136703564121424)
XLA Ops:
  0.6 33.8 %shard_map.103 = (f32[8,128,128]{2,1,0:T(8,128)S(1)}, f32[16,128]{1,0:T(8,128)S(1)}) custom-call(f32[8,128,128]{2,1,0:T(8,128)} %bitcast.9, f32[128,128]{1,0:T(8,128)} %bitcast.11, f32[128,128]{1,0:T(8,128)} %bitcast.12, f32[128,128]{1,0:T(8,128)} %bitcast.13, f32[128,128]{1,0:T(8,128)} %bitcast.14, s32[8,128,128]{2,1,0:T(8,128)} %bitcast.10, ...), custom_call_target="tpu_custom_call" | custom-call | flops 20000000 | bytes 2000000 | tf_op jit(solution)/shard_map/pallas_call | solution.py:529
  34.5 1.4 %shard_map.104 = (f32[8,128,128]{2,1,0:T(8,128)}, f32[27,37]{1,0:T(8,128)}, f32[1,37]{1,0:T(1,128)}) custom-call(f32[8,128,128]{2,1,0:T(8,128)S(1)} %get-tuple-element.8.v_in, f32[16,128]{1,0:T(8,128)S(1)} %get-tuple-element.9.f_in), custom_call_target="tpu_custom_call" | custom-call | tf_op jit(solution)/shard_map/pallas_call | solution.py:560

commit v7 on v5

--- a/solution.py
+++ b/solution.py
@@ -43,10 +43,11 @@
     bi, sup, aa, pp, ss, blk, cr1, tab,
     va, vb, sf, nn, tc, tzb, ec, sw, fl, hx, hxs, hxr, hzr, hxs2, hxr2, hzr2,
     rks, rkr, wt, oh, xb, es, cs, crv, hs, hr,
-    in_sem, out_sem, halo_s, halo_r, rk_s, rk_r, g_s, g_r, h_s, h_r,
+    round_y, round_z, in_sem, out_sem, halo_s, halo_r, rk_s, rk_r, g_s, g_r, h_s, h_r,
 ):
     lx, plane, own, width = dims
     gn, hn = 2 ** len(G_BITS), 2 ** len(H_BITS)
+    zc = hn // 2
     n_idx = hn * width
     ml, mp = lax.axis_index("layer"), lax.axis_index("plane")
 
@@ -95,18 +96,32 @@
     def greet(who):
         pl.semaphore_signal(barrier, inc=1, device_id=who, device_id_type=MESH)
 
+    def along_z(dz, dc):
+        return (ml, mp + dc * (1 - 2 * (mp % 2)) + 2 * ((mp // 2 + dz) % zc - (mp // 2) % zc))
+
+    x_mask = sum(1 << i for i, (axis, _) in enumerate(G_BITS) if axis == "layer")
+    x_peers = [r for r in range(1, gn) if r & x_mask == r]
+    y_peers = [r for r in range(1, gn) if r & x_mask == 0]
+    z_peers = [(dz, dc) for dz in (1, zc - 1, 2, zc - 2) for dc in (0, 1)] + [(0, 1)]
     greet(up_x)
     greet(down_x)
-    g_order = [1, 3, 2][:gn - 1] + list(range(4, gn))
-    for r in g_order[:2]:
+    for r in x_peers:
         greet(partner(g_flips, r))
     for load in loads[:3]:
         load.start()
-    for r in g_order[2:]:
+    for r in y_peers:
         greet(partner(g_flips, r))
-    loop(hn, lambda r: greet(partner(h_flips, r)), 1)
+    for dz, dc in z_peers:
+        greet(along_z(dz, dc))
     for load in loads[3:]:
         load.start()
+    greeted = 2 + len(x_peers) + len(y_peers) + len(z_peers)
+
+    def second_round():
+        for r in y_peers:
+            pl.semaphore_signal(round_y, inc=1, device_id=partner(g_flips, r), device_id_type=MESH)
+        for dz in (2, zc - 2):
+            pl.semaphore_signal(round_z, inc=1, device_id=along_z(dz, 0), device_id_type=MESH)
 
     lane = lax.broadcasted_iota(I32, (32, 128), 1)
     m, x = lane % 8, lax.broadcasted_iota(I32, (32, 128), 0) % 8
@@ -174,7 +189,7 @@
         if off:
             xs_buf[0, 0] = v[0, pl.ds(0, 16, stride=8), :]
             xs_buf[1, 0] = v[0, pl.ds(7, 16, stride=8), :]
-            pl.semaphore_wait(barrier, gn + hn)
+            pl.semaphore_wait(barrier, greeted)
         last, lead = v.at[pl.ds(0, off + 4), pl.ds(120, 8)], v.at[pl.ds(0, off + 4), pl.ds(0, 8)]
         copies = []
         for j, (src, dst, who) in enumerate((
@@ -186,6 +201,8 @@
                 device_id=who, device_id_type=MESH))
         for copy in copies:
             copy.start()
+        if off:
+            second_round()
         return copies
 
     def inner(v, off):
@@ -292,6 +309,7 @@
             src_ref=rks, dst_ref=rkr.at[r], send_sem=rk_s.at[r], recv_sem=rk_r.at[r],
             device_id=partner(g_flips, r), device_id_type=MESH)
 
+    pl.semaphore_wait(round_y, len(y_peers))
     loop(gn, lambda r: rank_copy(r).start(), 1)
     es[...] = jnp.zeros_like(es)
 
@@ -476,6 +494,7 @@
             src_ref=hs.at[r], dst_ref=hr.at[r], send_sem=h_s.at[r], recv_sem=h_r.at[r],
             device_id=partner(h_flips, r), device_id_type=MESH)
 
+    pl.semaphore_wait(round_z, 2)
     loop(hn, lambda r: h_copy(r).start(), 1)
     loop(hn, lambda r: h_copy(r).wait_recv(), 1)
     final = hs[0]
@@ -549,7 +568,7 @@
             pltpu.VMEM((128, gn * 128), BF16), pltpu.VMEM((4, 128, 128), F32),
             pltpu.VMEM((16, 128), F32), pltpu.VMEM((gn, 16, 128), F32),
             pltpu.VMEM((hn, width, 128), F32), pltpu.VMEM((hn, width, 128), F32),
-            dma((10,)), dma((1,)), dma((8,)), dma((8,)),
+            pltpu.SemaphoreType.REGULAR, pltpu.SemaphoreType.REGULAR, dma((10,)), dma((1,)), dma((8,)), dma((8,)),
             dma((gn,)), dma((gn,)), dma((gn,)), dma((gn,)), dma((hn,)), dma((hn,)),
         ],
         compiler_params=pltpu.CompilerParams(

time: 32.5 us -> 31.6 us (0.972)
  Pallas kernels: 31.8 us -> 30.8 us
    pallas_call x1, Pallas kernels: 30.4 us -> 29.4 us  [per_device(): pl.pallas_call(functools.partial(kernel, (lx, plane, own, width)), out_sh...]
where the time goes in v7:
time: 31.6 us; the launch traced here: 31.5 us
  Pallas kernels  30.8 us (97%)
  between operations  0.64 us (2%)
    pallas_call x1, Pallas kernels, per_device(): pl.pallas_call(functools.partial(kernel, (lx, plane, own, width)), out_sh...  29.4 us
    pallas_call x1, Pallas kernels, per_device(): pl.pallas_call(functools.partial(finish, own, width), out_shape=(jax.Shap...  1.41 us

profile of v7, /device:TPU:1, one launch (start us, length us, event | category | flops | bytes accessed | tf_op | source)
XLA Modules:
  0.0 31.5 jit_solution(1613659391539788420)
XLA Ops:
  0.6 29.4 %shard_map.103 = (f32[8,128,128]{2,1,0:T(8,128)S(1)}, f32[16,128]{1,0:T(8,128)S(1)}) custom-call(f32[8,128,128]{2,1,0:T(8,128)} %bitcast.9, f32[128,128]{1,0:T(8,128)} %bitcast.11, f32[128,128]{1,0:T(8,128)} %bitcast.12, f32[128,128]{1,0:T(8,128)} %bitcast.13, f32[128,128]{1,0:T(8,128)} %bitcast.14, s32[8,128,128]{2,1,0:T(8,128)} %bitcast.10, ...), custom_call_target="tpu_custom_call" | custom-call | flops 20000000 | bytes 2000000 | tf_op jit(solution)/shard_map/pallas_call | solution.py:550
  30.1 1.4 %shard_map.104 = (f32[8,128,128]{2,1,0:T(8,128)}, f32[27,37]{1,0:T(8,128)}, f32[1,37]{1,0:T(1,128)}) custom-call(f32[8,128,128]{2,1,0:T(8,128)S(1)} %get-tuple-element.8.v_in, f32[16,128]{1,0:T(8,128)S(1)} %get-tuple-element.9.f_in), custom_call_target="tpu_custom_call" | custom-call | tf_op jit(solution)/shard_map/pallas_call | solution.py:581

commit v8 on v7

--- a/solution.py
+++ b/solution.py
@@ -34,6 +34,18 @@
 
 def plane_sum(v):
     return v.reshape(-1, 8, 128).sum(axis=0)
+
+
+def far_first(bits):
+    def hops(r):
+        reach = {"layer": 0, "y": 0, "z": 0}
+        for i, (axis, bit) in enumerate(bits):
+            if (r >> i) & 1:
+                kind, step = (axis, bit) if axis == "layer" else ("y", bit // 16) if bit >= 16 else ("z", bit // 2)
+                reach[kind] += step
+        return sum(min(n, size - n) for n, size in ((reach["layer"], 4), (reach["y"], 4), (reach["z"], 8)))
+
+    return sorted(range(1, 2 ** len(bits)), key=lambda r: -hops(r))
 
 
 def kernel(
@@ -252,31 +264,8 @@
 
     sent = exchange(va, 1, hxs, hxr, hzr, 0)
     inner(va, 1)
-    loads[3].wait()
-    for copy in sent:
-        copy.wait_recv()
-
-    tc[TXB, pl.ds(0, 16, stride=8), :] = jnp.where(mp > 0, harmonic(hxs[0, 0], hxr[0, 0]), 0.0)
-    tc[TXB, pl.ds(7, 16, stride=8), :] = jnp.where(mp < plane - 1, harmonic(hxs[1, 0], hxr[1, 0]), 0.0)
-    tzb[0] = jnp.where(ml > 0, harmonic(va[0, 0:8, :], hzr[0, 0]), 0.0)
-    tzb[1] = jnp.where(ml < lx - 1, harmonic(va[0, 120:128, :], hzr[1, 0]), 0.0)
-
-    def scale(g):
-        rows = group(g)
-        diag = aa[rows, :]
-        for t in (TYM, TYP, TXM, TXP, TXB, TZM, TZP):
-            diag += tc[t, rows, :]
-        tc[RD, rows, :] = diag
-
-    loop(4, scale)
-    tc[RD, 0:8, :] += tzb[0]
-    tc[RD, 120:128, :] += tzb[1]
-    tc[RD] = TWO_THIRDS / tc[RD]
-
-    outer(va, 1, vb, 0, hxr, hzr, 1)
-    sent2 = exchange(vb, 0, hxs2, hxr2, hzr2, 4)
-
-    for load in loads[4:]:
+
+    for load in loads[3:]:
         load.wait()
     label = blk[0, 0:1, :]
     for u, (j, r) in enumerate(((0, 0), (0, 4), (1, 0), (1, 4), (2, 0), (2, 4), (1, 0), (1, 4))):
@@ -304,6 +293,29 @@
     rks[...] = rank
     rkr[0] = rank
 
+    def diagonal(g):
+        rows = group(g)
+        diag = aa[rows, :]
+        for t in (TYM, TYP, TXM, TXP, TZM, TZP):
+            diag += tc[t, rows, :]
+        tc[RD, rows, :] = diag
+
+    loop(4, diagonal)
+    for copy in sent:
+        copy.wait_recv()
+
+    tc[TXB, pl.ds(0, 16, stride=8), :] = jnp.where(mp > 0, harmonic(hxs[0, 0], hxr[0, 0]), 0.0)
+    tc[TXB, pl.ds(7, 16, stride=8), :] = jnp.where(mp < plane - 1, harmonic(hxs[1, 0], hxr[1, 0]), 0.0)
+    tzb[0] = jnp.where(ml > 0, harmonic(va[0, 0:8, :], hzr[0, 0]), 0.0)
+    tzb[1] = jnp.where(ml < lx - 1, harmonic(va[0, 120:128, :], hzr[1, 0]), 0.0)
+
+    tc[RD, 0:8, :] += tzb[0]
+    tc[RD, 120:128, :] += tzb[1]
+    tc[RD] = TWO_THIRDS / (tc[RD] + tc[TXB])
+
+    outer(va, 1, vb, 0, hxr, hzr, 1)
+    sent2 = exchange(vb, 0, hxs2, hxr2, hzr2, 4)
+
     def rank_copy(r):
         return pltpu.make_async_remote_copy(
             src_ref=rks, dst_ref=rkr.at[r], send_sem=rk_s.at[r], recv_sem=rk_r.at[r],
@@ -338,7 +350,7 @@
             ec[s, 8 * z:8 * z + 8, :] += t
 
     def x_swap(q):
-        return jnp.where(x1 == 3, roll_x(q, 7), jnp.where(x1 == 4, roll_x(q, 1), 0.0))
+        return roll_x(q, 4)
 
     def y_swap(q):
         return jnp.where(m1 == 7, roll_y(q, 127), jnp.where(m1 == 0, roll_y(q, 1), 0.0))
@@ -418,7 +430,8 @@
             src_ref=cs, dst_ref=crv.at[r], send_sem=g_s.at[r], recv_sem=g_r.at[r],
             device_id=partner(g_flips, r), device_id_type=MESH)
 
-    loop(gn, lambda r: g_copy(r).start(), 1)
+    for r in far_first(G_BITS):
+        g_copy(r).start()
 
     xb[64:128, :] = jnp.zeros((64, gn * 128), BF16)
 
@@ -486,16 +499,16 @@
         first_half = roll_y(part, 32 * q) if q else part
         second_half = part if q == 1 else roll_y(part, (32 * q + 96) % 128)
         packed = jnp.where(quarter == q, first_half + second_half, packed)
-    for r in range(hn):
-        hs[r] = packed[r * width:(r + 1) * width]
-
     def h_copy(r):
         return pltpu.make_async_remote_copy(
             src_ref=hs.at[r], dst_ref=hr.at[r], send_sem=h_s.at[r], recv_sem=h_r.at[r],
             device_id=partner(h_flips, r), device_id_type=MESH)
 
     pl.semaphore_wait(round_z, 2)
-    loop(hn, lambda r: h_copy(r).start(), 1)
+    for r in far_first(H_BITS):
+        hs[r] = packed[r * width:(r + 1) * width]
+        h_copy(r).start()
+    hs[0] = packed[0:width]
     loop(hn, lambda r: h_copy(r).wait_recv(), 1)
     final = hs[0]
     for r in range(1, hn):
@@ -514,9 +527,10 @@
     loop(hn, lambda r: h_copy(r).wait_send(), 1)
 
 
-def finish(own, width, v_in, f_in, v_out, cm_out, cr_out, ft, sem):
-    store = pltpu.make_async_copy(v_in, v_out, sem)
-    store.start()
+def finish(own, width, v_in, f_in, v_out, cm_hbm, cr_hbm, ft, cm_out, cr_out, sem):
+    stores = [pltpu.make_async_copy(src, dst, sem.at[i]) for i, (src, dst) in enumerate((
+        (v_in, v_out), (cm_out, cm_hbm), (cr_out, cr_hbm)))]
+    stores[0].start()
     ft[0:16, :] = f_in[...]
     turned = ft[...].T
     lane = lax.broadcasted_iota(I32, (32, 128), 1)
@@ -532,7 +546,10 @@
     cm_out[0:2, :] = done[30:32, 0:own]
     cm_out[2:3, :] = done[7:8, 0:own]
     cr_out[...] = done[6:7, 0:own]
-    store.wait()
+    stores[1].start()
+    stores[2].start()
+    for store in stores:
+        store.wait()
 
 
 def per_device(sizes, basis_init, permeability, accumulation, pressure, source, support, block_of, curve_rank):
@@ -586,8 +603,8 @@
             jax.ShapeDtypeStruct((1, own), F32),
         ),
         in_specs=[anywhere, vmem],
-        out_specs=(anywhere, vmem, vmem),
-        scratch_shapes=[cells(), dma],
+        out_specs=(anywhere, anywhere, anywhere),
+        scratch_shapes=[cells(), pltpu.VMEM((27, own), F32), pltpu.VMEM((1, own), F32), dma((3,))],
         compiler_params=pltpu.CompilerParams(vmem_limit_bytes=VMEM_GRANT),
     )(basis, rows)
     return basis.reshape(basis_init.shape), matrix, residual.reshape(own)

time: 31.6 us -> 30.3 us (0.959)
  Pallas kernels: 30.8 us -> 29.6 us
    pallas_call x1, Pallas kernels: 29.4 us -> 28.8 us  [per_device(): pl.pallas_call(functools.partial(kernel, (lx, plane, own, width)), out_sh...]
    pallas_call x1, Pallas kernels: 1.41 us -> 0.83 us  [per_device(): pl.pallas_call(functools.partial(finish, own, width), out_shape=(jax.Shap...]
where the time goes in v8:
time: 30.3 us; the launch traced here: 30.2 us
  Pallas kernels  29.6 us (98%)
  between operations  0.64 us (2%)
    pallas_call x1, Pallas kernels, per_device(): pl.pallas_call(functools.partial(kernel, (lx, plane, own, width)), out_sh...  28.8 us
    pallas_call x1, Pallas kernels, per_device(): pl.pallas_call(functools.partial(finish, own, width), out_shape=(jax.Shap...  0.83 us

profile of v8, /device:TPU:1, one launch (start us, length us, event | category | flops | bytes accessed | tf_op | source)
XLA Modules:
  0.0 30.2 jit_solution(13044328598181700958)
XLA Ops:
  0.6 28.8 %shard_map.103 = (f32[8,128,128]{2,1,0:T(8,128)S(1)}, f32[16,128]{1,0:T(8,128)S(1)}) custom-call(f32[8,128,128]{2,1,0:T(8,128)} %bitcast.9, f32[128,128]{1,0:T(8,128)} %bitcast.11, f32[128,128]{1,0:T(8,128)} %bitcast.12, f32[128,128]{1,0:T(8,128)} %bitcast.13, f32[128,128]{1,0:T(8,128)} %bitcast.14, s32[8,128,128]{2,1,0:T(8,128)} %bitcast.10, ...), custom_call_target="tpu_custom_call" | custom-call | flops 20000000 | bytes 2000000 | tf_op jit(solution)/shard_map/pallas_call | solution.py:567
  29.4 0.8 %shard_map.104 = (f32[8,128,128]{2,1,0:T(8,128)}, f32[27,37]{1,0:T(8,128)}, f32[1,37]{1,0:T(1,128)}) custom-call(f32[8,128,128]{2,1,0:T(8,128)S(1)} %get-tuple-element.8.v_in, f32[16,128]{1,0:T(8,128)S(1)} %get-tuple-element.9.f_in), custom_call_target="tpu_custom_call" | custom-call | tf_op jit(solution)/shard_map/pallas_call | solution.py:598

commit v9 on v8

--- a/solution.py
+++ b/solution.py
@@ -209,13 +209,15 @@
             (last, zr_buf.at[0], up_z), (lead, zr_buf.at[1], down_z),
         )):
             copies.append(pltpu.make_async_remote_copy(
-                src_ref=src, dst_ref=dst, send_sem=halo_s.at[base + j], recv_sem=halo_r.at[base + j],
+                src_ref=src, dst_ref=dst, send_sem=halo_s.at[base + j // 2], recv_sem=halo_r.at[base + j // 2],
                 device_id=who, device_id_type=MESH))
         for copy in copies:
             copy.start()
         if off:
             second_round()
-        return copies
+        return [pltpu.make_async_remote_copy(
+            src_ref=buf, dst_ref=buf, send_sem=halo_s.at[base + j], recv_sem=halo_r.at[base + j],
+            device_id=up_x, device_id_type=MESH) for j, buf in enumerate((xr_buf, zr_buf))]
 
     def inner(v, off):
         def part(g):
@@ -314,11 +316,16 @@
     tc[RD] = TWO_THIRDS / (tc[RD] + tc[TXB])
 
     outer(va, 1, vb, 0, hxr, hzr, 1)
-    sent2 = exchange(vb, 0, hxs2, hxr2, hzr2, 4)
+    sent2 = exchange(vb, 0, hxs2, hxr2, hzr2, 2)
+
+    def every(buf, sems):
+        return pltpu.make_async_remote_copy(
+            src_ref=buf.at[pl.ds(1, gn - 1)], dst_ref=buf.at[pl.ds(1, gn - 1)], send_sem=sems[0], recv_sem=sems[1],
+            device_id=partner(g_flips, 1), device_id_type=MESH)
 
     def rank_copy(r):
         return pltpu.make_async_remote_copy(
-            src_ref=rks, dst_ref=rkr.at[r], send_sem=rk_s.at[r], recv_sem=rk_r.at[r],
+            src_ref=rks, dst_ref=rkr.at[r], send_sem=rk_s, recv_sem=rk_r,
             device_id=partner(g_flips, r), device_id_type=MESH)
 
     pl.semaphore_wait(round_y, len(y_peers))
@@ -427,7 +434,7 @@
 
     def g_copy(r):
         return pltpu.make_async_remote_copy(
-            src_ref=cs, dst_ref=crv.at[r], send_sem=g_s.at[r], recv_sem=g_r.at[r],
+            src_ref=cs, dst_ref=crv.at[r], send_sem=g_s, recv_sem=g_r,
             device_id=partner(g_flips, r), device_id_type=MESH)
 
     for r in far_first(G_BITS):
@@ -450,7 +457,7 @@
 
     loop(n_idx // 8, wanted)
 
-    loop(gn, lambda r: rank_copy(r).wait_recv(), 1)
+    every(rkr, (rk_s, rk_r)).wait_recv()
 
     have = [rkr[r] for r in range(gn)]
 
@@ -481,17 +488,10 @@
         xb[0:32, lanes] = high
         xb[32:64, lanes] = (vals - high.astype(F32)).astype(BF16)
 
-    def product(part):
-        return lax.dot_general(
-            oh[:, part], xb[:, part], (((1,), (1,)), ((), ())), preferred_element_type=F32)
-
-    half = gn // 2
-    loop(half, lambda r: g_copy(r).wait_recv(), 1)
-    loop(half, spread)
-    routed = product(slice(0, half * 128))
-    loop(gn, lambda r: g_copy(r).wait_recv(), half)
-    loop(gn, spread, half)
-    routed += product(slice(half * 128, gn * 128))
+    every(crv, (g_s, g_r)).wait_recv()
+    loop(gn, spread)
+    routed = lax.dot_general(
+        oh[...], xb[...], (((1,), (1,)), ((), ())), preferred_element_type=F32)
     quarter = lax.broadcasted_iota(I32, (n_idx, 128), 1) >> 5
     packed = jnp.zeros((n_idx, 128), F32)
     for q in range(4):
@@ -509,22 +509,17 @@
         hs[r] = packed[r * width:(r + 1) * width]
         h_copy(r).start()
     hs[0] = packed[0:width]
+    store.wait()
+    for copy in sent2:
+        copy.wait_send()
+    every(rkr, (rk_s, rk_r)).wait_send()
+    every(crv, (g_s, g_r)).wait_send()
+    loop(hn, lambda r: h_copy(r).wait_send(), 1)
     loop(hn, lambda r: h_copy(r).wait_recv(), 1)
     final = hs[0]
     for r in range(1, hn):
         final += hr[r]
     f_out[0:width, :] = final
-
-    store.wait()
-    for copy in sent2:
-        copy.wait_send()
-
-    def drain(r):
-        rank_copy(r).wait_send()
-        g_copy(r).wait_send()
-
-    loop(gn, drain, 1)
-    loop(hn, lambda r: h_copy(r).wait_send(), 1)
 
 
 def finish(own, width, v_in, f_in, v_out, cm_hbm, cr_hbm, ft, cm_out, cr_out, sem):
@@ -585,8 +580,8 @@
             pltpu.VMEM((128, gn * 128), BF16), pltpu.VMEM((4, 128, 128), F32),
             pltpu.VMEM((16, 128), F32), pltpu.VMEM((gn, 16, 128), F32),
             pltpu.VMEM((hn, width, 128), F32), pltpu.VMEM((hn, width, 128), F32),
-            pltpu.SemaphoreType.REGULAR, pltpu.SemaphoreType.REGULAR, dma((10,)), dma((1,)), dma((8,)), dma((8,)),
-            dma((gn,)), dma((gn,)), dma((gn,)), dma((gn,)), dma((hn,)), dma((hn,)),
+            pltpu.SemaphoreType.REGULAR, pltpu.SemaphoreType.REGULAR, dma((10,)), dma((1,)), dma((4,)), dma((4,)),
+            dma, dma, dma, dma, dma((hn,)), dma((hn,)),
         ],
         compiler_params=pltpu.CompilerParams(
             collective_id=0, has_side_effects=True, vmem_limit_bytes=VMEM_GRANT),

time: 30.3 us -> 29.6 us (0.977)
  Pallas kernels: 29.6 us -> 28.9 us
    pallas_call x1, Pallas kernels: 28.8 us -> 28.1 us  [per_device(): pl.pallas_call(functools.partial(kernel, (lx, plane, own, width)), out_sh...]
where the time goes in v9:
time: 29.6 us; the launch traced here: 29.5 us
  Pallas kernels  28.9 us (98%)
  between operations  0.64 us (2%)
    pallas_call x1, Pallas kernels, per_device(): pl.pallas_call(functools.partial(kernel, (lx, plane, own, width)), out_sh...  28.1 us
    pallas_call x1, Pallas kernels, per_device(): pl.pallas_call(functools.partial(finish, own, width), out_shape=(jax.Shap...  0.83 us

profile of v9, /device:TPU:1, one launch (start us, length us, event | category | flops | bytes accessed | tf_op | source)
XLA Modules:
  0.0 29.5 jit_solution(14281960548987812173)
XLA Ops:
  0.6 28.1 %shard_map.103 = (f32[8,128,128]{2,1,0:T(8,128)S(1)}, f32[16,128]{1,0:T(8,128)S(1)}) custom-call(f32[8,128,128]{2,1,0:T(8,128)} %bitcast.9, f32[128,128]{1,0:T(8,128)} %bitcast.11, f32[128,128]{1,0:T(8,128)} %bitcast.12, f32[128,128]{1,0:T(8,128)} %bitcast.13, f32[128,128]{1,0:T(8,128)} %bitcast.14, s32[8,128,128]{2,1,0:T(8,128)} %bitcast.10, ...), custom_call_target="tpu_custom_call" | custom-call | flops 20000000 | bytes 2000000 | tf_op jit(solution)/shard_map/pallas_call | solution.py:562
  28.7 0.8 %shard_map.104 = (f32[8,128,128]{2,1,0:T(8,128)}, f32[27,37]{1,0:T(8,128)}, f32[1,37]{1,0:T(1,128)}) custom-call(f32[8,128,128]{2,1,0:T(8,128)S(1)} %get-tuple-element.8.v_in, f32[16,128]{1,0:T(8,128)S(1)} %get-tuple-element.9.f_in), custom_call_target="tpu_custom_call" | custom-call | tf_op jit(solution)/shard_map/pallas_call | solution.py:593

commit v10 on v9

--- a/solution.py
+++ b/solution.py
@@ -54,7 +54,7 @@
     v_out, f_out,
     bi, sup, aa, pp, ss, blk, cr1, tab,
     va, vb, sf, nn, tc, tzb, ec, sw, fl, hx, hxs, hxr, hzr, hxs2, hxr2, hzr2,
-    rks, rkr, wt, oh, xb, es, cs, crv, hs, hr,
+    rks, rkr, rkt, oh, xb, es, cs, crv, hs, hr,
     round_y, round_z, in_sem, out_sem, halo_s, halo_r, rk_s, rk_r, g_s, g_r, h_s, h_r,
 ):
     lx, plane, own, width = dims
@@ -440,35 +440,26 @@
     for r in far_first(G_BITS):
         g_copy(r).start()
 
-    xb[64:128, :] = jnp.zeros((64, gn * 128), BF16)
-
-    def wanted(i):
-        idx = row1 + i * 8
+    def wanted(t):
+        q, idx = (t, lane1) if t < 4 else (lane1 >> 5, 128 + (lane1 & 31))
         peer = jnp.zeros_like(idx)
-        for t in range(1, hn):
-            peer += jnp.where(idx >= t * width, 1, 0)
-        col = idx - peer * width
+        for p in range(1, hn):
+            peer += jnp.where(idx >= p * width, 1, 0)
+        col = idx - peer * width + q * width
         dev = jnp.zeros_like(idx) + (ml * plane + mp)
         for b, (on_layer, step) in enumerate(h_flips):
             dev += ((peer >> b) & 1) * (step * plane if on_layer else step)
-        want = dev * own + col
-        for q in range(4):
-            wt[one_plane(i + q * (n_idx // 8)), :] = jnp.where(col + q * width < own, want + q * width, -7)
-
-    loop(n_idx // 8, wanted)
-
+        return jnp.where((col < own) & (idx < n_idx), dev * own + col, -7)
+
+    wants = [wanted(t) for t in range(5)]
     every(rkr, (rk_s, rk_r)).wait_recv()
-
-    have = [rkr[r] for r in range(gn)]
-
-    def build(i, carry):
-        at = pl.multiple_of(i * 16, 16)
-        want = wt[pl.ds(at, 16), :]
-        for r in range(gn):
-            oh[pl.ds(at, 16), 128 * r:128 * r + 128] = jnp.where(want == have[r], 1.0, 0.0).astype(BF16)
-        return carry
-
-    lax.fori_loop(0, 4 * n_idx // 16, build, 0)
+    turned = jnp.concatenate([rkr[r] for r in range(gn)] + [jnp.zeros((128 - gn, 128), I32)], axis=0).astype(F32).T
+    rkt[...] = turned.astype(I32)
+    for r in range(gn):
+        have = jnp.broadcast_to(rkt[:, r:r + 1], (128, 128))
+        for t in range(5):
+            want = jnp.concatenate([wants[t]] * 16, axis=0)
+            oh[128 * r:128 * r + 128, 128 * t:128 * t + 128] = jnp.where(have == want, 1.0, 0.0).astype(BF16)
 
     odd = m1 % 2 == 1
     b1 = (x1 >= 3) & (x1 < 6)
@@ -490,15 +481,14 @@
 
     every(crv, (g_s, g_r)).wait_recv()
     loop(gn, spread)
-    routed = lax.dot_general(
-        oh[...], xb[...], (((1,), (1,)), ((), ())), preferred_element_type=F32)
-    quarter = lax.broadcasted_iota(I32, (n_idx, 128), 1) >> 5
-    packed = jnp.zeros((n_idx, 128), F32)
-    for q in range(4):
-        part = routed[q * n_idx:(q + 1) * n_idx]
-        first_half = roll_y(part, 32 * q) if q else part
-        second_half = part if q == 1 else roll_y(part, (32 * q + 96) % 128)
-        packed = jnp.where(quarter == q, first_half + second_half, packed)
+    routed = jnp.dot(xb[...], oh[...], preferred_element_type=F32)
+    both = routed[0:32] + routed[32:64]
+    parts = [both[:, 128 * q:128 * q + 128] for q in range(4)]
+    over = both[:, 512:640]
+    packed = jnp.concatenate([
+        jnp.concatenate(parts, axis=0).T,
+        jnp.concatenate([roll_y(over, (128 - 32 * q) % 128) if q else over for q in range(4)], axis=0).T], axis=0)
+
     def h_copy(r):
         return pltpu.make_async_remote_copy(
             src_ref=hs.at[r], dst_ref=hr.at[r], send_sem=h_s.at[r], recv_sem=h_r.at[r],
@@ -523,9 +513,11 @@
 
 
 def finish(own, width, v_in, f_in, v_out, cm_hbm, cr_hbm, ft, cm_out, cr_out, sem):
-    stores = [pltpu.make_async_copy(src, dst, sem.at[i]) for i, (src, dst) in enumerate((
-        (v_in, v_out), (cm_out, cm_hbm), (cr_out, cr_hbm)))]
-    stores[0].start()
+    pairs = [(v_in.at[pl.ds(2 * i, 2)], v_out.at[pl.ds(2 * i, 2)]) for i in range(4)]
+    pairs += [(cm_out, cm_hbm), (cr_out, cr_hbm)]
+    stores = [pltpu.make_async_copy(src, dst, sem.at[i]) for i, (src, dst) in enumerate(pairs)]
+    for store in stores[:4]:
+        store.start()
     ft[0:16, :] = f_in[...]
     turned = ft[...].T
     lane = lax.broadcasted_iota(I32, (32, 128), 1)
@@ -541,8 +533,8 @@
     cm_out[0:2, :] = done[30:32, 0:own]
     cm_out[2:3, :] = done[7:8, 0:own]
     cr_out[...] = done[6:7, 0:own]
-    stores[1].start()
-    stores[2].start()
+    stores[4].start()
+    stores[5].start()
     for store in stores:
         store.wait()
 
@@ -576,8 +568,8 @@
             pltpu.VMEM((2, 5, 16, 128), F32), pltpu.VMEM((2, 5, 16, 128), F32), pltpu.VMEM((2, 5, 8, 128), F32),
             pltpu.VMEM((2, 4, 16, 128), F32), pltpu.VMEM((2, 4, 16, 128), F32), pltpu.VMEM((2, 4, 8, 128), F32),
             pltpu.VMEM((1, 128), I32), pltpu.VMEM((gn, 1, 128), I32),
-            pltpu.VMEM((4 * hn * width, 128), I32), pltpu.VMEM((4 * hn * width, gn * 128), BF16),
-            pltpu.VMEM((128, gn * 128), BF16), pltpu.VMEM((4, 128, 128), F32),
+            pltpu.VMEM((128, 128), I32), pltpu.VMEM((gn * 128, 640), BF16),
+            pltpu.VMEM((64, gn * 128), BF16), pltpu.VMEM((4, 128, 128), F32),
             pltpu.VMEM((16, 128), F32), pltpu.VMEM((gn, 16, 128), F32),
             pltpu.VMEM((hn, width, 128), F32), pltpu.VMEM((hn, width, 128), F32),
             pltpu.SemaphoreType.REGULAR, pltpu.SemaphoreType.REGULAR, dma((10,)), dma((1,)), dma((4,)), dma((4,)),
@@ -599,7 +591,7 @@
         ),
         in_specs=[anywhere, vmem],
         out_specs=(anywhere, anywhere, anywhere),
-        scratch_shapes=[cells(), pltpu.VMEM((27, own), F32), pltpu.VMEM((1, own), F32), dma((3,))],
+        scratch_shapes=[cells(), pltpu.VMEM((27, own), F32), pltpu.VMEM((1, own), F32), dma((6,))],
         compiler_params=pltpu.CompilerParams(vmem_limit_bytes=VMEM_GRANT),
     )(basis, rows)
     return basis.reshape(basis_init.shape), matrix, residual.reshape(own)

time: 29.6 us -> 29.4 us (level)
  no operation moved by 1% of the time
where the time goes in v10:
time: 29.4 us; the launch traced here: 29.3 us
  Pallas kernels  28.7 us (98%)
  between operations  0.64 us (2%)
    pallas_call x1, Pallas kernels, per_device(): pl.pallas_call(functools.partial(kernel, (lx, plane, own, width)), out_sh...  27.8 us
    pallas_call x1, Pallas kernels, per_device(): pl.pallas_call(functools.partial(finish, own, width), out_shape=(jax.Shap...  0.84 us

profile of v10, /device:TPU:1, one launch (start us, length us, event | category | flops | bytes accessed | tf_op | source)
XLA Modules:
  0.0 29.3 jit_solution(1877130386186236901)
XLA Ops:
  0.6 27.8 %shard_map.103 = (f32[8,128,128]{2,1,0:T(8,128)S(1)}, f32[16,128]{1,0:T(8,128)S(1)}) custom-call(f32[8,128,128]{2,1,0:T(8,128)} %bitcast.9, f32[128,128]{1,0:T(8,128)} %bitcast.11, f32[128,128]{1,0:T(8,128)} %bitcast.12, f32[128,128]{1,0:T(8,128)} %bitcast.13, f32[128,128]{1,0:T(8,128)} %bitcast.14, s32[8,128,128]{2,1,0:T(8,128)} %bitcast.10, ...), custom_call_target="tpu_custom_call" | custom-call | flops 20000000 | bytes 2000000 | tf_op jit(solution)/shard_map/pallas_call | solution.py:554
  28.5 0.8 %shard_map.104 = (f32[8,128,128]{2,1,0:T(8,128)}, f32[27,37]{1,0:T(8,128)}, f32[1,37]{1,0:T(1,128)}) custom-call(f32[8,128,128]{2,1,0:T(8,128)S(1)} %get-tuple-element.8.v_in, f32[16,128]{1,0:T(8,128)S(1)} %get-tuple-element.9.f_in), custom_call_target="tpu_custom_call" | custom-call | tf_op jit(solution)/shard_map/pallas_call | solution.py:585

commit v11 on v10

--- a/solution.py
+++ b/solution.py
@@ -94,8 +94,10 @@
 
     loads = [
         pltpu.make_async_copy(k_hbm, va.at[0], in_sem.at[0]),
-        pltpu.make_async_copy(bi_hbm, bi, in_sem.at[1]),
-        pltpu.make_async_copy(sup_hbm, sup, in_sem.at[2]),
+        pltpu.make_async_copy(bi_hbm.at[:, pl.ds(0, 64)], bi.at[:, pl.ds(0, 64)], in_sem.at[1]),
+        pltpu.make_async_copy(sup_hbm.at[:, pl.ds(0, 64)], sup.at[:, pl.ds(0, 64)], in_sem.at[2]),
+        pltpu.make_async_copy(bi_hbm.at[:, pl.ds(64, 64)], bi.at[:, pl.ds(64, 64)], in_sem.at[10]),
+        pltpu.make_async_copy(sup_hbm.at[:, pl.ds(64, 64)], sup.at[:, pl.ds(64, 64)], in_sem.at[11]),
         pltpu.make_async_copy(a_hbm, aa, in_sem.at[3]),
         pltpu.make_async_copy(cr_hbm, cr1, in_sem.at[4]),
         pltpu.make_async_copy(p_hbm, pp, in_sem.at[5]),
@@ -119,13 +121,13 @@
     greet(down_x)
     for r in x_peers:
         greet(partner(g_flips, r))
-    for load in loads[:3]:
+    for load in loads[:5]:
         load.start()
     for r in y_peers:
         greet(partner(g_flips, r))
     for dz, dc in z_peers:
         greet(along_z(dz, dc))
-    for load in loads[3:]:
+    for load in loads[5:]:
         load.start()
     greeted = 2 + len(x_peers) + len(y_peers) + len(z_peers)
 
@@ -192,7 +194,10 @@
         for s in range(8):
             va[1 + s, rows, :] = vals[s] * inv
 
-    loop(4, first)
+    loop(2, first)
+    loads[3].wait()
+    loads[4].wait()
+    loop(4, first, 2)
 
     def exchange(v, off, xs_buf, xr_buf, zr_buf, base):
         for i, s in enumerate(B0):
@@ -267,7 +272,7 @@
     sent = exchange(va, 1, hxs, hxr, hzr, 0)
     inner(va, 1)
 
-    for load in loads[3:]:
+    for load in loads[5:]:
         load.wait()
     label = blk[0, 0:1, :]
     for u, (j, r) in enumerate(((0, 0), (0, 4), (1, 0), (1, 4), (2, 0), (2, 4), (1, 0), (1, 4))):
@@ -303,6 +308,19 @@
         tc[RD, rows, :] = diag
 
     loop(4, diagonal)
+
+    def every(buf, sems):
+        return pltpu.make_async_remote_copy(
+            src_ref=buf.at[pl.ds(1, gn - 1)], dst_ref=buf.at[pl.ds(1, gn - 1)], send_sem=sems[0], recv_sem=sems[1],
+            device_id=partner(g_flips, 1), device_id_type=MESH)
+
+    def rank_copy(r):
+        return pltpu.make_async_remote_copy(
+            src_ref=rks, dst_ref=rkr.at[r], send_sem=rk_s, recv_sem=rk_r,
+            device_id=partner(g_flips, r), device_id_type=MESH)
+
+    pl.semaphore_wait(round_y, len(y_peers))
+    loop(gn, lambda r: rank_copy(r).start(), 1)
     for copy in sent:
         copy.wait_recv()
 
@@ -318,18 +336,6 @@
     outer(va, 1, vb, 0, hxr, hzr, 1)
     sent2 = exchange(vb, 0, hxs2, hxr2, hzr2, 2)
 
-    def every(buf, sems):
-        return pltpu.make_async_remote_copy(
-            src_ref=buf.at[pl.ds(1, gn - 1)], dst_ref=buf.at[pl.ds(1, gn - 1)], send_sem=sems[0], recv_sem=sems[1],
-            device_id=partner(g_flips, 1), device_id_type=MESH)
-
-    def rank_copy(r):
-        return pltpu.make_async_remote_copy(
-            src_ref=rks, dst_ref=rkr.at[r], send_sem=rk_s, recv_sem=rk_r,
-            device_id=partner(g_flips, r), device_id_type=MESH)
-
-    pl.semaphore_wait(round_y, len(y_peers))
-    loop(gn, lambda r: rank_copy(r).start(), 1)
     es[...] = jnp.zeros_like(es)
 
     inner(vb, 0)
@@ -513,11 +519,9 @@
 
 
 def finish(own, width, v_in, f_in, v_out, cm_hbm, cr_hbm, ft, cm_out, cr_out, sem):
-    pairs = [(v_in.at[pl.ds(2 * i, 2)], v_out.at[pl.ds(2 * i, 2)]) for i in range(4)]
-    pairs += [(cm_out, cm_hbm), (cr_out, cr_hbm)]
-    stores = [pltpu.make_async_copy(src, dst, sem.at[i]) for i, (src, dst) in enumerate(pairs)]
-    for store in stores[:4]:
-        store.start()
+    stores = [pltpu.make_async_copy(src, dst, sem.at[i]) for i, (src, dst) in enumerate((
+        (v_in, v_out), (cm_out, cm_hbm), (cr_out, cr_hbm)))]
+    stores[0].start()
     ft[0:16, :] = f_in[...]
     turned = ft[...].T
     lane = lax.broadcasted_iota(I32, (32, 128), 1)
@@ -533,8 +537,8 @@
     cm_out[0:2, :] = done[30:32, 0:own]
     cm_out[2:3, :] = done[7:8, 0:own]
     cr_out[...] = done[6:7, 0:own]
-    stores[4].start()
-    stores[5].start()
+    stores[1].start()
+    stores[2].start()
     for store in stores:
         store.wait()
 
@@ -572,7 +576,7 @@
             pltpu.VMEM((64, gn * 128), BF16), pltpu.VMEM((4, 128, 128), F32),
             pltpu.VMEM((16, 128), F32), pltpu.VMEM((gn, 16, 128), F32),
             pltpu.VMEM((hn, width, 128), F32), pltpu.VMEM((hn, width, 128), F32),
-            pltpu.SemaphoreType.REGULAR, pltpu.SemaphoreType.REGULAR, dma((10,)), dma((1,)), dma((4,)), dma((4,)),
+            pltpu.SemaphoreType.REGULAR, pltpu.SemaphoreType.REGULAR, dma((12,)), dma((1,)), dma((4,)), dma((4,)),
             dma, dma, dma, dma, dma((hn,)), dma((hn,)),
         ],
         compiler_params=pltpu.CompilerParams(
@@ -591,7 +595,7 @@
         ),
         in_specs=[anywhere, vmem],
         out_specs=(anywhere, anywhere, anywhere),
-        scratch_shapes=[cells(), pltpu.VMEM((27, own), F32), pltpu.VMEM((1, own), F32), dma((6,))],
+        scratch_shapes=[cells(), pltpu.VMEM((27, own), F32), pltpu.VMEM((1, own), F32), dma((3,))],
         compiler_params=pltpu.CompilerParams(vmem_limit_bytes=VMEM_GRANT),
     )(basis, rows)
     return basis.reshape(basis_init.shape), matrix, residual.reshape(own)

time: 29.4 us -> 29.4 us (level)
  no operation moved by 1% of the time
where the time goes in v11:
time: 29.4 us; the launch traced here: 29.3 us
  Pallas kernels  28.7 us (98%)
  between operations  0.64 us (2%)
    pallas_call x1, Pallas kernels, per_device(): pl.pallas_call(functools.partial(kernel, (lx, plane, own, width)), out_sh...  27.9 us
    pallas_call x1, Pallas kernels, per_device(): pl.pallas_call(functools.partial(finish, own, width), out_shape=(jax.Shap...  0.83 us

profile of v11, /device:TPU:1, one launch (start us, length us, event | category | flops | bytes accessed | tf_op | source)
XLA Modules:
  0.0 29.3 jit_solution(5671313475205497144)
XLA Ops:
  0.6 27.9 %shard_map.103 = (f32[8,128,128]{2,1,0:T(8,128)S(1)}, f32[16,128]{1,0:T(8,128)S(1)}) custom-call(f32[8,128,128]{2,1,0:T(8,128)} %bitcast.9, f32[128,128]{1,0:T(8,128)} %bitcast.11, f32[128,128]{1,0:T(8,128)} %bitcast.12, f32[128,128]{1,0:T(8,128)} %bitcast.13, f32[128,128]{1,0:T(8,128)} %bitcast.14, s32[8,128,128]{2,1,0:T(8,128)} %bitcast.10, ...), custom_call_target="tpu_custom_call" | custom-call | flops 20000000 | bytes 2000000 | tf_op jit(solution)/shard_map/pallas_call | solution.py:558
  28.5 0.8 %shard_map.104 = (f32[8,128,128]{2,1,0:T(8,128)}, f32[27,37]{1,0:T(8,128)}, f32[1,37]{1,0:T(1,128)}) custom-call(f32[8,128,128]{2,1,0:T(8,128)S(1)} %get-tuple-element.8.v_in, f32[16,128]{1,0:T(8,128)S(1)} %get-tuple-element.9.f_in), custom_call_target="tpu_custom_call" | custom-call | tf_op jit(solution)/shard_map/pallas_call | solution.py:589

commit v12 on v11

--- a/solution.py
+++ b/solution.py
@@ -435,8 +435,10 @@
             merged.append(jnp.where(high, two, one) + jnp.where(high, roll_y(move, bit), roll_y(move, 128 - bit)))
         sums = merged
     rows_out = sums[0]
-    cs[...] = rows_out
-    crv[0] = rows_out
+    second = pltpu.roll(rows_out[8:16], 7, 0)
+    for buf in (cs, crv.at[0]):
+        buf[0:8, :] = jnp.where(x1 == 7, second, rows_out[0:8])
+        buf[8:13, :] = second[0:5]
 
     def g_copy(r):
         return pltpu.make_async_remote_copy(
@@ -472,8 +474,8 @@
     b1_odd = b1 & odd
 
     def spread(r):
-        got1, got2 = crv[r, 0:8, :], crv[r, 8:16, :]
-        pz1 = jnp.where(m1 < 6, got1, 0.0)
+        got1, got2 = crv[r, 0:8, :], pltpu.roll(crv[r, 5:13, :], 6, 0)
+        pz1 = jnp.where((m1 < 6) & (x1 < 7), got1, 0.0)
         pz2 = jnp.where(m1 < 4, got2, 0.0)
         pz0 = jnp.where(m1 < 4, 0.0, jnp.where(m1 < 6, got2, got1))
         low1, low2, low0 = (jnp.where(b1_odd, v, 0.0) for v in (pz1, pz2, pz0))
@@ -574,7 +576,7 @@
             pltpu.VMEM((1, 128), I32), pltpu.VMEM((gn, 1, 128), I32),
             pltpu.VMEM((128, 128), I32), pltpu.VMEM((gn * 128, 640), BF16),
             pltpu.VMEM((64, gn * 128), BF16), pltpu.VMEM((4, 128, 128), F32),
-            pltpu.VMEM((16, 128), F32), pltpu.VMEM((gn, 16, 128), F32),
+            pltpu.VMEM((13, 128), F32), pltpu.VMEM((gn, 13, 128), F32),
             pltpu.VMEM((hn, width, 128), F32), pltpu.VMEM((hn, width, 128), F32),
             pltpu.SemaphoreType.REGULAR, pltpu.SemaphoreType.REGULAR, dma((12,)), dma((1,)), dma((4,)), dma((4,)),
             dma, dma, dma, dma, dma((hn,)), dma((hn,)),

time: 29.4 us -> 29.4 us (level)
  no operation moved by 1% of the time
where the time goes in v12:
time: 29.4 us; the launch traced here: 29.2 us
  Pallas kernels  28.6 us (97%)
  between operations  0.64 us (2%)
    pallas_call x1, Pallas kernels, per_device(): pl.pallas_call(functools.partial(kernel, (lx, plane, own, width)), out_sh...  27.8 us
    pallas_call x1, Pallas kernels, per_device(): pl.pallas_call(functools.partial(finish, own, width), out_shape=(jax.Shap...  0.83 us

profile of v12, /device:TPU:1, one launch (start us, length us, event | category | flops | bytes accessed | tf_op | source)
XLA Modules:
  0.0 29.2 jit_solution(10812278538685325517)
XLA Ops:
  0.6 27.8 %shard_map.103 = (f32[8,128,128]{2,1,0:T(8,128)S(1)}, f32[16,128]{1,0:T(8,128)S(1)}) custom-call(f32[8,128,128]{2,1,0:T(8,128)} %bitcast.9, f32[128,128]{1,0:T(8,128)} %bitcast.11, f32[128,128]{1,0:T(8,128)} %bitcast.12, f32[128,128]{1,0:T(8,128)} %bitcast.13, f32[128,128]{1,0:T(8,128)} %bitcast.14, s32[8,128,128]{2,1,0:T(8,128)} %bitcast.10, ...), custom_call_target="tpu_custom_call" | custom-call | flops 20000000 | bytes 2000000 | tf_op jit(solution)/shard_map/pallas_call | solution.py:560
  28.4 0.8 %shard_map.104 = (f32[8,128,128]{2,1,0:T(8,128)}, f32[27,37]{1,0:T(8,128)}, f32[1,37]{1,0:T(1,128)}) custom-call(f32[8,128,128]{2,1,0:T(8,128)S(1)} %get-tuple-element.8.v_in, f32[16,128]{1,0:T(8,128)S(1)} %get-tuple-element.9.f_in), custom_call_target="tpu_custom_call" | custom-call | tf_op jit(solution)/shard_map/pallas_call | solution.py:591

commit v13 on v12

--- a/solution.py
+++ b/solution.py
@@ -54,7 +54,7 @@
     v_out, f_out,
     bi, sup, aa, pp, ss, blk, cr1, tab,
     va, vb, sf, nn, tc, tzb, ec, sw, fl, hx, hxs, hxr, hzr, hxs2, hxr2, hzr2,
-    rks, rkr, rkt, oh, xb, es, cs, crv, hs, hr,
+    rks, rkr, oh, xb, es, cs, crv, hs, hr,
     round_y, round_z, in_sem, out_sem, halo_s, halo_r, rk_s, rk_r, g_s, g_r, h_s, h_r,
 ):
     lx, plane, own, width = dims
@@ -86,11 +86,18 @@
         for i in range(start, n):
             body(i)
 
-    def group(g):
-        return slice(g * 32, g * 32 + 32)
+    def steps(n, body, start=0):
+        def step(i, carry):
+            body(i)
+            return carry
+
+        lax.fori_loop(start, n, step, 0)
+
+    def group(g, size=32):
+        return pl.ds(pl.multiple_of(g * 32, 32), size)
 
     def one_plane(z):
-        return slice(z * 8, z * 8 + 8)
+        return pl.ds(z * 8 if isinstance(z, int) else pl.multiple_of(z * 8, 8), 8)
 
     loads = [
         pltpu.make_async_copy(k_hbm, va.at[0], in_sem.at[0]),
@@ -164,12 +171,12 @@
         tz = harmonic(k, jnp.concatenate([va[0, below, :], k[0:24]], axis=0))
         tc[TZM, rows, :] = tz
         tc[TZP, below, :] = tz[0:8]
-        tc[TZP, slice(g * 32, g * 32 + 24), :] = tz[8:32]
+        tc[TZP, group(g, 24), :] = tz[8:32]
         tc[TZM1, rows, :] = tz
         tc[TZP1, below, :] = tz[0:8]
-        tc[TZP1, slice(g * 32, g * 32 + 24), :] = tz[8:32]
-
-    loop(4, faces)
+        tc[TZP1, group(g, 24), :] = tz[8:32]
+
+    steps(4, faces)
     nil = jnp.zeros((8, 128), F32)
     tc[TZM, 0:8, :] = nil
     tc[TZP, 120:128, :] = nil
@@ -194,10 +201,10 @@
         for s in range(8):
             va[1 + s, rows, :] = vals[s] * inv
 
-    loop(2, first)
+    steps(2, first)
     loads[3].wait()
     loads[4].wait()
-    loop(4, first, 2)
+    steps(4, first, 2)
 
     def exchange(v, off, xs_buf, xr_buf, zr_buf, base):
         for i, s in enumerate(B0):
@@ -245,7 +252,7 @@
                 near += zp * jnp.concatenate([here[8:32], hi], axis=0)
                 nn[s, rows, :] = near
 
-        loop(4, part)
+        steps(4, part)
 
     def outer(v, off, new, off2, xr_buf, zr_buf, extra):
         for i in range(4):
@@ -267,7 +274,7 @@
             for s in range(8):
                 new[off2 + s, rows, :] = vals[s] * inv
 
-        loop(4, part)
+        steps(4, part)
 
     sent = exchange(va, 1, hxs, hxr, hzr, 0)
     inner(va, 1)
@@ -281,9 +288,9 @@
     tab[labels // 128:, :] = jnp.zeros((t_rows - labels // 128, 128), I32)
 
     def table(t):
-        tab[t:t + 1, :] = cr1[pl.ds(t * 128, 128)].reshape(1, 128)
-
-    loop(labels // 128, table)
+        tab[pl.ds(t, 1), :] = cr1[pl.ds(pl.multiple_of(t * 128, 128), 128)].reshape(1, 128)
+
+    steps(labels // 128, table)
     if labels % 128:
         t = labels // 128
         tab[t:t + 1, 0:labels % 128] = cr1[pl.ds(t * 128, labels % 128)].reshape(1, labels % 128)
@@ -307,7 +314,7 @@
             diag += tc[t, rows, :]
         tc[RD, rows, :] = diag
 
-    loop(4, diagonal)
+    steps(4, diagonal)
 
     def every(buf, sems):
         return pltpu.make_async_remote_copy(
@@ -354,7 +361,7 @@
         ec[8, rows, :] = sx0
         ec[9, rows, :] = sy0
 
-    loop(4, weigh)
+    steps(4, weigh)
     for i, z in enumerate((3, 4, 11, 12)):
         for s in range(8):
             ec[s, 8 * z:8 * z + 8, :] += sw[i]
@@ -378,7 +385,7 @@
         fl[8, one_plane(g), :] = (
             full - x_swap(plane_sum(ec[8, rows, :] * here)) - y_swap(plane_sum(ec[9, rows, :] * here)))
 
-    loop(4, rest)
+    steps(4, rest)
 
     for copy in sent2:
         copy.wait_recv()
@@ -398,7 +405,7 @@
             full = plane_sum(ec[s, rows, :] * vals[s]) - sw[g] * va[1 + (s ^ 4), far(g), :]
             fl[s, one_plane(g), :] = full - qx[s ^ 2] - qy[s ^ 1]
 
-    loop(4, gather)
+    steps(4, gather)
 
     def z_part(j, pz, s):
         groups = ((0,), (1, 2), (3,))[j] if pz == 1 else {(1, 0): (1,), (2, 0): (3,), (0, 2): (0,), (1, 2): (2,)}[j, pz]
@@ -462,12 +469,16 @@
     wants = [wanted(t) for t in range(5)]
     every(rkr, (rk_s, rk_r)).wait_recv()
     turned = jnp.concatenate([rkr[r] for r in range(gn)] + [jnp.zeros((128 - gn, 128), I32)], axis=0).astype(F32).T
-    rkt[...] = turned.astype(I32)
-    for r in range(gn):
-        have = jnp.broadcast_to(rkt[:, r:r + 1], (128, 128))
+
+    def build(r, ranks):
+        have = jnp.broadcast_to(ranks[:, 0:1], (128, 128))
         for t in range(5):
             want = jnp.concatenate([wants[t]] * 16, axis=0)
-            oh[128 * r:128 * r + 128, 128 * t:128 * t + 128] = jnp.where(have == want, 1.0, 0.0).astype(BF16)
+            oh[pl.ds(pl.multiple_of(128 * r, 128), 128), 128 * t:128 * t + 128] = (
+                jnp.where(have == want, 1.0, 0.0).astype(BF16))
+        return roll_y(ranks, 127)
+
+    lax.fori_loop(0, gn, build, turned.astype(I32))
 
     odd = m1 % 2 == 1
     b1 = (x1 >= 3) & (x1 < 6)
@@ -483,12 +494,17 @@
         vals = jnp.concatenate([
             pz1 - low1 + jnp.where(x1 == 7, pltpu.roll(low0, 2, 0), 0.0), pz2 - low2, pz0 - low0, last], axis=0)
         high = vals.astype(BF16)
-        lanes = slice(128 * r, 128 * r + 128)
+        lanes = pl.ds(pl.multiple_of(128 * r, 128), 128)
         xb[0:32, lanes] = high
         xb[32:64, lanes] = (vals - high.astype(F32)).astype(BF16)
 
     every(crv, (g_s, g_r)).wait_recv()
-    loop(gn, spread)
+
+    def spread_four(i):
+        for j in range(4):
+            spread(4 * i + j)
+
+    steps(gn // 4, spread_four)
     routed = jnp.dot(xb[...], oh[...], preferred_element_type=F32)
     both = routed[0:32] + routed[32:64]
     parts = [both[:, 128 * q:128 * q + 128] for q in range(4)]
@@ -574,7 +590,7 @@
             pltpu.VMEM((2, 5, 16, 128), F32), pltpu.VMEM((2, 5, 16, 128), F32), pltpu.VMEM((2, 5, 8, 128), F32),
             pltpu.VMEM((2, 4, 16, 128), F32), pltpu.VMEM((2, 4, 16, 128), F32), pltpu.VMEM((2, 4, 8, 128), F32),
             pltpu.VMEM((1, 128), I32), pltpu.VMEM((gn, 1, 128), I32),
-            pltpu.VMEM((128, 128), I32), pltpu.VMEM((gn * 128, 640), BF16),
+            pltpu.VMEM((gn * 128, 640), BF16),
             pltpu.VMEM((64, gn * 128), BF16), pltpu.VMEM((4, 128, 128), F32),
             pltpu.VMEM((13, 128), F32), pltpu.VMEM((gn, 13, 128), F32),
             pltpu.VMEM((hn, width, 128), F32), pltpu.VMEM((hn, width, 128), F32),

time: 29.4 us -> 29.9 us (1.017)
  Pallas kernels: 28.6 us -> 29.1 us
    pallas_call x1, Pallas kernels: 27.8 us -> 28.3 us  [per_device(): pl.pallas_call(functools.partial(kernel, (lx, plane, own, width)), out_sh...]
where the time goes in v13:
time: 29.9 us; the launch traced here: 29.8 us
  Pallas kernels  29.1 us (97%)
  between operations  0.64 us (2%)
    pallas_call x1, Pallas kernels, per_device(): pl.pallas_call(functools.partial(kernel, (lx, plane, own, width)), out_sh...  28.3 us
    pallas_call x1, Pallas kernels, per_device(): pl.pallas_call(functools.partial(finish, own, width), out_shape=(jax.Shap...  0.83 us

profile of v13, /device:TPU:1, one launch (start us, length us, event | category | flops | bytes accessed | tf_op | source)
XLA Modules:
  0.0 29.8 jit_solution(16592607933486367011)
XLA Ops:
  0.6 28.3 %shard_map.103 = (f32[8,128,128]{2,1,0:T(8,128)S(1)}, f32[16,128]{1,0:T(8,128)S(1)}) custom-call(f32[8,128,128]{2,1,0:T(8,128)} %bitcast.9, f32[128,128]{1,0:T(8,128)} %bitcast.11, f32[128,128]{1,0:T(8,128)} %bitcast.12, f32[128,128]{1,0:T(8,128)} %bitcast.13, f32[128,128]{1,0:T(8,128)} %bitcast.14, s32[8,128,128]{2,1,0:T(8,128)} %bitcast.10, ...), custom_call_target="tpu_custom_call" | custom-call | flops 20000000 | bytes 2000000 | tf_op jit(solution)/shard_map/pallas_call | solution.py:576
  28.9 0.8 %shard_map.104 = (f32[8,128,128]{2,1,0:T(8,128)}, f32[27,37]{1,0:T(8,128)}, f32[1,37]{1,0:T(1,128)}) custom-call(f32[8,128,128]{2,1,0:T(8,128)S(1)} %get-tuple-element.8.v_in, f32[16,128]{1,0:T(8,128)S(1)} %get-tuple-element.9.f_in), custom_call_target="tpu_custom_call" | custom-call | tf_op jit(solution)/shard_map/pallas_call | solution.py:607

commit v14 on v12

--- a/solution.py
+++ b/solution.py
@@ -311,8 +311,8 @@
 
     def every(buf, sems):
         return pltpu.make_async_remote_copy(
-            src_ref=buf.at[pl.ds(1, gn - 1)], dst_ref=buf.at[pl.ds(1, gn - 1)], send_sem=sems[0], recv_sem=sems[1],
-            device_id=partner(g_flips, 1), device_id_type=MESH)
+            src_ref=buf.at[pl.ds(1, buf.shape[0] - 1)], dst_ref=buf.at[pl.ds(1, buf.shape[0] - 1)],
+            send_sem=sems[0], recv_sem=sems[1], device_id=partner(g_flips, 1), device_id_type=MESH)
 
     def rank_copy(r):
         return pltpu.make_async_remote_copy(
@@ -386,7 +386,6 @@
         copy.wait_send()
     outer(vb, 0, va, 1, hxr2, hzr2, 0)
     store = pltpu.make_async_copy(va.at[pl.ds(1, 8)], v_out, out_sem.at[0])
-    store.start()
 
     def gather(g):
         rows = group(g)
@@ -447,6 +446,7 @@
 
     for r in far_first(G_BITS):
         g_copy(r).start()
+    store.start()
 
     def wanted(t):
         q, idx = (t, lane1) if t < 4 else (lane1 >> 5, 128 + (lane1 & 31))
@@ -499,11 +499,11 @@
 
     def h_copy(r):
         return pltpu.make_async_remote_copy(
-            src_ref=hs.at[r], dst_ref=hr.at[r], send_sem=h_s.at[r], recv_sem=h_r.at[r],
+            src_ref=hs.at[r], dst_ref=hr.at[r], send_sem=h_s, recv_sem=h_r,
             device_id=partner(h_flips, r), device_id_type=MESH)
 
     pl.semaphore_wait(round_z, 2)
-    for r in far_first(H_BITS):
+    for r in sorted(far_first(H_BITS), key=lambda r: r < hn // 2):
         hs[r] = packed[r * width:(r + 1) * width]
         h_copy(r).start()
     hs[0] = packed[0:width]
@@ -512,8 +512,8 @@
         copy.wait_send()
     every(rkr, (rk_s, rk_r)).wait_send()
     every(crv, (g_s, g_r)).wait_send()
-    loop(hn, lambda r: h_copy(r).wait_send(), 1)
-    loop(hn, lambda r: h_copy(r).wait_recv(), 1)
+    every(hr, (h_s, h_r)).wait_send()
+    every(hr, (h_s, h_r)).wait_recv()
     final = hs[0]
     for r in range(1, hn):
         final += hr[r]
@@ -579,7 +579,7 @@
             pltpu.VMEM((13, 128), F32), pltpu.VMEM((gn, 13, 128), F32),
             pltpu.VMEM((hn, width, 128), F32), pltpu.VMEM((hn, width, 128), F32),
             pltpu.SemaphoreType.REGULAR, pltpu.SemaphoreType.REGULAR, dma((12,)), dma((1,)), dma((4,)), dma((4,)),
-            dma, dma, dma, dma, dma((hn,)), dma((hn,)),
+            dma, dma, dma, dma, dma, dma,
         ],
         compiler_params=pltpu.CompilerParams(
             collective_id=0, has_side_effects=True, vmem_limit_bytes=VMEM_GRANT),

time: 29.4 us -> 29 us (0.986)
  Pallas kernels: 28.6 us -> 28.3 us
    pallas_call x1, Pallas kernels: 27.8 us -> 27.4 us  [per_device(): pl.pallas_call(functools.partial(kernel, (lx, plane, own, width)), out_sh...]
where the time goes in v14:
time: 29 us; the launch traced here: 28.9 us
  Pallas kernels  28.3 us (98%)
  between operations  0.64 us (2%)
    pallas_call x1, Pallas kernels, per_device(): pl.pallas_call(functools.partial(kernel, (lx, plane, own, width)), out_sh...  27.4 us
    pallas_call x1, Pallas kernels, per_device(): pl.pallas_call(functools.partial(finish, own, width), out_shape=(jax.Shap...  0.83 us

profile of v14, /device:TPU:1, one launch (start us, length us, event | category | flops | bytes accessed | tf_op | source)
XLA Modules:
  0.0 28.9 jit_solution(7334852487783818028)
XLA Ops:
  0.6 27.4 %shard_map.103 = (f32[8,128,128]{2,1,0:T(8,128)S(1)}, f32[16,128]{1,0:T(8,128)S(1)}) custom-call(f32[8,128,128]{2,1,0:T(8,128)} %bitcast.9, f32[128,128]{1,0:T(8,128)} %bitcast.11, f32[128,128]{1,0:T(8,128)} %bitcast.12, f32[128,128]{1,0:T(8,128)} %bitcast.13, f32[128,128]{1,0:T(8,128)} %bitcast.14, s32[8,128,128]{2,1,0:T(8,128)} %bitcast.10, ...), custom_call_target="tpu_custom_call" | custom-call | flops 20000000 | bytes 2000000 | tf_op jit(solution)/shard_map/pallas_call | solution.py:560
  28.1 0.8 %shard_map.104 = (f32[8,128,128]{2,1,0:T(8,128)}, f32[27,37]{1,0:T(8,128)}, f32[1,37]{1,0:T(1,128)}) custom-call(f32[8,128,128]{2,1,0:T(8,128)S(1)} %get-tuple-element.8.v_in, f32[16,128]{1,0:T(8,128)S(1)} %get-tuple-element.9.f_in), custom_call_target="tpu_custom_call" | custom-call | tf_op jit(solution)/shard_map/pallas_call | solution.py:591

commit v15 on v14

--- a/solution.py
+++ b/solution.py
@@ -319,8 +319,6 @@
             src_ref=rks, dst_ref=rkr.at[r], send_sem=rk_s, recv_sem=rk_r,
             device_id=partner(g_flips, r), device_id_type=MESH)
 
-    pl.semaphore_wait(round_y, len(y_peers))
-    loop(gn, lambda r: rank_copy(r).start(), 1)
     for copy in sent:
         copy.wait_recv()
 
@@ -339,6 +337,8 @@
     es[...] = jnp.zeros_like(es)
 
     inner(vb, 0)
+    pl.semaphore_wait(round_y, len(y_peers))
+    loop(gn, lambda r: rank_copy(r).start(), 1)
 
     def weigh(g):
         rows = group(g)

time: 29 us -> 29 us (level)
  no operation moved by 1% of the time
where the time goes in v15:
time: 29 us; the launch traced here: 28.9 us
  Pallas kernels  28.2 us (97%)
  between operations  0.64 us (2%)
    pallas_call x1, Pallas kernels, per_device(): pl.pallas_call(functools.partial(kernel, (lx, plane, own, width)), out_sh...  27.4 us
    pallas_call x1, Pallas kernels, per_device(): pl.pallas_call(functools.partial(finish, own, width), out_shape=(jax.Shap...  0.83 us

profile of v15, /device:TPU:1, one launch (start us, length us, event | category | flops | bytes accessed | tf_op | source)
XLA Modules:
  0.0 28.9 jit_solution(6069987498399316362)
XLA Ops:
  0.6 27.4 %shard_map.103 = (f32[8,128,128]{2,1,0:T(8,128)S(1)}, f32[16,128]{1,0:T(8,128)S(1)}) custom-call(f32[8,128,128]{2,1,0:T(8,128)} %bitcast.9, f32[128,128]{1,0:T(8,128)} %bitcast.11, f32[128,128]{1,0:T(8,128)} %bitcast.12, f32[128,128]{1,0:T(8,128)} %bitcast.13, f32[128,128]{1,0:T(8,128)} %bitcast.14, s32[8,128,128]{2,1,0:T(8,128)} %bitcast.10, ...), custom_call_target="tpu_custom_call" | custom-call | flops 20000000 | bytes 2000000 | tf_op jit(solution)/shard_map/pallas_call | solution.py:560
  28.1 0.8 %shard_map.104 = (f32[8,128,128]{2,1,0:T(8,128)}, f32[27,37]{1,0:T(8,128)}, f32[1,37]{1,0:T(1,128)}) custom-call(f32[8,128,128]{2,1,0:T(8,128)S(1)} %get-tuple-element.8.v_in, f32[16,128]{1,0:T(8,128)S(1)} %get-tuple-element.9.f_in), custom_call_target="tpu_custom_call" | custom-call | tf_op jit(solution)/shard_map/pallas_call | solution.py:591

commit v16 on v15

--- a/solution.py
+++ b/solution.py
@@ -119,13 +119,17 @@
     z_peers = [(dz, dc) for dz in (1, zc - 1, 2, zc - 2) for dc in (0, 1)] + [(0, 1)]
     greet(up_x)
     greet(down_x)
-    for r in x_peers:
-        greet(partner(g_flips, r))
+    for dz, dc in z_peers[4:8]:
+        greet(along_z(dz, dc))
+    for peers in (x_peers, y_peers):
+        for r in peers[1:2]:
+            greet(partner(g_flips, r))
     for load in loads[:5]:
         load.start()
-    for r in y_peers:
-        greet(partner(g_flips, r))
-    for dz, dc in z_peers:
+    for peers in (x_peers, y_peers):
+        for r in peers[:1] + peers[2:]:
+            greet(partner(g_flips, r))
+    for dz, dc in z_peers[:4] + z_peers[8:]:
         greet(along_z(dz, dc))
     for load in loads[5:]:
         load.start()

time: 29 us -> 29 us (level)
  no operation moved by 1% of the time
where the time goes in v16:
time: 29 us; the launch traced here: 28.9 us
  Pallas kernels  28.2 us (97%)
  between operations  0.64 us (2%)
    pallas_call x1, Pallas kernels, per_device(): pl.pallas_call(functools.partial(kernel, (lx, plane, own, width)), out_sh...  27.4 us
    pallas_call x1, Pallas kernels, per_device(): pl.pallas_call(functools.partial(finish, own, width), out_shape=(jax.Shap...  0.83 us

profile of v16, /device:TPU:1, one launch (start us, length us, event | category | flops | bytes accessed | tf_op | source)
XLA Modules:
  0.0 28.9 jit_solution(14489609100958221518)
XLA Ops:
  0.6 27.4 %shard_map.103 = (f32[8,128,128]{2,1,0:T(8,128)S(1)}, f32[16,128]{1,0:T(8,128)S(1)}) custom-call(f32[8,128,128]{2,1,0:T(8,128)} %bitcast.9, f32[128,128]{1,0:T(8,128)} %bitcast.11, f32[128,128]{1,0:T(8,128)} %bitcast.12, f32[128,128]{1,0:T(8,128)} %bitcast.13, f32[128,128]{1,0:T(8,128)} %bitcast.14, s32[8,128,128]{2,1,0:T(8,128)} %bitcast.10, ...), custom_call_target="tpu_custom_call" | custom-call | flops 20000000 | bytes 2000000 | tf_op jit(solution)/shard_map/pallas_call | solution.py:564
  28.1 0.8 %shard_map.104 = (f32[8,128,128]{2,1,0:T(8,128)}, f32[27,37]{1,0:T(8,128)}, f32[1,37]{1,0:T(1,128)}) custom-call(f32[8,128,128]{2,1,0:T(8,128)S(1)} %get-tuple-element.8.v_in, f32[16,128]{1,0:T(8,128)S(1)} %get-tuple-element.9.f_in), custom_call_target="tpu_custom_call" | custom-call | tf_op jit(solution)/shard_map/pallas_call | solution.py:595

commit v17 on v15

--- a/solution.py
+++ b/solution.py
@@ -435,9 +435,9 @@
         sums = merged
     rows_out = sums[0]
     second = pltpu.roll(rows_out[8:16], 7, 0)
-    for buf in (cs, crv.at[0]):
-        buf[0:8, :] = jnp.where(x1 == 7, second, rows_out[0:8])
-        buf[8:13, :] = second[0:5]
+    first_rows = jnp.where(x1 == 7, second, rows_out[0:8])
+    cs[0:8, :] = first_rows
+    cs[8:13, :] = second[0:5]
 
     def g_copy(r):
         return pltpu.make_async_remote_copy(
@@ -447,6 +447,8 @@
     for r in far_first(G_BITS):
         g_copy(r).start()
     store.start()
+    crv[0, 0:8, :] = first_rows
+    crv[0, 8:13, :] = second[0:5]
 
     def wanted(t):
         q, idx = (t, lane1) if t < 4 else (lane1 >> 5, 128 + (lane1 & 31))
@@ -487,8 +489,10 @@
         xb[0:32, lanes] = high
         xb[32:64, lanes] = (vals - high.astype(F32)).astype(BF16)
 
+    spread(0)
+    pl.semaphore_wait(round_z, 2)
     every(crv, (g_s, g_r)).wait_recv()
-    loop(gn, spread)
+    loop(gn, spread, 1)
     routed = jnp.dot(xb[...], oh[...], preferred_element_type=F32)
     both = routed[0:32] + routed[32:64]
     parts = [both[:, 128 * q:128 * q + 128] for q in range(4)]
@@ -502,7 +506,6 @@
             src_ref=hs.at[r], dst_ref=hr.at[r], send_sem=h_s, recv_sem=h_r,
             device_id=partner(h_flips, r), device_id_type=MESH)
 
-    pl.semaphore_wait(round_z, 2)
     for r in sorted(far_first(H_BITS), key=lambda r: r < hn // 2):
         hs[r] = packed[r * width:(r + 1) * width]
         h_copy(r).start()

time: 29 us -> 29 us (level)
  no operation moved by 1% of the time
where the time goes in v17:
time: 29 us; the launch traced here: 28.9 us
  Pallas kernels  28.2 us (97%)
  between operations  0.64 us (2%)
    pallas_call x1, Pallas kernels, per_device(): pl.pallas_call(functools.partial(kernel, (lx, plane, own, width)), out_sh...  27.4 us
    pallas_call x1, Pallas kernels, per_device(): pl.pallas_call(functools.partial(finish, own, width), out_shape=(jax.Shap...  0.83 us

profile of v17, /device:TPU:1, one launch (start us, length us, event | category | flops | bytes accessed | tf_op | source)
XLA Modules:
  0.0 28.9 jit_solution(8738605511248719837)
XLA Ops:
  0.6 27.4 %shard_map.103 = (f32[8,128,128]{2,1,0:T(8,128)S(1)}, f32[16,128]{1,0:T(8,128)S(1)}) custom-call(f32[8,128,128]{2,1,0:T(8,128)} %bitcast.9, f32[128,128]{1,0:T(8,128)} %bitcast.11, f32[128,128]{1,0:T(8,128)} %bitcast.12, f32[128,128]{1,0:T(8,128)} %bitcast.13, f32[128,128]{1,0:T(8,128)} %bitcast.14, s32[8,128,128]{2,1,0:T(8,128)} %bitcast.10, ...), custom_call_target="tpu_custom_call" | custom-call | flops 20000000 | bytes 2000000 | tf_op jit(solution)/shard_map/pallas_call | solution.py:563
  28.0 0.8 %shard_map.104 = (f32[8,128,128]{2,1,0:T(8,128)}, f32[27,37]{1,0:T(8,128)}, f32[1,37]{1,0:T(1,128)}) custom-call(f32[8,128,128]{2,1,0:T(8,128)S(1)} %get-tuple-element.8.v_in, f32[16,128]{1,0:T(8,128)S(1)} %get-tuple-element.9.f_in), custom_call_target="tpu_custom_call" | custom-call | tf_op jit(solution)/shard_map/pallas_call | solution.py:594
